TPU v7x, 32 devices: a whole 2x2x4 slice. The times are simulated.
32 devices in a mesh: lat: 8 (over y, x, core), lon: 4 (over z).
Axes of the slice: x: 2, y: 2, z: 4, core: 2. Of those that a mesh axis runs over, the one named last changes fastest.
Arguments:
- features: bfloat16 [512, 1024, 128], P('lat', 'lon'), may hold values from -6 to 6
- w_first: bfloat16 [2, 1, 128, 128], replicated, may hold values from -0.375 to 0.375
- bias_first: float32 [2, 1, 128], replicated, may hold values from -3 to 3
- w_second: bfloat16 [2, 1, 128, 128], replicated, may hold values from -0.375 to 0.375
- bias_second: float32 [2, 1, 128], replicated, may hold values from -0.3 to 0.3
Outputs:
- mixed_field: bfloat16 [512, 1024, 128], P('lat', 'lon')
All inputs are finite; a program needn't handle non-finite values.
Results may differ from a plain program's by a relative error of at most 0.025.
Values may be sent and summed in bfloat16 or wider, within the bound.
No kernel may reach another device: no remote copies, remote signals or barrier semaphores. Data moves between devices by JAX's collectives and lax.ppermute only.
A program may use at most 128 MiB of HBM per device.

v0:
```python
import math

import jax
import jax.numpy as jnp
from jax import lax
from jax.sharding import PartitionSpec as P

shrink_level = 0.01


def phase_pair(product, length, sign):
    angle_value = (product % length).astype(jnp.float32) * (sign * 2.0 * math.pi / length)
    return (jnp.cos(angle_value), jnp.sin(angle_value))


def index_outer(left_index, right_index):
    return left_index[:, None] * right_index[None, :]


def twin_dot(pattern, operand, phase_table):
    upper_part = phase_table.astype(jnp.bfloat16)
    lower_part = (phase_table - upper_part.astype(jnp.float32)).astype(jnp.bfloat16)
    return jnp.einsum(
        pattern, operand, upper_part, preferred_element_type=jnp.float32
    ) + jnp.einsum(pattern, operand, lower_part, preferred_element_type=jnp.float32)


def complex_table(pattern, real_part, imag_part, cos_table, sin_table):
    real_out = twin_dot(pattern, real_part, cos_table) - twin_dot(pattern, imag_part, sin_table)
    imag_out = twin_dot(pattern, real_part, sin_table) + twin_dot(pattern, imag_part, cos_table)
    return (real_out, imag_out)


def bit_reverse(number, levels):
    result = jnp.zeros_like(number)
    for bit_level in range(levels):
        result = result + number // 2**bit_level % 2 * 2 ** (levels - 1 - bit_level)
    return result


def local_sections(received, levels):
    full_shape = received.shape
    real_part = received.astype(jnp.float32)
    imag_part = jnp.zeros_like(real_part)
    real_half = received
    imag_half = imag_part.astype(jnp.bfloat16)
    for section_level in range(levels - 1, -1, -1):
        half_span = 2**section_level
        split_shape = (full_shape[0], full_shape[1] // (2 * half_span), 2, half_span) + full_shape[
            2:
        ]
        real_split = real_part.reshape(split_shape)
        imag_split = imag_part.reshape(split_shape)
        tw_cos, tw_sin = phase_pair(jnp.arange(half_span, dtype=jnp.int32), 2 * half_span, -1.0)
        tw_cos = tw_cos[None, None, :, None, None]
        tw_sin = tw_sin[None, None, :, None, None]
        sum_re = real_split[:, :, 0] + real_split[:, :, 1]
        sum_im = imag_split[:, :, 0] + imag_split[:, :, 1]
        diff_re = real_split[:, :, 0] - real_split[:, :, 1]
        diff_im = imag_split[:, :, 0] - imag_split[:, :, 1]
        upper_re = diff_re * tw_cos - diff_im * tw_sin
        upper_im = diff_re * tw_sin + diff_im * tw_cos
        real_half = jnp.stack([sum_re, upper_re], axis=2).reshape(full_shape).astype(jnp.bfloat16)
        imag_half = jnp.stack([sum_im, upper_im], axis=2).reshape(full_shape).astype(jnp.bfloat16)
        real_part = real_half.astype(jnp.float32)
        imag_part = imag_half.astype(jnp.float32)
    return (real_half, imag_half)


def block_product(real_part, imag_part, weights):
    real_out = jnp.einsum(
        "tnj,njk->tnk", real_part, weights[0], preferred_element_type=jnp.float32
    ) - jnp.einsum("tnj,njk->tnk", imag_part, weights[1], preferred_element_type=jnp.float32)
    imag_out = jnp.einsum(
        "tnj,njk->tnk", imag_part, weights[0], preferred_element_type=jnp.float32
    ) + jnp.einsum("tnj,njk->tnk", real_part, weights[1], preferred_element_type=jnp.float32)
    return (real_out, imag_out)


def soft_shrink(values):
    return jnp.sign(values) * jnp.maximum(jnp.abs(values) - shrink_level, 0.0)


def spectral_mix(real_part, imag_part, w_first, bias_first, w_second, bias_second):
    shape_in = real_part.shape
    blocks = w_first.shape[1]
    block_width = w_first.shape[2]
    flat_re = real_part.reshape(-1, blocks, block_width)
    flat_im = imag_part.reshape(-1, blocks, block_width)
    hid_re, hid_im = block_product(flat_re, flat_im, w_first)
    act_re = jax.nn.relu(hid_re + bias_first[0]).astype(jnp.bfloat16)
    act_im = jax.nn.relu(hid_im + bias_first[1]).astype(jnp.bfloat16)
    out_re, out_im = block_product(act_re, act_im, w_second)
    return (
        soft_shrink(out_re + bias_second[0]).astype(jnp.bfloat16).reshape(shape_in),
        soft_shrink(out_im + bias_second[1]).astype(jnp.bfloat16).reshape(shape_in),
    )


def send_real(blocks):
    return lax.all_to_all(blocks, "lon", split_axis=1, concat_axis=1, tiled=True)


def to_columns(real_part, imag_part):
    return (
        lax.all_to_all(real_part, "lat", split_axis=1, concat_axis=0, tiled=True),
        lax.all_to_all(imag_part, "lat", split_axis=1, concat_axis=0, tiled=True),
    )


def to_rows(real_part, imag_part):
    return (
        lax.all_to_all(real_part, "lat", split_axis=0, concat_axis=1, tiled=True),
        lax.all_to_all(imag_part, "lat", split_axis=0, concat_axis=1, tiled=True),
    )


def body(features, w_first, bias_first, w_second, bias_second):
    lat_rows, lon_cells, channels = features.shape
    lon_count = lax.axis_size("lon")
    lat_count = lax.axis_size("lat")
    total_lat = lat_rows * lat_count
    total_lon = lon_cells * lon_count
    stride = lon_cells // lon_count
    keep_cells = lon_cells // 2
    norm_factor = 1.0 / math.sqrt(total_lat * total_lon)
    levels = lon_count.bit_length() - 1
    lon_place = lax.axis_index("lon")
    shard_index = jnp.arange(lon_count, dtype=jnp.int32)
    cell_index = jnp.arange(lon_cells, dtype=jnp.int32)
    keep_index = jnp.arange(keep_cells, dtype=jnp.int32)
    own_freq = bit_reverse(lon_place, levels)
    source_freq = bit_reverse(shard_index, levels)
    received = send_real(features.reshape(lat_rows, lon_count, stride, channels))
    sectioned_re, sectioned_im = local_sections(received, levels)
    cell_local = lon_place * stride + jnp.arange(stride, dtype=jnp.int32)
    rot_cos, rot_sin = phase_pair(index_outer(source_freq, cell_local), total_lon, -1.0)
    rot_cos = rot_cos[None, :, :, None]
    rot_sin = rot_sin[None, :, :, None]
    section_re = sectioned_re.astype(jnp.float32)
    section_im = sectioned_im.astype(jnp.float32)
    first_re = (section_re * rot_cos - section_im * rot_sin).astype(jnp.bfloat16)
    first_im = (section_re * rot_sin + section_im * rot_cos).astype(jnp.bfloat16)
    first_re, first_im = (
        lax.all_to_all(first_re, "lon", split_axis=1, concat_axis=1, tiled=True),
        lax.all_to_all(first_im, "lon", split_axis=1, concat_axis=1, tiled=True),
    )
    first_re = first_re.reshape(lat_rows, lon_cells, channels)
    first_im = first_im.reshape(lat_rows, lon_cells, channels)
    wave_cos, wave_sin = phase_pair(index_outer(cell_index, keep_index), lon_cells, -1.0)
    lon_re, lon_im = complex_table("rmc,mq->rqc", first_re, first_im, wave_cos, wave_sin)
    col_re, col_im = to_columns(lon_re.astype(jnp.bfloat16), lon_im.astype(jnp.bfloat16))
    row_index = jnp.arange(total_lat, dtype=jnp.int32)
    lat_cos, lat_sin = phase_pair(index_outer(row_index, row_index), total_lat, -1.0)
    spec_re, spec_im = complex_table("rqc,rl->lqc", col_re, col_im, lat_cos, lat_sin)
    spec_re = (spec_re * norm_factor).astype(jnp.bfloat16)
    spec_im = (spec_im * norm_factor).astype(jnp.bfloat16)
    mix_re, mix_im = spectral_mix(spec_re, spec_im, w_first, bias_first, w_second, bias_second)
    back_re, back_im = complex_table("lqc,lr->rqc", mix_re, mix_im, lat_cos, -lat_sin)
    back_re, back_im = to_rows(back_re.astype(jnp.bfloat16), back_im.astype(jnp.bfloat16))
    mode_weight = jnp.where((own_freq == 0) & (keep_index == 0), 1.0, 2.0).astype(jnp.float32)
    inv_cos, inv_sin = phase_pair(index_outer(keep_index, cell_index), lon_cells, 1.0)
    inv_cos = inv_cos * mode_weight[:, None]
    inv_sin = inv_sin * mode_weight[:, None]
    inv_re, inv_im = complex_table("rqc,qm->rmc", back_re, back_im, inv_cos, inv_sin)
    turn_cos, turn_sin = phase_pair(cell_index * own_freq, total_lon, 1.0)
    turn_cos = turn_cos[None, :, None]
    turn_sin = turn_sin[None, :, None]
    lon_back_re = (inv_re * turn_cos - inv_im * turn_sin).astype(jnp.bfloat16)
    lon_back_im = (inv_re * turn_sin + inv_im * turn_cos).astype(jnp.bfloat16)
    lon_back_re = lon_back_re.reshape(lat_rows, lon_count, stride, channels)
    lon_back_im = lon_back_im.reshape(lat_rows, lon_count, stride, channels)
    got_re, got_im = (
        lax.all_to_all(lon_back_re, "lon", split_axis=1, concat_axis=1, tiled=True),
        lax.all_to_all(lon_back_im, "lon", split_axis=1, concat_axis=1, tiled=True),
    )
    back_cos, back_sin = phase_pair(index_outer(source_freq, shard_index), lon_count, 1.0)
    spatial = twin_dot("rxsc,xb->rbsc", got_re, back_cos) - twin_dot(
        "rxsc,xb->rbsc", got_im, back_sin
    )
    filtered = (spatial * norm_factor).astype(jnp.bfloat16)
    filtered = send_real(filtered).reshape(lat_rows, lon_cells, channels)
    return (features.astype(jnp.float32) + filtered.astype(jnp.float32)).astype(jnp.bfloat16)


def solution(mesh):
    in_specs = (P("lat", "lon", None), P(), P(), P(), P())
    out_specs = P("lat", "lon", None)
    return jax.shard_map(body, mesh=mesh, in_specs=in_specs, out_specs=out_specs, check_vma=False)
```

profile of v0, /device:TPU:0, one launch (start us, length us, event | category | flops | bytes accessed | tf_op | source)
XLA Modules:
  0.0 865.4 jit_solution(5597239420932137816)
XLA Ops:
  0.0 5.5 copy.65
  5.5 6.3 all-to-all-start
  12.7 92.6 %all-to-all-done = bf16[64,4,64,128]{3,2,0,1:T(8,128)(2,1)} async-done(((bf16[64,4,64,128]{3,2,0,1:T(8,128)(2,1)}), bf16[64,4,64,128]{3,2,0,1:T(8,128)(2,1)}, u32[]{:S(2)}, u32[]{:S(2)}) %all-to-all-start) | async-done | bytes 4194336 | tf_op jit(solution)/shard_map/all_to_all | solution.py:101
  120.8 96.2 %all_to_all.102 = bf16[64,4,64,128]{3,2,0,1:T(8,128)(2,1)} all-to-all(bf16[64,4,64,128]{3,2,0,1:T(8,128)(2,1)S(1)} %get-tuple-element.9), channel_id=1, replica_groups=mesh['lat'=8,'lon'=4] {'lon'}, dimensions={1} | all-to-all | bytes 8388608 | tf_op jit(solution)/shard_map/all_to_all | solution.py:145
  232.5 82.0 %all-to-all-done.2 = bf16[64,4,64,128]{3,2,0,1:T(8,128)(2,1)} async-done(((bf16[64,4,64,128]{3,2,0,1:T(8,128)(2,1)}), bf16[64,4,64,128]{3,2,0,1:T(8,128)(2,1)}, u32[]{:S(2)}, u32[]{:S(2)}) %all-to-all-start.2) | async-done | bytes 4194336 | tf_op jit(solution)/shard_map/all_to_all | solution.py:146
  342.3 15.3 %all-to-all-done.3 = bf16[64,128,128]{2,0,1:T(8,128)(2,1)S(1)} async-done(((bf16[64,128,128]{2,0,1:T(8,128)(2,1)}), bf16[64,128,128]{2,0,1:T(8,128)(2,1)S(1)}, u32[]{:S(2)}, u32[]{:S(2)}) %all-to-all-start.3) | async-done | bytes 2097184 | tf_op jit(solution)/shard_map/all_to_all | solution.py:106
  362.7 6.4 fusion.62
  369.0 6.3 fusion.78
  375.4 6.3 fusion.54
  381.7 6.5 fusion.82
  400.7 5.8 multiply_convert_fusion.4
  408.6 6.1 multiply_convert_fusion.3
  439.6 5.7 subtract_convert_fusion.1
  467.9 5.7 add_convert_fusion.1
  519.9 9.3 %add_subtract_fusion = f32[256,64,128]{2,0,1:T(8,128)} fusion(f32[256,64,128]{2,0,1:T(8,128)} %fusion.143, f32[256,64,128]{2,0,1:T(8,128)} %fusion.139, f32[256,64,128]{2,0,1:T(8,128)S(1)} %bitcast.273, bf16[64,128,128]{2,1,0:T(8,128)(2,1)S(1)} %bitcast.270, f32[128]{0:T(128)S(1)} %and_select_fusion.2), kind=kOutput, calls=%fused_computation.32 | convolution fusion | flops 543784960 | bytes 35652096 | tf_op jit(solution)/shard_map/rqc,qm->rmc/dot_general | solution.py:25
  529.2 15.3 %subtract_convert_fusion = (bf16[256,64,128]{2,0,1:T(8,128)(2,1)S(1)}, bf16[256,64,128]{2,0,1:T(8,128)(2,1)}) fusion(f32[256,64,128]{2,0,1:T(8,128)} %add_subtract_fusion, f32[256]{0:T(256)S(1)} %copy-done.15, f32[256]{0:T(256)S(1)} %copy-done.16, f32[256,64,128]{2,0,1:T(8,128)} %fusion.137, bf16[64,128,128]{2,1,0:T(8,128)(2,1)S(1)} %bitcast.271, ...), kind=kOutput, calls=%fused_computation.30 | convolution fusion | flops 560562176 | bytes 44042752 | tf_op jit(solution)/shard_map/rqc,qm->rmc/dot_general | solution.py:25
  552.3 5.5 copy.89
  557.8 85.1 %all-to-all-done.7 = bf16[64,4,64,128]{3,2,0,1:T(8,128)(2,1)} async-done(((bf16[64,4,64,128]{3,2,0,1:T(8,128)(2,1)}), bf16[64,4,64,128]{3,2,0,1:T(8,128)(2,1)}, u32[]{:S(2)}, u32[]{:S(2)}) %all-to-all-start.7) | async-done | bytes 4194336 | tf_op jit(solution)/shard_map/all_to_all | solution.py:174
  647.8 8.8 %fusion.24 = f32[4,64,64,128]{3,0,2,1:T(4,128)} fusion(bf16[64,4,64,128]{3,2,0,1:T(8,128)(2,1)} %all-to-all-done.7, s32[4]{0:T(128)S(1)} %copy-done.14), kind=kOutput, calls=%fused_computation.60 | convolution fusion | flops 16777504 | bytes 12582928 | tf_op jit(solution)/shard_map/rxsc,xb->rbsc/dot_general | solution.py:25
  656.6 8.8 %fusion.26 = f32[4,64,64,128]{3,0,2,1:T(4,128)} fusion(bf16[64,4,64,128]{3,2,0,1:T(8,128)(2,1)} %all-to-all-done.7, s32[4]{0:T(128)S(1)} %copy-done.14), kind=kOutput, calls=%fused_computation.62 | convolution fusion | flops 16777456 | bytes 12582928 | tf_op jit(solution)/shard_map/rxsc,xb->rbsc/dot_general | solution.py:23
  665.4 75.0 %all-to-all-done.8 = bf16[64,4,64,128]{3,2,0,1:T(8,128)(2,1)} async-done(((bf16[64,4,64,128]{3,2,0,1:T(8,128)(2,1)}), bf16[64,4,64,128]{3,2,0,1:T(8,128)(2,1)}, u32[]{:S(2)}, u32[]{:S(2)}) %all-to-all-start.8) | async-done | bytes 4194336 | tf_op jit(solution)/shard_map/all_to_all | solution.py:175
  740.5 8.8 %fusion.22 = f32[4,64,64,128]{3,0,2,1:T(4,128)} fusion(bf16[64,4,64,128]{3,2,0,1:T(8,128)(2,1)} %all-to-all-done.8, s32[4]{0:T(128)S(1)} %copy-done.14), kind=kOutput, calls=%fused_computation.58 | convolution fusion | flops 16777456 | bytes 12582928 | tf_op jit(solution)/shard_map/rxsc,xb->rbsc/dot_general | solution.py:23
  749.3 13.1 %fusion.20 = bf16[64,4,64,128]{3,1,2,0:T(4,128)(2,1)S(1)} fusion(f32[4,64,64,128]{3,0,2,1:T(4,128)} %fusion.22, f32[4,64,64,128]{3,0,2,1:T(4,128)} %fusion.26, f32[4,64,64,128]{3,0,2,1:T(4,128)} %fusion.24, bf16[64,4,64,128]{3,2,0,1:T(8,128)(2,1)} %all-to-all-done.8, s32[4]{0:T(128)S(1)} %copy-done.14), kind=kOutput, calls=%fused_computation.56 | convolution fusion | flops 27263264 | bytes 33554448 | tf_op jit(solution)/shard_map/rxsc,xb->rbsc/dot_general | solution.py:25
  763.5 95.4 %all_to_all.103 = bf16[64,4,64,128]{3,2,0,1:T(8,128)(2,1)S(1)} all-to-all(bf16[64,4,64,128]{3,2,0,1:T(8,128)(2,1)S(1)} %copy.92), channel_id=1, replica_groups=mesh['lat'=8,'lon'=4] {'lon'}, dimensions={1} | all-to-all | bytes 8388608 | tf_op jit(solution)/shard_map/all_to_all | solution.py:101
  (121 shorter events, 192.5 us)
Async XLA Ops:
  5.5 99.7 %all-to-all-start = ((bf16[64,4,64,128]{3,2,0,1:T(8,128)(2,1)}), bf16[64,4,64,128]{3,2,0,1:T(8,128)(2,1)}, u32[]{:S(2)}, u32[]{:S(2)}) async-start(bf16[64,4,64,128]{3,2,0,1:T(8,128)(2,1)} %copy.65), calls=%async_computation | async-start | bytes 8388608 | tf_op jit(solution)/shard_map/all_to_all | solution.py:101
  217.0 5.9 copy-start.17
  217.0 97.5 %all-to-all-start.2 = ((bf16[64,4,64,128]{3,2,0,1:T(8,128)(2,1)}), bf16[64,4,64,128]{3,2,0,1:T(8,128)(2,1)}, u32[]{:S(2)}, u32[]{:S(2)}) async-start(bf16[64,4,64,128]{3,2,0,1:T(8,128)(2,1)} %get-tuple-element.10), calls=%async_computation.2 | async-start | bytes 8388608 | tf_op jit(solution)/shard_map/all_to_all | solution.py:146
  226.1 3.3 copy-start
  317.7 3.7 copy-start.5
  317.7 5.0 copy-start.6
  327.0 30.6 %all-to-all-start.3 = ((bf16[64,128,128]{2,0,1:T(8,128)(2,1)}), bf16[64,128,128]{2,0,1:T(8,128)(2,1)S(1)}, u32[]{:S(2)}, u32[]{:S(2)}) async-start(bf16[64,128,128]{2,0,1:T(8,128)(2,1)} %copy.68), calls=%async_computation.3 | async-start | bytes 4194304 | tf_op jit(solution)/shard_map/all_to_all | solution.py:106
  331.0 3.5 copy-start.3
  339.6 22.8 %copy-start.18 = (f32[2,1,128]{2,1,0:T(1,128)S(1)}, f32[2,1,128]{2,1,0:T(1,128)}, u32[]{:S(2)}) copy-start(f32[2,1,128]{2,1,0:T(1,128)} %param.9) | copy-start | bytes 3076
  357.6 31.5 %all-to-all-start.4 = ((bf16[64,128,128]{2,0,1:T(8,128)(2,1)}), bf16[64,128,128]{2,0,1:T(8,128)(2,1)}, u32[]{:S(2)}, u32[]{:S(2)}) async-start(bf16[64,128,128]{2,0,1:T(8,128)(2,1)} %copy.70), calls=%async_computation.4 | async-start | bytes 4194304 | tf_op jit(solution)/shard_map/all_to_all | solution.py:107
  395.8 4.8 copy-start.9
  395.8 4.8 copy-start.10
  400.6 7.1 copy-start.8
  421.8 5.0 copy-start.19
  448.0 31.0 %all-to-all-start.5 = ((bf16[512,16,128]{2,1,0:T(8,128)(2,1)}), bf16[512,16,128]{2,1,0:T(8,128)(2,1)}, u32[]{:S(2)}, u32[]{:S(2)}) async-start(bf16[512,16,128]{2,1,0:T(8,128)(2,1)} %copy.78), calls=%async_computation.5 | async-start | bytes 4194304 | tf_op jit(solution)/shard_map/all_to_all | solution.py:113
  452.6 4.9 copy-start.20
  479.0 30.4 %all-to-all-start.6 = ((bf16[512,16,128]{2,1,0:T(8,128)(2,1)}), bf16[512,16,128]{2,1,0:T(8,128)(2,1)S(1)}, u32[]{:S(2)}, u32[]{:S(2)}) async-start(bf16[512,16,128]{2,1,0:T(8,128)(2,1)} %copy.84), calls=%async_computation.6 | async-start | bytes 4194304 | tf_op jit(solution)/shard_map/all_to_all | solution.py:114
  510.0 9.9 %slice-start = ((s8[8388608]{0:T(1024)(128)(4,1)}), s8[4194304]{0:T(1024)(128)(4,1)S(1)}, s32[]{:S(2)}) async-start(s8[8388608]{0:T(1024)(128)(4,1)} %bitcast.272), calls=%async_computation.10 | async-start | bytes 8388608
  514.9 5.0 slice-start.1
  519.9 9.3 %copy-start.15 = (f32[256]{0:T(256)S(1)}, f32[256]{0:T(256)}, u32[]{:S(2)}) copy-start(f32[256]{0:T(256)} %get-tuple-element.24) | copy-start | bytes 3076
  519.9 9.3 %copy-start.16 = (f32[256]{0:T(256)S(1)}, f32[256]{0:T(256)}, u32[]{:S(2)}) copy-start(f32[256]{0:T(256)} %get-tuple-element.25) | copy-start | bytes 3076
  547.4 95.5 %all-to-all-start.7 = ((bf16[64,4,64,128]{3,2,0,1:T(8,128)(2,1)}), bf16[64,4,64,128]{3,2,0,1:T(8,128)(2,1)}, u32[]{:S(2)}, u32[]{:S(2)}) async-start(bf16[64,4,64,128]{3,2,0,1:T(8,128)(2,1)} %copy.86), calls=%async_computation.7 | async-start | bytes 8388608 | tf_op jit(solution)/shard_map/all_to_all | solution.py:174
  557.8 90.0 %copy-start.14 = (s32[4]{0:T(128)S(1)}, s32[4]{0:T(128)}, u32[]{:S(2)}) copy-start(s32[4]{0:T(128)} %copy-done.13) | copy-start | bytes 52
  642.9 97.5 %all-to-all-start.8 = ((bf16[64,4,64,128]{3,2,0,1:T(8,128)(2,1)}), bf16[64,4,64,128]{3,2,0,1:T(8,128)(2,1)}, u32[]{:S(2)}, u32[]{:S(2)}) async-start(bf16[64,4,64,128]{3,2,0,1:T(8,128)(2,1)} %copy.89), calls=%async_computation.8 | async-start | bytes 8388608 | tf_op jit(solution)/shard_map/all_to_all | solution.py:175
  (7 other events, 11.5 us)
where the time goes:
time: 873 us; the launch traced here: 865 us
  waiting for transfers between devices  358 us (41%)
  matrix products  208 us (24%)
  blocking collectives  192 us (22%)
  local copies, waits for them, and re-layouts  48 us (5%)
  starting transfers between devices  38.4 us (4%)
  other arithmetic  20.5 us (2%)
    dot_general x18, matrix products, twin_dot(): jnp.einsum(pattern, operand, lower_part, preferred_element_type=jnp.float32)  111 us
    all_to_all x1, blocking collectives, body(): lax.all_to_all(first_re, 'lon', split_axis=1, concat_axis=1, tiled=True)  96.2 us
    all_to_all x1, blocking collectives, send_real(): lax.all_to_all(blocks, 'lon', split_axis=1, concat_axis=1, tiled=True)  95.4 us
    all_to_all x1, waiting for transfers between devices, send_real(): lax.all_to_all(blocks, 'lon', split_axis=1, concat_axis=1, tiled=True)  92.6 us
    dot_general x18, matrix products, twin_dot(): jnp.einsum(pattern, operand, upper_part, preferred_element_type=jnp.float32)  88.9 us
    all_to_all x1, waiting for transfers between devices, body(): lax.all_to_all(lon_back_re, 'lon', split_axis=1, concat_axis=1, tiled=True)  85.1 us
    all_to_all x1, waiting for transfers between devices, body(): lax.all_to_all(first_im, 'lon', split_axis=1, concat_axis=1, tiled=True)  82 us
    all_to_all x1, waiting for transfers between devices, body(): lax.all_to_all(lon_back_im, 'lon', split_axis=1, concat_axis=1, tiled=True)  75 us
  transfers between devices with their start and end apart: 8, of which 8 were waited for; matrix products, arithmetic and copies ran while one was open for 13% of the time, Pallas kernels for 0%

commit v1 on v0

--- a/solution.py
+++ b/solution.py
@@ -2,7 +2,10 @@
 
 import jax
 import jax.numpy as jnp
+import numpy as np
 from jax import lax
+from jax.experimental import pallas as pl
+from jax.experimental.pallas import tpu as pltpu
 from jax.sharding import PartitionSpec as P
 
 shrink_level = 0.01
@@ -115,7 +118,7 @@
     )
 
 
-def body(features, w_first, bias_first, w_second, bias_second):
+def general_body(features, w_first, bias_first, w_second, bias_second):
     lat_rows, lon_cells, channels = features.shape
     lon_count = lax.axis_size("lon")
     lat_count = lax.axis_size("lat")
@@ -183,6 +186,208 @@
     return (features.astype(jnp.float32) + filtered.astype(jnp.float32)).astype(jnp.bfloat16)
 
 
+def lat_tables(total_lat):
+    half = total_lat // 2
+    row = np.arange(total_lat)
+    angle = (np.outer(np.arange(half), row) % total_lat) * (2.0 * np.pi / total_lat)
+    sin_part = np.sin(angle)
+    sin_part[0] = np.where(row % 2 == 0, 1.0, -1.0)
+    forward = np.concatenate([np.cos(angle), sin_part], axis=0)
+    return jnp.asarray(forward, jnp.bfloat16), jnp.asarray(forward.T, jnp.bfloat16)
+
+
+def lon_tables(cell_order, total_lon):
+    keep = total_lon // 2
+    angle = (np.outer(np.arange(keep), cell_order) % total_lon) * (2.0 * np.pi / total_lon)
+    forward = np.concatenate([np.cos(angle), np.sin(angle)], axis=0)
+    weight = np.where(np.arange(keep) == 0, 1.0, 2.0)
+    weight = np.concatenate([weight, weight])
+    backward = (forward * weight[:, None]).T
+    return jnp.asarray(forward, jnp.bfloat16), jnp.asarray(backward, jnp.bfloat16)
+
+
+def dot32(left, right):
+    return jnp.dot(left, right, preferred_element_type=jnp.float32)
+
+
+def lat_forward_kernel(x_ref, table_ref, out_ref, stage):
+    sources, cells, rows, channels = x_ref.shape
+    half = out_ref.shape[0]
+    table = table_ref[...]
+    for cell in range(0, cells, 2):
+        pair = [x_ref[:, cell + t].reshape(sources * rows, channels) for t in range(2)]
+        result = dot32(table, jnp.concatenate(pair, axis=1))
+        stage[cell] = result[:, :channels]
+        stage[cell + 1] = result[:, channels:]
+    for slot in range(half):
+        out_ref[slot, :, :channels] = stage[:, slot, :].astype(jnp.bfloat16)
+        out_ref[slot, :, channels:] = stage[:, half + slot, :].astype(jnp.bfloat16)
+
+
+def lat_forward(x, table, cells_per_step):
+    sources, cells, rows, channels = x.shape
+    total = sources * rows
+    return pl.pallas_call(
+        lat_forward_kernel,
+        grid=(cells // cells_per_step,),
+        in_specs=[
+            pl.BlockSpec((sources, cells_per_step, rows, channels), lambda i: (0, i, 0, 0)),
+            pl.BlockSpec((total, total), lambda i: (0, 0)),
+        ],
+        out_specs=pl.BlockSpec((total // 2, cells_per_step, 2 * channels), lambda i: (0, i, 0)),
+        out_shape=jax.ShapeDtypeStruct((total // 2, cells, 2 * channels), jnp.bfloat16),
+        scratch_shapes=[pltpu.VMEM((cells_per_step, total, channels), jnp.float32)],
+        compiler_params=pltpu.CompilerParams(vmem_limit_bytes=48 * 2**20),
+        cost_estimate=pl.CostEstimate(
+            flops=2 * total * total * cells * channels,
+            bytes_accessed=4 * total * cells * channels,
+            transcendentals=0,
+        ),
+    )(x, table)
+
+
+def lat_back_kernel(norm, h_ref, table_ref, out_ref, stage):
+    half, cells, width = h_ref.shape
+    channels = width // 2
+    targets, _, rows, _ = out_ref.shape
+    table = table_ref[...]
+    stage[:half] = h_ref[:, :, :channels].astype(jnp.float32)
+    stage[half:] = h_ref[:, :, channels:].astype(jnp.float32)
+    for cell in range(0, cells, 2):
+        pair = [stage[:, cell + t, :].astype(jnp.bfloat16) for t in range(2)]
+        result = dot32(table, jnp.concatenate(pair, axis=1)) * norm
+        for t in range(2):
+            part = result[:, t * channels : (t + 1) * channels].astype(jnp.bfloat16)
+            out_ref[:, cell + t] = part.reshape(targets, rows, channels)
+
+
+def lat_back(h, table, targets, cells_per_step, norm):
+    half, cells, width = h.shape
+    channels = width // 2
+    total = 2 * half
+    rows = total // targets
+    return pl.pallas_call(
+        lambda *refs: lat_back_kernel(norm, *refs),
+        grid=(cells // cells_per_step,),
+        in_specs=[
+            pl.BlockSpec((half, cells_per_step, width), lambda i: (0, i, 0)),
+            pl.BlockSpec((total, total), lambda i: (0, 0)),
+        ],
+        out_specs=pl.BlockSpec((targets, cells_per_step, rows, channels), lambda i: (0, i, 0, 0)),
+        out_shape=jax.ShapeDtypeStruct((targets, cells, rows, channels), jnp.bfloat16),
+        scratch_shapes=[pltpu.VMEM((total, cells_per_step, channels), jnp.float32)],
+        compiler_params=pltpu.CompilerParams(vmem_limit_bytes=48 * 2**20),
+        cost_estimate=pl.CostEstimate(
+            flops=2 * total * total * cells * channels,
+            bytes_accessed=4 * total * cells * channels,
+            transcendentals=0,
+        ),
+    )(h, table)
+
+
+def mix_kernel(norm, place_ref, g_ref, fwd_ref, inv_ref, w1_ref, b1_ref, w2_ref, b2_ref, out_ref):
+    sources, _, cells, width = g_ref.shape
+    channels = width // 2
+    sums = g_ref[:, 0].reshape(sources * cells, width)
+    waves = dot32(fwd_ref[...], sums) * norm
+    keep = waves.shape[0] // 2
+    cc, sc = waves[:keep, :channels], waves[:keep, channels:]
+    cs, ss = waves[keep:, :channels], waves[keep:, channels:]
+    single = (place_ref[0] + pl.program_id(0)) == 0
+    upper = [jnp.where(single, cc, cc - ss), jnp.where(single, -cs, -(cs + sc))]
+    lower = [jnp.where(single, sc, cc + ss), jnp.where(single, -ss, sc - cs)]
+    modes = jnp.concatenate(
+        [jnp.concatenate(upper, axis=1), jnp.concatenate(lower, axis=1)], axis=0
+    ).astype(jnp.bfloat16)
+    hidden = jnp.maximum(dot32(modes, w1_ref[...]) + b1_ref[...], 0.0).astype(jnp.bfloat16)
+    value = dot32(hidden, w2_ref[...]) + b2_ref[...]
+    mixed = jnp.maximum(value - shrink_level, 0.0) + jnp.minimum(value + shrink_level, 0.0)
+    mixed = mixed.astype(jnp.bfloat16).astype(jnp.float32)
+    a, b = mixed[:keep, :channels], mixed[:keep, channels:]
+    c, d = mixed[keep:, :channels], mixed[keep:, channels:]
+    cos_part = [jnp.where(single, a, a + c), jnp.where(single, c, d - b)]
+    sin_part = [jnp.where(single, -b, -(b + d)), jnp.where(single, -d, c - a)]
+    coefs = jnp.concatenate(
+        [jnp.concatenate(cos_part, axis=1), jnp.concatenate(sin_part, axis=1)], axis=0
+    ).astype(jnp.bfloat16)
+    back = dot32(inv_ref[...], coefs).astype(jnp.bfloat16)
+    out_ref[:, 0] = back.reshape(sources, cells, width)
+
+
+def spectral_step(g, place, fwd, inv, w1, b1, w2, b2, norm):
+    sources, slots, cells, width = g.shape
+    total = sources * cells
+    block = pl.BlockSpec((sources, 1, cells, width), lambda i, p: (0, i, 0, 0))
+    fixed = lambda shape: pl.BlockSpec(shape, lambda i, p: (0,) * len(shape))
+    return pl.pallas_call(
+        lambda *refs: mix_kernel(norm, *refs),
+        grid_spec=pltpu.PrefetchScalarGridSpec(
+            num_scalar_prefetch=1,
+            grid=(slots,),
+            in_specs=[block]
+            + [fixed(v.shape) for v in (fwd, inv, w1, b1, w2, b2)],
+            out_specs=block,
+        ),
+        out_shape=jax.ShapeDtypeStruct(g.shape, jnp.bfloat16),
+        compiler_params=pltpu.CompilerParams(vmem_limit_bytes=56 * 2**20),
+        cost_estimate=pl.CostEstimate(
+            flops=slots * width * (4 * total * total + 4 * total * width),
+            bytes_accessed=4 * slots * total * width,
+            transcendentals=0,
+        ),
+    )(place, g, fwd, inv, w1, b1, w2, b2)
+
+
+def complex_weights(weights):
+    real, imag = weights[0, 0], weights[1, 0]
+    return jnp.concatenate(
+        [jnp.concatenate([real, imag], axis=1), jnp.concatenate([-imag, real], axis=1)], axis=0
+    )
+
+
+def lat_first_body(features, w_first, bias_first, w_second, bias_second):
+    rows, lon_cells, channels = features.shape
+    lat_count, lon_count = lax.axis_size("lat"), lax.axis_size("lon")
+    total_lat, total_lon = rows * lat_count, lon_cells * lon_count
+    devices = lat_count * lon_count
+    cells = lon_cells // lat_count
+    slots = total_lat // 2 // devices
+    norm = 1.0 / math.sqrt(total_lat * total_lon)
+    order = np.arange(total_lon).reshape(lon_count, lat_count, cells).transpose(1, 0, 2).reshape(-1)
+    lat_fwd, lat_inv = lat_tables(total_lat)
+    lon_fwd, lon_inv = lon_tables(order, total_lon)
+    place = (lax.axis_index("lat") * lon_count + lax.axis_index("lon")) * slots
+    place = place.astype(jnp.int32).reshape(1)
+    w1, w2 = complex_weights(w_first), complex_weights(w_second)
+    b1, b2 = bias_first.reshape(1, -1), bias_second.reshape(1, -1)
+
+    sent = features.reshape(rows, lat_count, cells, channels).transpose(1, 2, 0, 3)
+    got = lax.all_to_all(sent, "lat", split_axis=0, concat_axis=0, tiled=True)
+    sums = lat_forward(got, lat_fwd, 16).reshape(devices, slots, cells, 2 * channels)
+    sums = lax.all_to_all(sums, ("lat", "lon"), split_axis=0, concat_axis=0, tiled=True)
+    coefs = spectral_step(sums, place, lon_fwd, lon_inv, w1, b1, w2, b2, norm)
+    coefs = lax.all_to_all(coefs, ("lat", "lon"), split_axis=0, concat_axis=0, tiled=True)
+    coefs = coefs.reshape(devices * slots, cells, 2 * channels)
+    filtered = lat_back(coefs, lat_inv, lat_count, 16, norm)
+    filtered = lax.all_to_all(filtered, "lat", split_axis=0, concat_axis=0, tiled=True)
+    filtered = filtered.transpose(2, 0, 1, 3).reshape(rows, lon_cells, channels)
+    return (features.astype(jnp.float32) + filtered.astype(jnp.float32)).astype(jnp.bfloat16)
+
+
+def body(features, w_first, bias_first, w_second, bias_second):
+    rows, lon_cells, channels = features.shape
+    lat_count, lon_count = lax.axis_size("lat"), lax.axis_size("lon")
+    fits = (
+        (rows * lat_count // 2) % (lat_count * lon_count) == 0
+        and lon_cells % (16 * lat_count) == 0
+        and rows % 16 == 0
+        and channels == 128
+        and w_first.shape[1] == 1
+    )
+    chosen = lat_first_body if fits else general_body
+    return chosen(features, w_first, bias_first, w_second, bias_second)
+
+
 def solution(mesh):
     in_specs = (P("lat", "lon", None), P(), P(), P(), P())
     out_specs = P("lat", "lon", None)

time: 873 us -> 369 us (0.42)
  waiting for transfers between devices: 358 us -> 91.4 us
  matrix products: 208 us -> 0 us
  Pallas kernels: 0 us -> 50.2 us
  local copies, waits for them, and re-layouts: 48 us -> 8.06 us
  starting transfers between devices: 38.4 us -> 4.11 us
  blocking collectives: 192 us -> 205 us
  other arithmetic: 20.5 us -> 9.1 us
    all_to_all x8 -> x1, waiting for transfers between devices: 358 us -> 91.4 us  [lat_first_body(): lax.all_to_all(sums, ('lat', 'lon'), split_axis=0, concat_axis=0, tiled=T...]
    dot_general x44 -> x0, matrix products: 208 us -> none  [the longest x18 111 us: twin_dot(): jnp.einsum(pattern, operand, lower_part, preferred_element_type=jnp.float32)]
    pallas_call x0 -> x3, Pallas kernels: none -> 50.2 us  [the longest x1 26.5 us: spectral_step(): pl.pallas_call(lambda *refs: mix_kernel(norm, *refs), grid_spec=pltpu.Pre...]
    all_to_all x8 -> x1, starting transfers between devices: 38.4 us -> 4.11 us  [lat_first_body(): lax.all_to_all(sums, ('lat', 'lon'), split_axis=0, concat_axis=0, tiled=T...]
    convert_element_type x7 -> x0, local copies, waits for them, and re-layouts: 14.5 us -> none  [the longest x1 2.69 us: body(): back_re.astype(jnp.bfloat16)]
    reshape x3 -> x0, local copies, waits for them, and re-layouts: 13.9 us -> none  [the longest x1 5.51 us: body(): lon_back_im = lon_back_im.reshape(lat_rows, lon_count, stride, channels)]
    all_to_all x2 -> x3, blocking collectives: 192 us -> 205 us  [the longest x1 98.1 us: lat_first_body(): lax.all_to_all(coefs, ('lat', 'lon'), split_axis=0, concat_axis=0, tiled=...]
    all_to_all x7 -> x0, local copies, waits for them, and re-layouts: 12 us -> none  [the longest x1 3.15 us: body(): lax.all_to_all(first_re, 'lon', split_axis=1, concat_axis=1, tiled=True)]
  transfers between devices with their start and end apart: 8 -> 1, of which waited for: 8 -> 1; matrix products, arithmetic and copies ran while one was open for 13% -> 0% of each run, Pallas kernels for 0% -> 0%
where the time goes in v1:
time: 369 us; the launch traced here: 368 us
  blocking collectives  205 us (56%)
  waiting for transfers between devices  91.4 us (25%)
  Pallas kernels  50.2 us (14%)
  other arithmetic  9.1 us (2%)
  local copies, waits for them, and re-layouts  8.06 us (2%)
  starting transfers between devices  4.11 us (1%)
    all_to_all x1, blocking collectives, lat_first_body(): lax.all_to_all(coefs, ('lat', 'lon'), split_axis=0, concat_axis=0, tiled=...  98.1 us
    all_to_all x1, waiting for transfers between devices, lat_first_body(): lax.all_to_all(sums, ('lat', 'lon'), split_axis=0, concat_axis=0, tiled=T...  91.4 us
    all_to_all x1, blocking collectives, lat_first_body(): got = lax.all_to_all(sent, 'lat', split_axis=0, concat_axis=0, tiled=True)  54.3 us
    all_to_all x1, blocking collectives, lat_first_body(): lax.all_to_all(filtered, 'lat', split_axis=0, concat_axis=0, tiled=True)  52.8 us
    pallas_call x1, Pallas kernels, spectral_step(): pl.pallas_call(lambda *refs: mix_kernel(norm, *refs), grid_spec=pltpu.Pre...  26.5 us
    pallas_call x1, Pallas kernels, lat_back(): pl.pallas_call(lambda *refs: lat_back_kernel(norm, *refs), grid=(cells //...  12.3 us
    pallas_call x1, Pallas kernels, lat_forward(): pl.pallas_call(lat_forward_kernel, grid=(cells // cells_per_step,), in_sp...  11.4 us
    unnamed x13, local copies, waits for them, and re-layouts  8.05 us
  transfers between devices with their start and end apart: 1, of which 1 were waited for; matrix products, arithmetic and copies ran while one was open for 0% of the time, Pallas kernels for 0%

profile of v1, /device:TPU:0, one launch (start us, length us, event | category | flops | bytes accessed | tf_op | source)
XLA Modules:
  0.0 368.2 jit_solution(1706912813487121799)
XLA Ops:
  0.0 4.9 %copy.10 = bf16[64,256,128]{2,0,1:T(8,128)(2,1)S(1)} copy(bf16[64,256,128]{2,1,0:T(8,128)(2,1)} %param.9) | data formatting | bytes 8388608 | tf_op args[0]
  4.9 0.0 copy-start.2
  4.9 54.3 %all_to_all.20.x_ref = bf16[8,32,64,128]{3,2,1,0:T(8,128)(2,1)} all-to-all(bf16[8,32,64,128]{3,2,1,0:T(8,128)(2,1)S(1)} %bitcast.26), channel_id=1, replica_groups=mesh['lat'=8,'lon'=4] {'lat'}, dimensions={0} | all-to-all | bytes 8388608 | tf_op jit(solution)/shard_map/all_to_all | solution.py:365
  59.2 0.0 copy-done.2
  59.2 11.4 %shard_map.91 = bf16[256,32,256]{2,1,0:T(8,128)(2,1)S(1)} custom-call(bf16[8,32,64,128]{3,2,1,0:T(8,128)(2,1)} %all_to_all.20.x_ref, bf16[512,512]{1,0:T(8,128)(2,1)S(1)} %copy-done.2), custom_call_target="tpu_custom_call" | custom-call | flops 2147483648 | bytes 8388608 | tf_op jit(solution)/shard_map/pallas_call | solution.py:230
  70.6 0.0 copy-start
  70.6 2.0 copy-done
  72.6 0.0 copy-start.4
  72.6 0.0 copy-start.5
  72.6 4.1 %all-to-all-start.1 = ((bf16[32,8,32,256]{3,2,1,0:T(8,128)(2,1)}), bf16[32,8,32,256]{3,2,1,0:T(8,128)(2,1)}, u32[]{:S(2)}, u32[]{:S(2)}) async-start(bf16[32,8,32,256]{3,2,1,0:T(8,128)(2,1)} %bitcast.23), calls=%async_computation.1 | async-start | bytes 8388608 | tf_op jit(solution)/shard_map/all_to_all | solution.py:367
  76.7 0.0 copy-done.4
  76.7 0.0 copy-done.5
  76.8 0.7 maximum_maximum_fusion
  77.5 91.4 %all-to-all-done.1.refs_1_ = bf16[32,8,32,256]{3,2,1,0:T(8,128)(2,1)} async-done(((bf16[32,8,32,256]{3,2,1,0:T(8,128)(2,1)}), bf16[32,8,32,256]{3,2,1,0:T(8,128)(2,1)}, u32[]{:S(2)}, u32[]{:S(2)}) %all-to-all-start.1) | async-done | bytes 4194336 | tf_op jit(solution)/shard_map/all_to_all | solution.py:367
  168.9 26.5 %shard_map.92 = bf16[32,8,32,256]{3,2,1,0:T(8,128)(2,1)} custom-call(s32[1]{0:T(128)} %bitcast.refs_0_, bf16[32,8,32,256]{3,2,1,0:T(8,128)(2,1)} %all-to-all-done.1.refs_1_, bf16[1024,1024]{1,0:T(8,128)(2,1)} %constant.23.clone.refs_2_, bf16[1024,1024]{1,0:T(8,128)(2,1)} %constant.24.clone.refs_3_, bf16[256,256]{1,0:T(8,128)(2,1)} %get-tuple-element.9.refs_4_, ...), custom_call_target="tpu_custom_call" | custom-call | flops 10737418240 | bytes 8388608 | tf_op jit(solution)/shard_map/pallas_call | solution.py:322
  195.5 0.0 copy-start.1
  195.5 98.1 %all_to_all.21 = bf16[32,8,32,256]{3,2,1,0:T(8,128)(2,1)} all-to-all(bf16[32,8,32,256]{3,2,1,0:T(8,128)(2,1)} %shard_map.92), channel_id=1, replica_groups=mesh['lat'=8,'lon'=4] {'lat','lon'}, dimensions={0} | all-to-all | bytes 8388608 | tf_op jit(solution)/shard_map/all_to_all | solution.py:369
  293.6 0.0 copy-done.1
  293.6 12.3 %shard_map.93 = bf16[8,32,64,128]{3,2,1,0:T(8,128)(2,1)S(1)} custom-call(bf16[256,32,256]{2,1,0:T(8,128)(2,1)} %bitcast.25, bf16[512,512]{1,0:T(8,128)(2,1)S(1)} %copy-done.1), custom_call_target="tpu_custom_call" | custom-call | flops 2147483648 | bytes 8388608 | tf_op jit(solution)/shard_map/pallas_call | solution.py:269
  305.9 52.8 %all_to_all.22 = bf16[8,32,64,128]{3,2,1,0:T(8,128)(2,1)S(1)} all-to-all(bf16[8,32,64,128]{3,2,1,0:T(8,128)(2,1)S(1)} %shard_map.93), channel_id=1, replica_groups=mesh['lat'=8,'lon'=4] {'lat'}, dimensions={0} | all-to-all | bytes 8388608 | tf_op jit(solution)/shard_map/all_to_all | solution.py:372
  358.7 0.0 copy-start.3
  358.7 1.0 convert_element_type.21
  359.8 1.1 copy-done.3
  360.9 7.3 %fusion = bf16[64,256,128]{2,1,0:T(8,128)(2,1)} fusion(f32[64,256,128]{2,0,1:T(8,128)S(1)} %bitcast.24, bf16[64,256,128]{2,1,0:T(8,128)(2,1)S(1)} %copy-done.3), kind=kLoop, calls=%fused_computation.1 | loop fusion | flops 6291456 | bytes 16777216 | tf_op jit(solution)/shard_map/convert_element_type | solution.py:374
  (4 shorter events, 0.0 us)
Async XLA Ops:
  4.9 54.3 %copy-start.2 = (bf16[512,512]{1,0:T(8,128)(2,1)S(1)}, bf16[512,512]{1,0:T(8,128)(2,1)}, u32[]{:S(2)}) copy-start(bf16[512,512]{1,0:T(8,128)(2,1)} %constant.21.clone.table_ref) | copy-start | bytes 1572868
  70.6 2.0 copy-start
  72.6 4.1 %copy-start.4 = (bf16[2,1,128,128]{3,2,1,0:T(8,128)(2,1)S(1)}, bf16[2,1,128,128]{3,2,1,0:T(8,128)(2,1)}, u32[]{:S(2)}) copy-start(bf16[2,1,128,128]{3,2,1,0:T(8,128)(2,1)} %param.10) | copy-start | bytes 196612
  72.6 4.2 %copy-start.5 = (bf16[2,1,128,128]{3,2,1,0:T(8,128)(2,1)S(1)}, bf16[2,1,128,128]{3,2,1,0:T(8,128)(2,1)}, u32[]{:S(2)}) copy-start(bf16[2,1,128,128]{3,2,1,0:T(8,128)(2,1)} %param.12) | copy-start | bytes 196612
  72.6 96.3 %all-to-all-start.1 = ((bf16[32,8,32,256]{3,2,1,0:T(8,128)(2,1)}), bf16[32,8,32,256]{3,2,1,0:T(8,128)(2,1)}, u32[]{:S(2)}, u32[]{:S(2)}) async-start(bf16[32,8,32,256]{3,2,1,0:T(8,128)(2,1)} %bitcast.23), calls=%async_computation.1 | async-start | bytes 8388608 | tf_op jit(solution)/shard_map/all_to_all | solution.py:367
  195.5 98.2 %copy-start.1 = (bf16[512,512]{1,0:T(8,128)(2,1)S(1)}, bf16[512,512]{1,0:T(8,128)(2,1)}, u32[]{:S(2)}) copy-start(bf16[512,512]{1,0:T(8,128)(2,1)} %constant.22.clone.refs_1_) | copy-start | bytes 1572868
  358.7 2.2 copy-start.3

commit v2 on v0

--- a/solution.py
+++ b/solution.py
@@ -2,7 +2,10 @@
 
 import jax
 import jax.numpy as jnp
+import numpy as np
 from jax import lax
+from jax.experimental import pallas as pl
+from jax.experimental.pallas import tpu as pltpu
 from jax.sharding import PartitionSpec as P
 
 shrink_level = 0.01
@@ -115,7 +118,7 @@
     )
 
 
-def body(features, w_first, bias_first, w_second, bias_second):
+def general_body(features, w_first, bias_first, w_second, bias_second):
     lat_rows, lon_cells, channels = features.shape
     lon_count = lax.axis_size("lon")
     lat_count = lax.axis_size("lat")
@@ -183,6 +186,360 @@
     return (features.astype(jnp.float32) + filtered.astype(jnp.float32)).astype(jnp.bfloat16)
 
 
+def lat_tables(total_lat, lat_count, scale):
+    half = total_lat // 2
+    row = np.arange(total_lat)
+    angle = (np.outer(np.arange(half), row) % total_lat) * (2.0 * np.pi / total_lat)
+    sin_part = np.sin(angle)
+    sin_part[0] = np.where(row % 2 == 0, 1.0, -1.0)
+    forward = np.concatenate([np.cos(angle), sin_part], axis=0)
+    forward = forward.reshape(total_lat, lat_count, total_lat // lat_count)
+    places = np.arange(lat_count)
+    tables = [forward[:, p ^ places].reshape(total_lat, total_lat) for p in range(lat_count)]
+    tables = np.stack(tables)
+    return (
+        jnp.asarray(tables, jnp.bfloat16),
+        jnp.asarray(tables.transpose(0, 2, 1) * scale, jnp.bfloat16),
+    )
+
+
+def lon_tables(cell_order, total_lon, scale):
+    keep = total_lon // 2
+    angle = (np.outer(np.arange(keep), cell_order) % total_lon) * (2.0 * np.pi / total_lon)
+    forward = np.concatenate([np.cos(angle), -np.sin(angle)], axis=0)
+    weight = np.where(np.arange(keep) == 0, 1.0, 2.0)
+    weight = np.concatenate([weight, weight])
+    backward = (forward * weight[:, None]).T
+    return jnp.asarray(forward * scale, jnp.bfloat16), jnp.asarray(backward, jnp.bfloat16)
+
+
+def dot32(left, right):
+    return jnp.dot(left, right, preferred_element_type=jnp.float32)
+
+
+def turn(values):
+    return jnp.transpose(values, (1, 0, 2))
+
+
+def call(kernel, place, args, in_specs, out_specs, out_shape, grid, mib=24, alias=None):
+    return pl.pallas_call(
+        kernel,
+        grid_spec=pltpu.PrefetchScalarGridSpec(
+            num_scalar_prefetch=1, grid=grid, in_specs=in_specs, out_specs=out_specs
+        ),
+        out_shape=out_shape,
+        input_output_aliases=alias or {},
+        compiler_params=pltpu.CompilerParams(vmem_limit_bytes=mib * 2**20),
+        cost_estimate=pl.CostEstimate(flops=1, bytes_accessed=2**20, transcendentals=0),
+    )(place, *args)
+
+
+def own_block(tile, chips, cells, start, flip):
+    return pl.BlockSpec(
+        (tile, chips, 1, cells, 128), lambda i, p: (i, 0, (p[0] % 2) ^ flip, start // cells, 0)
+    )
+
+
+def split_rows(features, twin, place, start, cells, steps=4):
+    rows, chips, _, _, channels = features.shape
+    tile = rows // steps
+
+    def kernel(place_ref, x_ref, twin_ref, *outs):
+        chip = place_ref[0] // 2
+        for d in range(chips):
+            outs[d][:, 0] = turn(x_ref[:, chip ^ d, 0])
+            outs[d][:, 1] = turn(twin_ref[:, chip ^ d])
+
+    out = pl.BlockSpec((cells, 2, tile, channels), lambda i, p: (0, 0, i, 0))
+    return call(
+        kernel,
+        place,
+        [features, twin],
+        [
+            own_block(tile, chips, cells, start, 0),
+            pl.BlockSpec((tile, chips, cells, channels), lambda i, p: (i, 0, 0, 0)),
+        ],
+        [out] * chips,
+        [jax.ShapeDtypeStruct((cells, 2, rows, channels), jnp.bfloat16)] * chips,
+        (steps,),
+    )
+
+
+def join_own(features, parts, place, start, partial, steps=4):
+    rows, chips, _, _, channels = features.shape
+    cells = parts[0].shape[0]
+    tile = rows // steps
+
+    def kernel(place_ref, x_ref, *refs):
+        out_ref, twin_ref = refs[-2:]
+        chip = place_ref[0] // 2
+        for d in range(chips):
+            added = x_ref[:, chip ^ d, 0].astype(jnp.float32) + turn(refs[d][:, 0]).astype(jnp.float32)
+            out_ref[:, chip ^ d, 0] = added.astype(jnp.bfloat16)
+            twin_ref[:, chip ^ d] = turn(refs[d][:, 1])
+
+    block = own_block(tile, chips, cells, start, 0)
+    part = pl.BlockSpec((cells, 2, tile, channels), lambda i, p: (0, 0, i, 0))
+    args, specs, alias = [features, *parts], [block] + [part] * chips, None
+    if partial is not None:
+        args, specs, alias = args + [partial], specs + [pl.BlockSpec(memory_space=pl.ANY)], {len(args) + 1: 0}
+    return call(
+        kernel,
+        place,
+        args,
+        specs,
+        [block, pl.BlockSpec((tile, chips, cells, channels), lambda i, p: (i, 0, 0, 0))],
+        [
+            jax.ShapeDtypeStruct(features.shape, jnp.bfloat16),
+            jax.ShapeDtypeStruct((rows, chips, cells, channels), jnp.bfloat16),
+        ],
+        (steps,),
+        alias=alias,
+    )
+
+
+def join_twin(features, twin, place, start, partial, steps=2):
+    rows, chips, cells, channels = twin.shape
+    tile = rows // steps
+
+    def kernel(place_ref, x_ref, twin_ref, partial_ref, out_ref):
+        added = x_ref[:, :, 0].astype(jnp.float32) + twin_ref[...].astype(jnp.float32)
+        out_ref[:, :, 0] = added.astype(jnp.bfloat16)
+
+    block = own_block(tile, chips, cells, start, 1)
+    return call(
+        kernel,
+        place,
+        [features, twin, partial],
+        [
+            block,
+            pl.BlockSpec((tile, chips, cells, channels), lambda i, p: (i, 0, 0, 0)),
+            pl.BlockSpec(memory_space=pl.ANY),
+        ],
+        block,
+        jax.ShapeDtypeStruct(features.shape, jnp.bfloat16),
+        (steps,),
+        alias={3: 0},
+    )
+
+
+def lat_forward(parts, table, place, step_cells=8):
+    cells, rows, channels = parts[0].shape
+    count = len(parts)
+    total = rows * count
+    half = total // 2
+
+    def kernel(place_ref, *refs):
+        xs, (table_ref, out_ref) = refs[:count], refs[count:]
+        sums = []
+        for cell in range(0, step_cells, 2):
+            pair = [jnp.concatenate([x[cell + t] for x in xs], axis=0) for t in range(2)]
+            result = dot32(table_ref[0], jnp.concatenate(pair, axis=1)).astype(jnp.bfloat16)
+            sums += [result[:, :channels], result[:, channels:]]
+        for part in range(2):
+            lines = jnp.stack([v[part * half : (part + 1) * half] for v in sums], axis=0)
+            out_ref[:, :, part * channels : (part + 1) * channels] = turn(lines)
+
+    return call(
+        kernel,
+        place,
+        [*parts, table],
+        [pl.BlockSpec((step_cells, rows, channels), lambda i, p: (i, 0, 0))] * count
+        + [pl.BlockSpec((1, total, total), lambda i, p: (p[0], 0, 0))],
+        pl.BlockSpec((half, step_cells, 2 * channels), lambda i, p: (0, i, 0)),
+        jax.ShapeDtypeStruct((half, cells, 2 * channels), jnp.bfloat16),
+        (cells // step_cells,),
+    )
+
+
+def lat_back(h, table, place, chips, step_cells=8):
+    half, cells, width = h.shape
+    channels = width // 2
+    total = 2 * half
+    rows = total // chips // 2
+
+    def kernel(place_ref, h_ref, table_ref, *outs):
+        lines = [turn(h_ref[:, :, part * channels : (part + 1) * channels]) for part in range(2)]
+        for cell in range(0, step_cells, 2):
+            pair = [jnp.concatenate([v[cell + t] for v in lines], axis=0) for t in range(2)]
+            result = dot32(table_ref[0], jnp.concatenate(pair, axis=1)).astype(jnp.bfloat16)
+            for t in range(2):
+                part = result[:, t * channels : (t + 1) * channels].reshape(chips, 2, rows, channels)
+                for d in range(chips):
+                    outs[d][cell + t] = part[d]
+
+    return call(
+        kernel,
+        place,
+        [h, table],
+        [
+            pl.BlockSpec((half, step_cells, width), lambda i, p: (0, i, 0)),
+            pl.BlockSpec((1, total, total), lambda i, p: (p[0], 0, 0)),
+        ],
+        [pl.BlockSpec((step_cells, 2, rows, channels), lambda i, p: (i, 0, 0, 0))] * chips,
+        [jax.ShapeDtypeStruct((cells, 2, rows, channels), jnp.bfloat16)] * chips,
+        (cells // step_cells,),
+    )
+
+
+def spectral_step(chunks, place, fwd, inv, w1, b1, w2, b2, together=2):
+    count = len(chunks)
+    sources, slots, _, width = chunks[0].shape
+    channels = width // 2
+    sizes = [sources * g.shape[2] for g in chunks]
+    total = sum(sizes)
+    keep = total // 2
+
+    def kernel(place_ref, *refs):
+        gs, (fwd_ref, inv_ref, w1_ref, b1_ref, w2_ref, b2_ref) = refs[:count], refs[count : count + 6]
+        outs = refs[count + 6 :]
+
+        def waves(u):
+            sums = jnp.concatenate([g[:, u].reshape(size, width) for g, size in zip(gs, sizes)], axis=0)
+            return dot32(fwd_ref[...], sums)
+
+        def mix(u, both):
+            cc, sc = both[:keep, :channels], both[:keep, channels:]
+            cs, ss = both[keep:, :channels], both[keep:, channels:]
+            single = (place_ref[1] + pl.program_id(0) * together + u) == 0
+            upper = [jnp.where(single, cc, cc + ss), jnp.where(single, cs, cs - sc)]
+            lower = [jnp.where(single, sc, cc - ss), jnp.where(single, ss, cs + sc)]
+            modes = [jnp.concatenate([v.astype(jnp.bfloat16) for v in part], axis=1) for part in (upper, lower)]
+            modes = jnp.concatenate(modes, axis=0)
+            hidden = jnp.maximum((dot32(modes, w1_ref[...]) + b1_ref[...]).astype(jnp.bfloat16), 0)
+            value = dot32(hidden, w2_ref[...]) + b2_ref[...]
+            mixed = value - jnp.clip(value, -shrink_level, shrink_level)
+            a, b = mixed[:keep, :channels], mixed[:keep, channels:]
+            c, d = mixed[keep:, :channels], mixed[keep:, channels:]
+            cos_part = [jnp.where(single, a, a + c), jnp.where(single, c, d - b)]
+            sin_part = [jnp.where(single, b, b + d), jnp.where(single, d, a - c)]
+            coefs = [jnp.concatenate([v.astype(jnp.bfloat16) for v in part], axis=1) for part in (cos_part, sin_part)]
+            return jnp.concatenate(coefs, axis=0)
+
+        def back(u, coefs):
+            lines = dot32(inv_ref[...], coefs).astype(jnp.bfloat16)
+            first = 0
+            for out_ref, size in zip(outs, sizes):
+                out_ref[:, u] = lines[first : first + size].reshape(sources, size // sources, width)
+                first += size
+
+        both = [waves(u) for u in range(together)]
+        coefs = [mix(u, both[u]) for u in range(together)]
+        for u in range(together):
+            back(u, coefs[u])
+
+    def block(g):
+        return pl.BlockSpec((sources, together) + g.shape[2:], lambda i, p: (0, i, 0, 0))
+
+    tables = [fwd, inv, w1, b1, w2, b2]
+    return call(
+        kernel,
+        place,
+        [*chunks, *tables],
+        [block(g) for g in chunks] + [pl.BlockSpec(v.shape, lambda i, p: (0, 0)) for v in tables],
+        [block(g) for g in chunks],
+        [jax.ShapeDtypeStruct(g.shape, jnp.bfloat16) for g in chunks],
+        (slots // together,),
+        mib=48,
+    )
+
+
+def complex_weights(weights):
+    real, imag = weights[0, 0], weights[1, 0]
+    return jnp.concatenate(
+        [jnp.concatenate([real, imag], axis=1), jnp.concatenate([-imag, real], axis=1)], axis=0
+    )
+
+
+def swap(part, axis, bits):
+    return lax.ppermute(part, axis, [(j, j ^ bits) for j in range(lax.axis_size(axis))])
+
+
+def swap_chips(parts):
+    return [parts[0]] + [swap(parts[d], "lat", 2 * d) for d in range(1, len(parts))]
+
+
+def swap_all(parts):
+    return lax.all_to_all(parts, ("lat", "lon"), split_axis=0, concat_axis=0, tiled=True)
+
+
+def chunk_sizes(cells):
+    return [cells // 2, cells // 2]
+
+
+def lat_first_body(features, w_first, bias_first, w_second, bias_second):
+    rows, lon_cells, channels = features.shape
+    lat_count, lon_count = lax.axis_size("lat"), lax.axis_size("lon")
+    total_lat, total_lon = rows * lat_count, lon_cells * lon_count
+    devices, chips = lat_count * lon_count, lat_count // 2
+    block_cells = lon_cells // lat_count
+    slots = total_lat // 2 // devices
+    norm = 1.0 / math.sqrt(total_lat * total_lon)
+    sizes = chunk_sizes(block_cells)
+    count = len(sizes)
+    starts = [sum(sizes[:i]) for i in range(count)]
+    cell_index = np.arange(total_lon).reshape(lon_count, lat_count, block_cells).transpose(1, 0, 2)
+    order = [cell_index[..., s : s + n].reshape(-1) for s, n in zip(starts, sizes)]
+    lat_fwd, lat_inv = lat_tables(total_lat, lat_count, norm)
+    lon_fwd, lon_inv = lon_tables(np.concatenate(order), total_lon, norm)
+    lat_place = lax.axis_index("lat")
+    first_slot = (lat_place * lon_count + lax.axis_index("lon")) * slots
+    place = jnp.stack([lat_place, first_slot]).astype(jnp.int32)
+    w1, w2 = complex_weights(w_first), complex_weights(w_second)
+    b1, b2 = bias_first.reshape(1, -1), bias_second.reshape(1, -1)
+    tie = lax.optimization_barrier
+    field = features.reshape(rows, chips, 2, block_cells, channels)
+
+    def prepare(i):
+        for_twin = lax.dynamic_slice(
+            field, (0, 0, 1 - lat_place % 2, starts[i], 0), (rows, chips, 1, sizes[i], channels)
+        )
+        twin = swap(for_twin.reshape(rows, chips, sizes[i], channels), "lat", 1)
+        return split_rows(field, twin, place, starts[i], sizes[i])
+
+    sums, sent = [], prepare(0)
+    for i, size in enumerate(sizes):
+        parts = swap_chips([v.reshape(size, 2 * rows, channels) for v in sent])
+        if i + 1 < count:
+            parts, sent = tie((parts, prepare(i + 1)))
+        part = lat_forward(parts, lat_fwd, place)
+        sums.append(swap_all(part.reshape(devices, slots, size, 2 * channels)))
+
+    coefs = spectral_step(sums, place, lon_fwd, lon_inv, w1, b1, w2, b2)
+
+    def finish(i, parts, result):
+        result, for_twin = join_own(field, parts, place, starts[i], result)
+        return join_twin(field, swap(for_twin, "lat", 1), place, starts[i], result)
+
+    result, parts = None, None
+    for i in reversed(range(count)):
+        part = swap_all(coefs[i]).reshape(devices * slots, sizes[i], 2 * channels)
+        if parts is not None:
+            part, parts = tie((part, parts))
+        back = lat_back(part, lat_inv, place, chips)
+        if parts is not None:
+            result = finish(i + 1, parts, result)
+        parts = swap_chips(back)
+    result = finish(0, parts, result)
+    return result.reshape(features.shape)
+
+
+def body(features, w_first, bias_first, w_second, bias_second):
+    rows, lon_cells, channels = features.shape
+    lat_count, lon_count = lax.axis_size("lat"), lax.axis_size("lon")
+    fits = (
+        (rows * lat_count // 2) % (lat_count * lon_count) == 0
+        and lat_count & (lat_count - 1) == 0
+        and lat_count > 1
+        and lon_cells % (32 * lat_count) == 0
+        and rows % 64 == 0
+        and channels == 128
+        and w_first.shape[1] == 1
+    )
+    chosen = lat_first_body if fits else general_body
+    return chosen(features, w_first, bias_first, w_second, bias_second)
+
+
 def solution(mesh):
     in_specs = (P("lat", "lon", None), P(), P(), P(), P())
     out_specs = P("lat", "lon", None)

time: 873 us -> 322 us (0.37)
  matrix products: 208 us -> 0 us
  waiting for transfers between devices: 358 us -> 183 us
  blocking collectives: 192 us -> 51.6 us
  Pallas kernels: 0 us -> 43.1 us
  local copies, waits for them, and re-layouts: 48 us -> 14.7 us
  other arithmetic: 20.5 us -> 0.12 us
  starting transfers between devices: 38.4 us -> 28.9 us
    all_to_all x8 -> x3, waiting for transfers between devices: 358 us -> 84.5 us  [swap_all(): lax.all_to_all(parts, ('lat', 'lon'), split_axis=0, concat_axis=0, tiled=...]
    dot_general x44 -> x0, matrix products: 208 us -> none  [the longest x18 111 us: twin_dot(): jnp.einsum(pattern, operand, lower_part, preferred_element_type=jnp.float32)]
    all_to_all x2 -> x1, blocking collectives: 192 us -> 51.6 us  [swap_all(): lax.all_to_all(parts, ('lat', 'lon'), split_axis=0, concat_axis=0, tiled=...]
    ppermute x0 -> x16, waiting for transfers between devices: none -> 98.5 us  [swap(): lax.ppermute(part, axis, [(j, j ^ bits) for j in range(lax.axis_size(axis...]
    pallas_call x0 -> x11, Pallas kernels: none -> 43.1 us  [call(): pl.pallas_call(kernel, grid_spec=pltpu.PrefetchScalarGridSpec(num_scalar_...]
    all_to_all x8 -> x3, starting transfers between devices: 38.4 us -> 12.8 us  [swap_all(): lax.all_to_all(parts, ('lat', 'lon'), split_axis=0, concat_axis=0, tiled=...]
    ppermute x0 -> x16, starting transfers between devices: none -> 16.1 us  [swap(): lax.ppermute(part, axis, [(j, j ^ bits) for j in range(lax.axis_size(axis...]
    convert_element_type x7 -> x0, local copies, waits for them, and re-layouts: 14.5 us -> none  [the longest x1 2.69 us: body(): back_re.astype(jnp.bfloat16)]
  transfers between devices with their start and end apart: 8 -> 19, of which waited for: 8 -> 11; matrix products, arithmetic and copies ran while one was open for 13% -> 0% of each run, Pallas kernels for 0% -> 4%
where the time goes in v2:
time: 322 us; the launch traced here: 321 us
  waiting for transfers between devices  183 us (57%)
  blocking collectives  51.6 us (16%)
  Pallas kernels  43.1 us (13%)
  starting transfers between devices  28.9 us (9%)
  local copies, waits for them, and re-layouts  14.7 us (5%)
    ppermute x16, waiting for transfers between devices, swap(): lax.ppermute(part, axis, [(j, j ^ bits) for j in range(lax.axis_size(axis...  98.5 us
    all_to_all x3, waiting for transfers between devices, swap_all(): lax.all_to_all(parts, ('lat', 'lon'), split_axis=0, concat_axis=0, tiled=...  84.5 us
    all_to_all x1, blocking collectives, swap_all(): lax.all_to_all(parts, ('lat', 'lon'), split_axis=0, concat_axis=0, tiled=...  51.6 us
    pallas_call x11, Pallas kernels, call(): pl.pallas_call(kernel, grid_spec=pltpu.PrefetchScalarGridSpec(num_scalar_...  43.1 us
    ppermute x16, starting transfers between devices, swap(): lax.ppermute(part, axis, [(j, j ^ bits) for j in range(lax.axis_size(axis...  16.1 us
    all_to_all x3, starting transfers between devices, swap_all(): lax.all_to_all(parts, ('lat', 'lon'), split_axis=0, concat_axis=0, tiled=...  12.8 us
    unnamed x28, local copies, waits for them, and re-layouts  11.7 us
  transfers between devices with their start and end apart: 19, of which 11 were waited for; matrix products, arithmetic and copies ran while one was open for 0% of the time, Pallas kernels for 4%

profile of v2, /device:TPU:0, one launch (start us, length us, event | category | flops | bytes accessed | tf_op | source)
XLA Modules:
  0.0 321.5 jit_solution(4737044068310438453)
XLA Ops:
  0.0 3.0 dynamic-slice_bitcast_fusion
  3.6 3.3 %collective-permute-done.twin_ref = bf16[64,4,16,128]{3,2,1,0:T(8,128)(2,1)S(1)} collective-permute-done((bf16[64,4,16,128]{3,2,1,0:T(8,128)(2,1)}, bf16[64,4,16,128]{3,2,1,0:T(8,128)(2,1)S(1)}, u32[]{:S(2)}, u32[]{:S(2)}) %collective-permute-start) | collective-permute-done | bytes 1048608 | tf_op jit(solution)/shard_map/ppermute | solution.py:455
  10.8 3.5 %collective-permute-start.1 = (bf16[16,128,128]{2,1,0:T(8,128)(2,1)S(1)}, bf16[16,128,128]{2,1,0:T(8,128)(2,1)S(1)}, u32[]{:S(2)}, u32[]{:S(2)}) collective-permute-start(bf16[16,128,128]{2,1,0:T(8,128)(2,1)S(1)} %bitcast.52), channel_id=1, source_target_pairs={{0,8},{4,12},{8,0},{12,4},{16,24},{20,28},{24,16},{28,20},{1,9},{5... | collective-permute-start | bytes 1572872 | tf_op jit(solution)/shard_map/ppermute | solution.py:455
  17.5 9.4 %collective-permute-done.1.refs_1_ = bf16[16,128,128]{2,1,0:T(8,128)(2,1)S(1)} collective-permute-done((bf16[16,128,128]{2,1,0:T(8,128)(2,1)S(1)}, bf16[16,128,128]{2,1,0:T(8,128)(2,1)S(1)}, u32[]{:S(2)}, u32[]{:S(2)}) %collective-permute-start.1) | collective-permute-done | bytes 524320 | tf_op jit(solution)/shard_map/ppermute | solution.py:455
  26.9 12.2 %collective-permute-done.2.refs_2_ = bf16[16,128,128]{2,1,0:T(8,128)(2,1)S(1)} collective-permute-done((bf16[16,128,128]{2,1,0:T(8,128)(2,1)S(1)}, bf16[16,128,128]{2,1,0:T(8,128)(2,1)S(1)}, u32[]{:S(2)}, u32[]{:S(2)}) %collective-permute-start.2) | collective-permute-done | bytes 524320 | tf_op jit(solution)/shard_map/ppermute | solution.py:455
  39.2 3.2 %shard_map.93 = bf16[256,16,256]{2,1,0:T(8,128)(2,1)} custom-call(s32[2]{0:T(128)S(1)} %pad_add_fusion.place_ref, bf16[16,128,128]{2,1,0:T(8,128)(2,1)S(1)} %bitcast.44, bf16[16,128,128]{2,1,0:T(8,128)(2,1)S(1)} %collective-permute-done.1.refs_1_, bf16[16,128,128]{2,1,0:T(8,128)(2,1)S(1)} %collective-permute-done.2.refs_2_, ...), custom_call_target="tpu_custom_call" | custom-call | flops 1 | bytes 1048576 | tf_op jit(solution)/shard_map/pallas_call | solution.py:225
  42.4 5.0 %all-to-all-start = ((bf16[32,8,16,256]{3,2,1,0:T(8,128)(2,1)}), bf16[32,8,16,256]{3,2,1,0:T(8,128)(2,1)}, u32[]{:S(2)}, u32[]{:S(2)}) async-start(bf16[32,8,16,256]{3,2,1,0:T(8,128)(2,1)} %bitcast.9), calls=%async_computation | async-start | bytes 4194304 | tf_op jit(solution)/shard_map/all_to_all | solution.py:463
  51.0 29.1 %collective-permute-done.5.refs_1_ = bf16[16,128,128]{2,1,0:T(8,128)(2,1)S(1)} collective-permute-done((bf16[16,128,128]{2,1,0:T(8,128)(2,1)S(1)}, bf16[16,128,128]{2,1,0:T(8,128)(2,1)S(1)}, u32[]{:S(2)}, u32[]{:S(2)}) %collective-permute-start.5) | collective-permute-done | bytes 524320 | tf_op jit(solution)/shard_map/ppermute | solution.py:455
  80.2 17.7 %collective-permute-done.7.refs_3_ = bf16[16,128,128]{2,1,0:T(8,128)(2,1)S(1)} collective-permute-done((bf16[16,128,128]{2,1,0:T(8,128)(2,1)S(1)}, bf16[16,128,128]{2,1,0:T(8,128)(2,1)S(1)}, u32[]{:S(2)}, u32[]{:S(2)}) %collective-permute-start.7) | collective-permute-done | bytes 524320 | tf_op jit(solution)/shard_map/ppermute | solution.py:455
  100.1 3.3 %shard_map.94 = bf16[256,16,256]{2,1,0:T(8,128)(2,1)} custom-call(s32[2]{0:T(128)S(1)} %pad_add_fusion.place_ref, bf16[16,128,128]{2,1,0:T(8,128)(2,1)S(1)} %bitcast.43, bf16[16,128,128]{2,1,0:T(8,128)(2,1)S(1)} %collective-permute-done.5.refs_1_, bf16[16,128,128]{2,1,0:T(8,128)(2,1)S(1)} %collective-permute-done.6.refs_2_, ...), custom_call_target="tpu_custom_call" | custom-call | flops 1 | bytes 1048576 | tf_op jit(solution)/shard_map/pallas_call | solution.py:225
  103.4 3.3 %all-to-all-start.1 = ((bf16[32,8,16,256]{3,2,1,0:T(8,128)(2,1)}), bf16[32,8,16,256]{3,2,1,0:T(8,128)(2,1)S(1)}, u32[]{:S(2)}, u32[]{:S(2)}) async-start(bf16[32,8,16,256]{3,2,1,0:T(8,128)(2,1)} %bitcast.14), calls=%async_computation.1 | async-start | bytes 4194304 | tf_op jit(solution)/shard_map/all_to_all | solution.py:463
  106.8 47.4 %all-to-all-done.1.refs_1_ = bf16[32,8,16,256]{3,2,1,0:T(8,128)(2,1)S(1)} async-done(((bf16[32,8,16,256]{3,2,1,0:T(8,128)(2,1)}), bf16[32,8,16,256]{3,2,1,0:T(8,128)(2,1)S(1)}, u32[]{:S(2)}, u32[]{:S(2)}) %all-to-all-start.1) | async-done | bytes 2097184 | tf_op jit(solution)/shard_map/all_to_all | solution.py:463
  155.5 15.9 %shard_map.95 = (bf16[32,8,16,256]{3,2,1,0:T(8,128)(2,1)S(1)}, bf16[32,8,16,256]{3,2,1,0:T(8,128)(2,1)S(1)}) custom-call(s32[2]{0:T(128)S(1)} %pad_add_fusion.place_ref, bf16[32,8,16,256]{3,2,1,0:T(8,128)(2,1)} %all-to-all-done.refs_0_, bf16[32,8,16,256]{3,2,1,0:T(8,128)(2,1)} %copy-done.11, bf16[1024,1024]{1,0:T(8,128)(2,1)} %constant.44.clone.refs_2_, ...), custom_call_target="tpu_custom_call" | custom-call | flops 1 | bytes 1048576 | tf_op jit(solution)/shard_map/pallas_call | solution.py:225
  171.4 51.6 %all_to_all.20 = bf16[32,8,16,256]{3,2,1,0:T(8,128)(2,1)} all-to-all(bf16[32,8,16,256]{3,2,1,0:T(8,128)(2,1)S(1)} %get-tuple-element.57), channel_id=1, replica_groups=mesh['lat'=8,'lon'=4] {'lat','lon'}, dimensions={0} | all-to-all | bytes 4194304 | tf_op jit(solution)/shard_map/all_to_all | solution.py:463
  223.0 4.5 %all-to-all-start.2 = ((bf16[32,8,16,256]{3,2,1,0:T(8,128)(2,1)}), bf16[32,8,16,256]{3,2,1,0:T(8,128)(2,1)S(1)}, u32[]{:S(2)}, u32[]{:S(2)}) async-start(bf16[32,8,16,256]{3,2,1,0:T(8,128)(2,1)} %copy-done.8), calls=%async_computation.2 | async-start | bytes 4194304 | tf_op jit(solution)/shard_map/all_to_all | solution.py:463
  231.3 3.2 shard_map.96
  237.9 37.0 %all-to-all-done.2 = bf16[32,8,16,256]{3,2,1,0:T(8,128)(2,1)S(1)} async-done(((bf16[32,8,16,256]{3,2,1,0:T(8,128)(2,1)}), bf16[32,8,16,256]{3,2,1,0:T(8,128)(2,1)S(1)}, u32[]{:S(2)}, u32[]{:S(2)}) %all-to-all-start.2) | async-done | bytes 2097184 | tf_op jit(solution)/shard_map/all_to_all | solution.py:463
  275.0 3.2 collective-permute-done.10.refs_3_
  280.3 4.9 %shard_map.98 = (bf16[64,4,2,32,128]{4,3,2,1,0:T(8,128)(2,1)}, bf16[64,4,16,128]{3,2,1,0:T(8,128)(2,1)S(1)}) custom-call(s32[2]{0:T(128)S(1)} %pad_add_fusion.place_ref, bf16[64,4,2,32,128]{4,3,2,1,0:T(8,128)(2,1)S(1)} %bitcast.37, bf16[16,2,64,128]{3,2,1,0:T(8,128)(2,1)S(1)} %get-tuple-element.67.refs_0_, ...), custom_call_target="tpu_custom_call" | custom-call | flops 1 | bytes 1048576 | tf_op jit(solution)/shard_map/pallas_call | solution.py:225
  285.3 2.3 shard_map.97
  293.0 9.4 %collective-permute-done.11.refs_1_ = bf16[16,2,64,128]{3,2,1,0:T(8,128)(2,1)S(1)} collective-permute-done((bf16[16,2,64,128]{3,2,1,0:T(8,128)(2,1)S(1)}, bf16[16,2,64,128]{3,2,1,0:T(8,128)(2,1)S(1)}, u32[]{:S(2)}, u32[]{:S(2)}) %collective-permute-start.11) | collective-permute-done | bytes 524320 | tf_op jit(solution)/shard_map/ppermute | solution.py:455
  302.4 11.4 %collective-permute-done.12.refs_2_ = bf16[16,2,64,128]{3,2,1,0:T(8,128)(2,1)S(1)} collective-permute-done((bf16[16,2,64,128]{3,2,1,0:T(8,128)(2,1)S(1)}, bf16[16,2,64,128]{3,2,1,0:T(8,128)(2,1)S(1)}, u32[]{:S(2)}, u32[]{:S(2)}) %collective-permute-start.12) | collective-permute-done | bytes 524320 | tf_op jit(solution)/shard_map/ppermute | solution.py:455
  313.8 3.1 shard_map.100
  317.0 2.7 collective-permute-done.15.twin_ref
  (61 shorter events, 31.6 us)
Async XLA Ops:
  3.0 3.9 %collective-permute-start = (bf16[64,4,16,128]{3,2,1,0:T(8,128)(2,1)}, bf16[64,4,16,128]{3,2,1,0:T(8,128)(2,1)S(1)}, u32[]{:S(2)}, u32[]{:S(2)}) collective-permute-start(bf16[64,4,16,128]{3,2,1,0:T(8,128)(2,1)} %get-tuple-element.76), channel_id=1, source_target_pairs={{0,4},{4,0},{8,12},{12,8},{16,20},{20,16},{24,28},{28,24},{1,5},{5... | collective-permute-start | bytes 3145736 | tf_op jit(solution)/shard_map/ppermute | solution.py:455
  3.4 12.3 %collective-permute-start.4 = (bf16[64,4,16,128]{3,2,1,0:T(8,128)(2,1)S(1)}, bf16[64,4,16,128]{3,2,1,0:T(8,128)(2,1)S(1)}, u32[]{:S(2)}, u32[]{:S(2)}) collective-permute-start(bf16[64,4,16,128]{3,2,1,0:T(8,128)(2,1)S(1)} %get-tuple-element.75), channel_id=1, source_target_pairs={{0,4},{4,0},{8,12},{12,8},{16,20},{20,16},{24,28},{28,24},{1,5},{5... | collective-permute-start | bytes 3145736 | tf_op jit(solution)/shard_map/ppermute | solution.py:455
  10.8 16.2 %collective-permute-start.1 = (bf16[16,128,128]{2,1,0:T(8,128)(2,1)S(1)}, bf16[16,128,128]{2,1,0:T(8,128)(2,1)S(1)}, u32[]{:S(2)}, u32[]{:S(2)}) collective-permute-start(bf16[16,128,128]{2,1,0:T(8,128)(2,1)S(1)} %bitcast.52), channel_id=1, source_target_pairs={{0,8},{4,12},{8,0},{12,4},{16,24},{20,28},{24,16},{28,20},{1,9},{5... | collective-permute-start | bytes 1572872 | tf_op jit(solution)/shard_map/ppermute | solution.py:455
  14.2 24.9 %collective-permute-start.2 = (bf16[16,128,128]{2,1,0:T(8,128)(2,1)S(1)}, bf16[16,128,128]{2,1,0:T(8,128)(2,1)S(1)}, u32[]{:S(2)}, u32[]{:S(2)}) collective-permute-start(bf16[16,128,128]{2,1,0:T(8,128)(2,1)S(1)} %bitcast.51), channel_id=1, source_target_pairs={{0,16},{4,20},{8,24},{12,28},{16,0},{20,4},{24,8},{28,12},{1,17},{... | collective-permute-start | bytes 1572872 | tf_op jit(solution)/shard_map/ppermute | solution.py:455
  15.8 23.4 %copy-start.5 = (bf16[8,512,512]{2,1,0:T(8,128)(2,1)S(1)}, bf16[8,512,512]{2,1,0:T(8,128)(2,1)}, u32[]{:S(2)}) copy-start(bf16[8,512,512]{2,1,0:T(8,128)(2,1)} %constant.42.clone.refs_4_) | copy-start | bytes 12582916
  15.8 23.4 %collective-permute-start.3 = (bf16[16,128,128]{2,1,0:T(8,128)(2,1)S(1)}, bf16[16,128,128]{2,1,0:T(8,128)(2,1)S(1)}, u32[]{:S(2)}, u32[]{:S(2)}) collective-permute-start(bf16[16,128,128]{2,1,0:T(8,128)(2,1)S(1)} %bitcast.50), channel_id=1, source_target_pairs={{0,24},{4,28},{8,16},{12,20},{16,8},{20,12},{24,0},{28,4},{1,25},{... | collective-permute-start | bytes 1572872 | tf_op jit(solution)/shard_map/ppermute | solution.py:455
  42.4 61.0 %all-to-all-start = ((bf16[32,8,16,256]{3,2,1,0:T(8,128)(2,1)}), bf16[32,8,16,256]{3,2,1,0:T(8,128)(2,1)}, u32[]{:S(2)}, u32[]{:S(2)}) async-start(bf16[32,8,16,256]{3,2,1,0:T(8,128)(2,1)} %bitcast.9), calls=%async_computation | async-start | bytes 4194304 | tf_op jit(solution)/shard_map/all_to_all | solution.py:463
  47.5 32.7 %collective-permute-start.5 = (bf16[16,128,128]{2,1,0:T(8,128)(2,1)S(1)}, bf16[16,128,128]{2,1,0:T(8,128)(2,1)S(1)}, u32[]{:S(2)}, u32[]{:S(2)}) collective-permute-start(bf16[16,128,128]{2,1,0:T(8,128)(2,1)S(1)} %bitcast.49), channel_id=1, source_target_pairs={{0,8},{4,12},{8,0},{12,4},{16,24},{20,28},{24,16},{28,20},{1,9},{5... | collective-permute-start | bytes 1572872 | tf_op jit(solution)/shard_map/ppermute | solution.py:455
  49.2 30.9 %collective-permute-start.6 = (bf16[16,128,128]{2,1,0:T(8,128)(2,1)S(1)}, bf16[16,128,128]{2,1,0:T(8,128)(2,1)S(1)}, u32[]{:S(2)}, u32[]{:S(2)}) collective-permute-start(bf16[16,128,128]{2,1,0:T(8,128)(2,1)S(1)} %bitcast.48), channel_id=1, source_target_pairs={{0,16},{4,20},{8,24},{12,28},{16,0},{20,4},{24,8},{28,12},{1,17},{... | collective-permute-start | bytes 1572872 | tf_op jit(solution)/shard_map/ppermute | solution.py:455
  50.7 47.2 %collective-permute-start.7 = (bf16[16,128,128]{2,1,0:T(8,128)(2,1)S(1)}, bf16[16,128,128]{2,1,0:T(8,128)(2,1)S(1)}, u32[]{:S(2)}, u32[]{:S(2)}) collective-permute-start(bf16[16,128,128]{2,1,0:T(8,128)(2,1)S(1)} %bitcast.47), channel_id=1, source_target_pairs={{0,24},{4,28},{8,16},{12,20},{16,8},{20,12},{24,0},{28,4},{1,25},{... | collective-permute-start | bytes 1572872 | tf_op jit(solution)/shard_map/ppermute | solution.py:455
  103.4 52.1 %copy-start.9 = (f32[2,1,128]{2,1,0:T(1,128)S(1)}, f32[2,1,128]{2,1,0:T(1,128)}, u32[]{:S(2)}) copy-start(f32[2,1,128]{2,1,0:T(1,128)} %param.11) | copy-start | bytes 3076
  103.4 52.1 %copy-start.10 = (f32[2,1,128]{2,1,0:T(1,128)S(1)}, f32[2,1,128]{2,1,0:T(1,128)}, u32[]{:S(2)}) copy-start(f32[2,1,128]{2,1,0:T(1,128)} %param.13) | copy-start | bytes 3076
  103.4 50.8 %all-to-all-start.1 = ((bf16[32,8,16,256]{3,2,1,0:T(8,128)(2,1)}), bf16[32,8,16,256]{3,2,1,0:T(8,128)(2,1)S(1)}, u32[]{:S(2)}, u32[]{:S(2)}) async-start(bf16[32,8,16,256]{3,2,1,0:T(8,128)(2,1)} %bitcast.14), calls=%async_computation.1 | async-start | bytes 4194304 | tf_op jit(solution)/shard_map/all_to_all | solution.py:463
  171.4 51.6 %copy-start.8 = (bf16[32,8,16,256]{3,2,1,0:T(8,128)(2,1)}, bf16[32,8,16,256]{3,2,1,0:T(8,128)(2,1)S(1)}, u32[]{:S(2)}) copy-start(bf16[32,8,16,256]{3,2,1,0:T(8,128)(2,1)S(1)} %get-tuple-element.56) | copy-start | bytes 6291460
  223.0 51.9 %all-to-all-start.2 = ((bf16[32,8,16,256]{3,2,1,0:T(8,128)(2,1)}), bf16[32,8,16,256]{3,2,1,0:T(8,128)(2,1)S(1)}, u32[]{:S(2)}, u32[]{:S(2)}) async-start(bf16[32,8,16,256]{3,2,1,0:T(8,128)(2,1)} %copy-done.8), calls=%async_computation.2 | async-start | bytes 4194304 | tf_op jit(solution)/shard_map/all_to_all | solution.py:463
  234.4 40.5 %collective-permute-start.8 = (bf16[16,2,64,128]{3,2,1,0:T(8,128)(2,1)}, bf16[16,2,64,128]{3,2,1,0:T(8,128)(2,1)S(1)}, u32[]{:S(2)}, u32[]{:S(2)}) collective-permute-start(bf16[16,2,64,128]{3,2,1,0:T(8,128)(2,1)} %get-tuple-element.59), channel_id=1, source_target_pairs={{0,8},{4,12},{8,0},{12,4},{16,24},{20,28},{24,16},{28,20},{1,9},{5... | collective-permute-start | bytes 1572872 | tf_op jit(solution)/shard_map/ppermute | solution.py:455
  236.2 38.8 %collective-permute-start.9 = (bf16[16,2,64,128]{3,2,1,0:T(8,128)(2,1)}, bf16[16,2,64,128]{3,2,1,0:T(8,128)(2,1)}, u32[]{:S(2)}, u32[]{:S(2)}) collective-permute-start(bf16[16,2,64,128]{3,2,1,0:T(8,128)(2,1)} %get-tuple-element.60), channel_id=1, source_target_pairs={{0,16},{4,20},{8,24},{12,28},{16,0},{20,4},{24,8},{28,12},{1,17},{... | collective-permute-start | bytes 1572872 | tf_op jit(solution)/shard_map/ppermute | solution.py:455
  237.6 40.5 %collective-permute-start.10 = (bf16[16,2,64,128]{3,2,1,0:T(8,128)(2,1)}, bf16[16,2,64,128]{3,2,1,0:T(8,128)(2,1)}, u32[]{:S(2)}, u32[]{:S(2)}) collective-permute-start(bf16[16,2,64,128]{3,2,1,0:T(8,128)(2,1)} %get-tuple-element.61), channel_id=1, source_target_pairs={{0,24},{4,28},{8,16},{12,20},{16,8},{20,12},{24,0},{28,4},{1,25},{... | collective-permute-start | bytes 1572872 | tf_op jit(solution)/shard_map/ppermute | solution.py:455
  285.3 5.9 %copy-start.2 = (bf16[64,256,128]{2,1,0:T(8,128)(2,1)S(1)}, bf16[64,256,128]{2,1,0:T(8,128)(2,1)}, u32[]{:S(2)}) copy-start(bf16[64,256,128]{2,1,0:T(8,128)(2,1)} %param.9) | copy-start | bytes 12582916
  285.3 5.9 %collective-permute-start.14 = (bf16[64,4,16,128]{3,2,1,0:T(8,128)(2,1)S(1)}, bf16[64,4,16,128]{3,2,1,0:T(8,128)(2,1)S(1)}, u32[]{:S(2)}, u32[]{:S(2)}) collective-permute-start(bf16[64,4,16,128]{3,2,1,0:T(8,128)(2,1)S(1)} %get-tuple-element.71), channel_id=1, source_target_pairs={{0,4},{4,0},{8,12},{12,8},{16,20},{20,16},{24,28},{28,24},{1,5},{5... | collective-permute-start | bytes 3145736 | tf_op jit(solution)/shard_map/ppermute | solution.py:455
  287.6 14.8 %collective-permute-start.11 = (bf16[16,2,64,128]{3,2,1,0:T(8,128)(2,1)S(1)}, bf16[16,2,64,128]{3,2,1,0:T(8,128)(2,1)S(1)}, u32[]{:S(2)}, u32[]{:S(2)}) collective-permute-start(bf16[16,2,64,128]{3,2,1,0:T(8,128)(2,1)S(1)} %get-tuple-element.64), channel_id=1, source_target_pairs={{0,8},{4,12},{8,0},{12,4},{16,24},{20,28},{24,16},{28,20},{1,9},{5... | collective-permute-start | bytes 1572872 | tf_op jit(solution)/shard_map/ppermute | solution.py:455
  288.5 25.3 %collective-permute-start.12 = (bf16[16,2,64,128]{3,2,1,0:T(8,128)(2,1)S(1)}, bf16[16,2,64,128]{3,2,1,0:T(8,128)(2,1)S(1)}, u32[]{:S(2)}, u32[]{:S(2)}) collective-permute-start(bf16[16,2,64,128]{3,2,1,0:T(8,128)(2,1)S(1)} %get-tuple-element.65), channel_id=1, source_target_pairs={{0,16},{4,20},{8,24},{12,28},{16,0},{20,4},{24,8},{28,12},{1,17},{... | collective-permute-start | bytes 1572872 | tf_op jit(solution)/shard_map/ppermute | solution.py:455
  288.9 24.9 %collective-permute-start.13 = (bf16[16,2,64,128]{3,2,1,0:T(8,128)(2,1)S(1)}, bf16[16,2,64,128]{3,2,1,0:T(8,128)(2,1)S(1)}, u32[]{:S(2)}, u32[]{:S(2)}) collective-permute-start(bf16[16,2,64,128]{3,2,1,0:T(8,128)(2,1)S(1)} %get-tuple-element.66), channel_id=1, source_target_pairs={{0,24},{4,28},{8,16},{12,20},{16,8},{20,12},{24,0},{28,4},{1,25},{... | collective-permute-start | bytes 1572872 | tf_op jit(solution)/shard_map/ppermute | solution.py:455
  317.0 2.7 collective-permute-start.15
  (9 other events, 23.2 us)

commit v3 on v2

--- a/solution.py
+++ b/solution.py
@@ -197,10 +197,8 @@
     places = np.arange(lat_count)
     tables = [forward[:, p ^ places].reshape(total_lat, total_lat) for p in range(lat_count)]
     tables = np.stack(tables)
-    return (
-        jnp.asarray(tables, jnp.bfloat16),
-        jnp.asarray(tables.transpose(0, 2, 1) * scale, jnp.bfloat16),
-    )
+    back = tables.transpose(0, 2, 1) * scale
+    return jnp.asarray(tables, jnp.bfloat16), jnp.asarray(back, jnp.bfloat16)
 
 
 def lon_tables(cell_order, total_lon, scale):
@@ -247,10 +245,10 @@
     def kernel(place_ref, x_ref, twin_ref, *outs):
         chip = place_ref[0] // 2
         for d in range(chips):
-            outs[d][:, 0] = turn(x_ref[:, chip ^ d, 0])
-            outs[d][:, 1] = turn(twin_ref[:, chip ^ d])
-
-    out = pl.BlockSpec((cells, 2, tile, channels), lambda i, p: (0, 0, i, 0))
+            outs[d][0] = turn(x_ref[:, chip ^ d, 0])
+            outs[d][1] = turn(twin_ref[:, chip ^ d])
+
+    out = pl.BlockSpec((2, cells, tile, channels), lambda i, p: (0, 0, i, 0))
     return call(
         kernel,
         place,
@@ -260,26 +258,26 @@
             pl.BlockSpec((tile, chips, cells, channels), lambda i, p: (i, 0, 0, 0)),
         ],
         [out] * chips,
-        [jax.ShapeDtypeStruct((cells, 2, rows, channels), jnp.bfloat16)] * chips,
+        [jax.ShapeDtypeStruct((2, cells, rows, channels), jnp.bfloat16)] * chips,
         (steps,),
     )
 
 
 def join_own(features, parts, place, start, partial, steps=4):
     rows, chips, _, _, channels = features.shape
-    cells = parts[0].shape[0]
+    cells = parts[0].shape[1]
     tile = rows // steps
 
     def kernel(place_ref, x_ref, *refs):
         out_ref, twin_ref = refs[-2:]
         chip = place_ref[0] // 2
         for d in range(chips):
-            added = x_ref[:, chip ^ d, 0].astype(jnp.float32) + turn(refs[d][:, 0]).astype(jnp.float32)
+            added = x_ref[:, chip ^ d, 0].astype(jnp.float32) + turn(refs[d][0]).astype(jnp.float32)
             out_ref[:, chip ^ d, 0] = added.astype(jnp.bfloat16)
-            twin_ref[:, chip ^ d] = turn(refs[d][:, 1])
+            twin_ref[:, chip ^ d] = turn(refs[d][1])
 
     block = own_block(tile, chips, cells, start, 0)
-    part = pl.BlockSpec((cells, 2, tile, channels), lambda i, p: (0, 0, i, 0))
+    part = pl.BlockSpec((2, cells, tile, channels), lambda i, p: (0, 0, i, 0))
     args, specs, alias = [features, *parts], [block] + [part] * chips, None
     if partial is not None:
         args, specs, alias = args + [partial], specs + [pl.BlockSpec(memory_space=pl.ANY)], {len(args) + 1: 0}
@@ -323,18 +321,70 @@
     )
 
 
+def split_all(features, place, start, cells, steps=4):
+    rows, chips, cores, _, channels = features.shape
+    tile = rows // steps
+
+    def kernel(place_ref, x_ref, out_ref):
+        for j in range(chips * cores):
+            out_ref[j] = turn(x_ref[:, j // cores, j % cores])
+
+    return call(
+        kernel,
+        place,
+        [features],
+        [pl.BlockSpec((tile, chips, cores, cells, channels), lambda i, p: (i, 0, 0, start // cells, 0))],
+        pl.BlockSpec((chips * cores, cells, tile, channels), lambda i, p: (0, 0, i, 0)),
+        jax.ShapeDtypeStruct((chips * cores, cells, rows, channels), jnp.bfloat16),
+        (steps,),
+    )
+
+
+def join_all(features, part, place, start, partial, steps=4):
+    rows, chips, cores, _, channels = features.shape
+    cells = part.shape[1]
+    tile = rows // steps
+
+    def kernel(place_ref, x_ref, part_ref, partial_ref, out_ref):
+        for j in range(chips * cores):
+            at = (slice(None), j // cores, j % cores)
+            added = x_ref[at].astype(jnp.float32) + turn(part_ref[j]).astype(jnp.float32)
+            out_ref[at] = added.astype(jnp.bfloat16)
+
+    block = pl.BlockSpec(
+        (tile, chips, cores, cells, channels), lambda i, p: (i, 0, 0, start // cells, 0)
+    )
+    return call(
+        kernel,
+        place,
+        [features, part, partial],
+        [
+            block,
+            pl.BlockSpec((chips * cores, cells, tile, channels), lambda i, p: (0, 0, i, 0)),
+            pl.BlockSpec(memory_space=pl.ANY),
+        ],
+        block,
+        jax.ShapeDtypeStruct(features.shape, jnp.bfloat16),
+        (steps,),
+        alias={3: 0},
+    )
+
+
 def lat_forward(parts, table, place, step_cells=8):
-    cells, rows, channels = parts[0].shape
+    sources, cells, rows, channels = parts[0].shape
     count = len(parts)
-    total = rows * count
+    total = sources * rows * count
     half = total // 2
 
     def kernel(place_ref, *refs):
         xs, (table_ref, out_ref) = refs[:count], refs[count:]
         sums = []
         for cell in range(0, step_cells, 2):
-            pair = [jnp.concatenate([x[cell + t] for x in xs], axis=0) for t in range(2)]
-            result = dot32(table_ref[0], jnp.concatenate(pair, axis=1)).astype(jnp.bfloat16)
+            pair = [
+                jnp.concatenate([x[j, cell + t] for x in xs for j in range(sources)], axis=0)
+                for t in range(2)
+            ]
+            result = dot32(table_ref[...], jnp.concatenate(pair, axis=1)).astype(jnp.bfloat16)
             sums += [result[:, :channels], result[:, channels:]]
         for part in range(2):
             lines = jnp.stack([v[part * half : (part + 1) * half] for v in sums], axis=0)
@@ -344,29 +394,29 @@
         kernel,
         place,
         [*parts, table],
-        [pl.BlockSpec((step_cells, rows, channels), lambda i, p: (i, 0, 0))] * count
-        + [pl.BlockSpec((1, total, total), lambda i, p: (p[0], 0, 0))],
+        [pl.BlockSpec((sources, step_cells, rows, channels), lambda i, p: (0, i, 0, 0))] * count
+        + [pl.BlockSpec((total, total), lambda i, p: (0, 0))],
         pl.BlockSpec((half, step_cells, 2 * channels), lambda i, p: (0, i, 0)),
         jax.ShapeDtypeStruct((half, cells, 2 * channels), jnp.bfloat16),
         (cells // step_cells,),
     )
 
 
-def lat_back(h, table, place, chips, step_cells=8):
+def lat_back(h, table, place, groups, count, step_cells=8):
     half, cells, width = h.shape
     channels = width // 2
     total = 2 * half
-    rows = total // chips // 2
+    rows = total // groups // count
 
     def kernel(place_ref, h_ref, table_ref, *outs):
         lines = [turn(h_ref[:, :, part * channels : (part + 1) * channels]) for part in range(2)]
         for cell in range(0, step_cells, 2):
             pair = [jnp.concatenate([v[cell + t] for v in lines], axis=0) for t in range(2)]
-            result = dot32(table_ref[0], jnp.concatenate(pair, axis=1)).astype(jnp.bfloat16)
+            result = dot32(table_ref[...], jnp.concatenate(pair, axis=1)).astype(jnp.bfloat16)
             for t in range(2):
-                part = result[:, t * channels : (t + 1) * channels].reshape(chips, 2, rows, channels)
-                for d in range(chips):
-                    outs[d][cell + t] = part[d]
+                part = result[:, t * channels : (t + 1) * channels].reshape(count, groups, rows, channels)
+                for d in range(count):
+                    outs[d][:, cell + t] = part[d]
 
     return call(
         kernel,
@@ -374,10 +424,10 @@
         [h, table],
         [
             pl.BlockSpec((half, step_cells, width), lambda i, p: (0, i, 0)),
-            pl.BlockSpec((1, total, total), lambda i, p: (p[0], 0, 0)),
+            pl.BlockSpec((total, total), lambda i, p: (0, 0)),
         ],
-        [pl.BlockSpec((step_cells, 2, rows, channels), lambda i, p: (i, 0, 0, 0))] * chips,
-        [jax.ShapeDtypeStruct((cells, 2, rows, channels), jnp.bfloat16)] * chips,
+        [pl.BlockSpec((groups, step_cells, rows, channels), lambda i, p: (0, i, 0, 0))] * count,
+        [jax.ShapeDtypeStruct((groups, cells, rows, channels), jnp.bfloat16)] * count,
         (cells // step_cells,),
     )
 
@@ -461,6 +511,10 @@
 
 def swap_all(parts):
     return lax.all_to_all(parts, ("lat", "lon"), split_axis=0, concat_axis=0, tiled=True)
+
+
+def swap_lat(parts):
+    return lax.all_to_all(parts, "lat", split_axis=0, concat_axis=0, tiled=True)
 
 
 def chunk_sizes(cells):
@@ -485,42 +539,39 @@
     lat_place = lax.axis_index("lat")
     first_slot = (lat_place * lon_count + lax.axis_index("lon")) * slots
     place = jnp.stack([lat_place, first_slot]).astype(jnp.int32)
+    own_fwd = lax.dynamic_index_in_dim(lat_fwd, lat_place, 0, keepdims=False)
+    own_inv = lax.dynamic_index_in_dim(lat_inv, lat_place, 0, keepdims=False)
     w1, w2 = complex_weights(w_first), complex_weights(w_second)
     b1, b2 = bias_first.reshape(1, -1), bias_second.reshape(1, -1)
     tie = lax.optimization_barrier
     field = features.reshape(rows, chips, 2, block_cells, channels)
 
-    def prepare(i):
-        for_twin = lax.dynamic_slice(
-            field, (0, 0, 1 - lat_place % 2, starts[i], 0), (rows, chips, 1, sizes[i], channels)
-        )
-        twin = swap(for_twin.reshape(rows, chips, sizes[i], channels), "lat", 1)
-        return split_rows(field, twin, place, starts[i], sizes[i])
-
-    sums, sent = [], prepare(0)
-    for i, size in enumerate(sizes):
-        parts = swap_chips([v.reshape(size, 2 * rows, channels) for v in sent])
-        if i + 1 < count:
-            parts, sent = tie((parts, prepare(i + 1)))
-        part = lat_forward(parts, lat_fwd, place)
-        sums.append(swap_all(part.reshape(devices, slots, size, 2 * channels)))
+    def slot_sums(parts, table, i):
+        part = lat_forward(parts, table, place)
+        return swap_all(part.reshape(devices, slots, sizes[i], 2 * channels))
+
+    first = split_all(field, place, starts[0], sizes[0])
+    later, first = tie((field, first))
+    for_twin = lax.dynamic_slice(
+        later, (0, 0, 1 - lat_place % 2, starts[1], 0), (rows, chips, 1, sizes[1], channels)
+    )
+    twin = swap(for_twin.reshape(rows, chips, sizes[1], channels), "lat", 1)
+    second = split_rows(later, twin, place, starts[1], sizes[1])
+    first, second = tie((swap_lat(first), second))
+    sums = [slot_sums([first], lat_fwd[0], 0), slot_sums(swap_chips(second), own_fwd, 1)]
 
     coefs = spectral_step(sums, place, lon_fwd, lon_inv, w1, b1, w2, b2)
 
-    def finish(i, parts, result):
-        result, for_twin = join_own(field, parts, place, starts[i], result)
-        return join_twin(field, swap(for_twin, "lat", 1), place, starts[i], result)
-
-    result, parts = None, None
-    for i in reversed(range(count)):
-        part = swap_all(coefs[i]).reshape(devices * slots, sizes[i], 2 * channels)
-        if parts is not None:
-            part, parts = tie((part, parts))
-        back = lat_back(part, lat_inv, place, chips)
-        if parts is not None:
-            result = finish(i + 1, parts, result)
-        parts = swap_chips(back)
-    result = finish(0, parts, result)
+    second = swap_all(coefs[1]).reshape(devices * slots, sizes[1], 2 * channels)
+    second = swap_chips(lat_back(second, own_inv, place, 2, chips))
+    first = swap_all(coefs[0]).reshape(devices * slots, sizes[0], 2 * channels)
+    first, second = tie((first, second))
+    first = lat_back(first, lat_inv[0], place, lat_count, 1)[0]
+    first, second = tie((first, second))
+    first = swap_lat(first)
+    result, for_twin = join_own(field, second, place, starts[1], None)
+    result = join_twin(field, swap(for_twin, "lat", 1), place, starts[1], result)
+    result = join_all(field, first, place, starts[0], result)
     return result.reshape(features.shape)
 
 

time: 322 us -> 314 us (0.975)
  waiting for transfers between devices: 183 us -> 170 us
  local copies, waits for them, and re-layouts: 14.7 us -> 19.7 us
    ppermute x16 -> x8, waiting for transfers between devices: 98.5 us -> 53.6 us  [swap(): lax.ppermute(part, axis, [(j, j ^ bits) for j in range(lax.axis_size(axis...]
    all_to_all x0 -> x2, waiting for transfers between devices: none -> 31 us  [swap_lat(): return lax.all_to_all(parts, 'lat', split_axis=0, concat_axis=0, tiled=True)]
    all_to_all x0 -> x2, starting transfers between devices: none -> 8.77 us  [swap_lat(): return lax.all_to_all(parts, 'lat', split_axis=0, concat_axis=0, tiled=True)]
    ppermute x16 -> x8, starting transfers between devices: 16.1 us -> 8 us  [swap(): lax.ppermute(part, axis, [(j, j ^ bits) for j in range(lax.axis_size(axis...]
    unnamed x28 -> x38, local copies, waits for them, and re-layouts: 11.7 us -> 16 us
    pallas_call x11 -> x10, Pallas kernels: 43.1 us -> 42.9 us  [call(): pl.pallas_call(kernel, grid_spec=pltpu.PrefetchScalarGridSpec(num_scalar_...]
  transfers between devices with their start and end apart: 19 -> 13, of which waited for: 11 -> 9; matrix products, arithmetic and copies ran while one was open for 0% -> 1% of each run, Pallas kernels for 4% -> 5%
where the time goes in v3:
time: 314 us; the launch traced here: 313 us
  waiting for transfers between devices  170 us (54%)
  blocking collectives  51.6 us (16%)
  Pallas kernels  42.9 us (14%)
  starting transfers between devices  28.6 us (9%)
  local copies, waits for them, and re-layouts  19.7 us (6%)
    all_to_all x3, waiting for transfers between devices, swap_all(): lax.all_to_all(parts, ('lat', 'lon'), split_axis=0, concat_axis=0, tiled=...  85.4 us
    ppermute x8, waiting for transfers between devices, swap(): lax.ppermute(part, axis, [(j, j ^ bits) for j in range(lax.axis_size(axis...  53.6 us
    all_to_all x1, blocking collectives, swap_all(): lax.all_to_all(parts, ('lat', 'lon'), split_axis=0, concat_axis=0, tiled=...  51.6 us
    pallas_call x10, Pallas kernels, call(): pl.pallas_call(kernel, grid_spec=pltpu.PrefetchScalarGridSpec(num_scalar_...  42.9 us
    all_to_all x2, waiting for transfers between devices, swap_lat(): return lax.all_to_all(parts, 'lat', split_axis=0, concat_axis=0, tiled=True)  31 us
    unnamed x38, local copies, waits for them, and re-layouts  16 us
    all_to_all x3, starting transfers between devices, swap_all(): lax.all_to_all(parts, ('lat', 'lon'), split_axis=0, concat_axis=0, tiled=...  11.8 us
    all_to_all x2, starting transfers between devices, swap_lat(): return lax.all_to_all(parts, 'lat', split_axis=0, concat_axis=0, tiled=True)  8.77 us
  transfers between devices with their start and end apart: 13, of which 9 were waited for; matrix products, arithmetic and copies ran while one was open for 1% of the time, Pallas kernels for 5%

profile of v3, /device:TPU:0, one launch (start us, length us, event | category | flops | bytes accessed | tf_op | source)
XLA Modules:
  0.0 313.1 jit_solution(5863761753880843140)
XLA Ops:
  2.3 2.8 shard_map.91
  5.0 5.2 %all-to-all-start = ((bf16[8,16,64,128]{3,2,1,0:T(8,128)(2,1)}), bf16[8,16,64,128]{3,2,1,0:T(8,128)(2,1)S(1)}, u32[]{:S(2)}, u32[]{:S(2)}) async-start(bf16[8,16,64,128]{3,2,1,0:T(8,128)(2,1)} %shard_map.91), calls=%async_computation | async-start | bytes 4194304 | tf_op jit(solution)/shard_map/all_to_all | solution.py:517
  12.3 2.3 collective-permute-done.twin_ref
  16.8 2.6 shard_map.92
  21.0 15.9 %all-to-all-done.refs_0_ = bf16[8,16,64,128]{3,2,1,0:T(8,128)(2,1)S(1)} async-done(((bf16[8,16,64,128]{3,2,1,0:T(8,128)(2,1)}), bf16[8,16,64,128]{3,2,1,0:T(8,128)(2,1)S(1)}, u32[]{:S(2)}, u32[]{:S(2)}) %all-to-all-start) | async-done | bytes 2097184 | tf_op jit(solution)/shard_map/all_to_all | solution.py:517
  36.9 2.6 shard_map.93
  40.8 4.1 %all-to-all-start.1 = ((bf16[32,8,16,256]{3,2,1,0:T(8,128)(2,1)}), bf16[32,8,16,256]{3,2,1,0:T(8,128)(2,1)}, u32[]{:S(2)}, u32[]{:S(2)}) async-start(bf16[32,8,16,256]{3,2,1,0:T(8,128)(2,1)} %bitcast.35), calls=%async_computation.1 | async-start | bytes 4194304 | tf_op jit(solution)/shard_map/all_to_all | solution.py:513
  49.5 28.1 %collective-permute-done.1.refs_1_ = bf16[2,16,64,128]{3,2,1,0:T(8,128)(2,1)S(1)} collective-permute-done((bf16[2,16,64,128]{3,2,1,0:T(8,128)(2,1)}, bf16[2,16,64,128]{3,2,1,0:T(8,128)(2,1)S(1)}, u32[]{:S(2)}, u32[]{:S(2)}) %collective-permute-start.1) | collective-permute-done | bytes 524320 | tf_op jit(solution)/shard_map/ppermute | solution.py:505
  77.6 17.7 %collective-permute-done.3.refs_3_ = bf16[2,16,64,128]{3,2,1,0:T(8,128)(2,1)S(1)} collective-permute-done((bf16[2,16,64,128]{3,2,1,0:T(8,128)(2,1)S(1)}, bf16[2,16,64,128]{3,2,1,0:T(8,128)(2,1)S(1)}, u32[]{:S(2)}, u32[]{:S(2)}) %collective-permute-start.3) | collective-permute-done | bytes 524320 | tf_op jit(solution)/shard_map/ppermute | solution.py:505
  95.4 3.4 %shard_map.94 = bf16[256,16,256]{2,1,0:T(8,128)(2,1)} custom-call(s32[2]{0:T(128)S(1)} %pad_add_fusion.place_ref, bf16[2,16,64,128]{3,2,1,0:T(8,128)(2,1)S(1)} %get-tuple-element.41.refs_0_, bf16[2,16,64,128]{3,2,1,0:T(8,128)(2,1)S(1)} %collective-permute-done.1.refs_1_, bf16[2,16,64,128]{3,2,1,0:T(8,128)(2,1)S(1)} %collective-permute-done.2.refs_2_, ...), custom_call_target="tpu_custom_call" | custom-call | flops 1 | bytes 1048576 | tf_op jit(solution)/shard_map/pallas_call | solution.py:223
  98.8 3.3 %all-to-all-start.2 = ((bf16[32,8,16,256]{3,2,1,0:T(8,128)(2,1)}), bf16[32,8,16,256]{3,2,1,0:T(8,128)(2,1)S(1)}, u32[]{:S(2)}, u32[]{:S(2)}) async-start(bf16[32,8,16,256]{3,2,1,0:T(8,128)(2,1)} %bitcast.6), calls=%async_computation.2 | async-start | bytes 4194304 | tf_op jit(solution)/shard_map/all_to_all | solution.py:513
  102.2 47.4 %all-to-all-done.2.refs_1_ = bf16[32,8,16,256]{3,2,1,0:T(8,128)(2,1)S(1)} async-done(((bf16[32,8,16,256]{3,2,1,0:T(8,128)(2,1)}), bf16[32,8,16,256]{3,2,1,0:T(8,128)(2,1)S(1)}, u32[]{:S(2)}, u32[]{:S(2)}) %all-to-all-start.2) | async-done | bytes 2097184 | tf_op jit(solution)/shard_map/all_to_all | solution.py:513
  150.9 15.9 %shard_map.95 = (bf16[32,8,16,256]{3,2,1,0:T(8,128)(2,1)S(1)}, bf16[32,8,16,256]{3,2,1,0:T(8,128)(2,1)S(1)}) custom-call(s32[2]{0:T(128)S(1)} %pad_add_fusion.place_ref, bf16[32,8,16,256]{3,2,1,0:T(8,128)(2,1)} %all-to-all-done.1.refs_0_, bf16[32,8,16,256]{3,2,1,0:T(8,128)(2,1)} %copy-done.16, bf16[1024,1024]{1,0:T(8,128)(2,1)} %constant.48.clone.refs_2_, ...), custom_call_target="tpu_custom_call" | custom-call | flops 1 | bytes 1048576 | tf_op jit(solution)/shard_map/pallas_call | solution.py:223
  166.8 51.6 %all_to_all.30 = bf16[32,8,16,256]{3,2,1,0:T(8,128)(2,1)} all-to-all(bf16[32,8,16,256]{3,2,1,0:T(8,128)(2,1)S(1)} %get-tuple-element.46), channel_id=1, replica_groups=mesh['lat'=8,'lon'=4] {'lat','lon'}, dimensions={0} | all-to-all | bytes 4194304 | tf_op jit(solution)/shard_map/all_to_all | solution.py:513
  218.4 4.5 %all-to-all-start.3 = ((bf16[32,8,16,256]{3,2,1,0:T(8,128)(2,1)}), bf16[32,8,16,256]{3,2,1,0:T(8,128)(2,1)S(1)}, u32[]{:S(2)}, u32[]{:S(2)}) async-start(bf16[32,8,16,256]{3,2,1,0:T(8,128)(2,1)} %copy-done.7), calls=%async_computation.3 | async-start | bytes 4194304 | tf_op jit(solution)/shard_map/all_to_all | solution.py:513
  225.6 3.3 %shard_map.96 = (bf16[2,16,64,128]{3,2,1,0:T(8,128)(2,1)S(1)}, bf16[2,16,64,128]{3,2,1,0:T(8,128)(2,1)}, bf16[2,16,64,128]{3,2,1,0:T(8,128)(2,1)}, bf16[2,16,64,128]{3,2,1,0:T(8,128)(2,1)}) custom-call(s32[2]{0:T(128)S(1)} %pad_add_fusion.place_ref, bf16[256,16,256]{2,1,0:T(8,128)(2,1)S(1)} %bitcast.36, ...), custom_call_target="tpu_custom_call" | custom-call | flops 1 | bytes 1048576 | tf_op jit(solution)/shard_map/pallas_call | solution.py:223
  232.4 38.0 %all-to-all-done.3 = bf16[32,8,16,256]{3,2,1,0:T(8,128)(2,1)S(1)} async-done(((bf16[32,8,16,256]{3,2,1,0:T(8,128)(2,1)}), bf16[32,8,16,256]{3,2,1,0:T(8,128)(2,1)S(1)}, u32[]{:S(2)}, u32[]{:S(2)}) %all-to-all-start.3) | async-done | bytes 2097184 | tf_op jit(solution)/shard_map/all_to_all | solution.py:513
  270.4 3.2 %collective-permute-done.6.refs_3_ = bf16[2,16,64,128]{3,2,1,0:T(8,128)(2,1)} collective-permute-done((bf16[2,16,64,128]{3,2,1,0:T(8,128)(2,1)}, bf16[2,16,64,128]{3,2,1,0:T(8,128)(2,1)}, u32[]{:S(2)}, u32[]{:S(2)}) %collective-permute-start.6) | collective-permute-done | bytes 524320 | tf_op jit(solution)/shard_map/ppermute | solution.py:505
  273.6 2.4 shard_map.97
  277.4 3.6 %all-to-all-start.5 = ((bf16[8,16,64,128]{3,2,1,0:T(8,128)(2,1)}), bf16[8,16,64,128]{3,2,1,0:T(8,128)(2,1)S(1)}, u32[]{:S(2)}, u32[]{:S(2)}) async-start(bf16[8,16,64,128]{3,2,1,0:T(8,128)(2,1)} %copy-done.5), calls=%async_computation.5 | async-start | bytes 4194304 | tf_op jit(solution)/shard_map/all_to_all | solution.py:517
  283.2 4.7 %shard_map.98 = (bf16[64,4,2,32,128]{4,3,2,1,0:T(8,128)(2,1)}, bf16[64,4,16,128]{3,2,1,0:T(8,128)(2,1)S(1)}) custom-call(s32[2]{0:T(128)S(1)} %pad_add_fusion.place_ref, bf16[64,4,2,32,128]{4,3,2,1,0:T(8,128)(2,1)S(1)} %bitcast.31, bf16[2,16,64,128]{3,2,1,0:T(8,128)(2,1)S(1)} %get-tuple-element.57.refs_0_, ...), custom_call_target="tpu_custom_call" | custom-call | flops 1 | bytes 1048576 | tf_op jit(solution)/shard_map/pallas_call | solution.py:223
  288.3 2.3 collective-permute-done.7.twin_ref
  292.4 15.2 %all-to-all-done.5.part_ref = bf16[8,16,64,128]{3,2,1,0:T(8,128)(2,1)S(1)} async-done(((bf16[8,16,64,128]{3,2,1,0:T(8,128)(2,1)}), bf16[8,16,64,128]{3,2,1,0:T(8,128)(2,1)S(1)}, u32[]{:S(2)}, u32[]{:S(2)}) %all-to-all-start.5) | async-done | bytes 2097184 | tf_op jit(solution)/shard_map/all_to_all | solution.py:517
  309.8 3.3 %shard_map.100 = bf16[64,4,2,32,128]{4,3,2,1,0:T(8,128)(2,1)} custom-call(s32[2]{0:T(128)S(1)} %pad_add_fusion.place_ref, bf16[64,4,2,32,128]{4,3,2,1,0:T(8,128)(2,1)S(1)} %bitcast.33, bf16[8,16,64,128]{3,2,1,0:T(8,128)(2,1)S(1)} %all-to-all-done.5.part_ref, bf16[64,4,2,32,128]{4,3,2,1,0:T(8,128)(2,1)} %shard_map.99.partial_ref), custom_call_target="tpu_custom_call", output_to_operand_aliasing={{}: (3, {})} | custom-call | flops 1 | bytes 1048576 | tf_op jit(solution)/shard_map/pallas_call | solution.py:223
  (60 shorter events, 29.7 us)
Async XLA Ops:
  5.0 31.8 %all-to-all-start = ((bf16[8,16,64,128]{3,2,1,0:T(8,128)(2,1)}), bf16[8,16,64,128]{3,2,1,0:T(8,128)(2,1)S(1)}, u32[]{:S(2)}, u32[]{:S(2)}) async-start(bf16[8,16,64,128]{3,2,1,0:T(8,128)(2,1)} %shard_map.91), calls=%async_computation | async-start | bytes 4194304 | tf_op jit(solution)/shard_map/all_to_all | solution.py:517
  10.2 26.6 %copy-start.9 = (bf16[512,512]{1,0:T(8,128)(2,1)S(1)}, bf16[512,512]{1,0:T(8,128)(2,1)}, u32[]{:S(2)}) copy-start(bf16[512,512]{1,0:T(8,128)(2,1)} %constant.51.refs_1_) | copy-start | bytes 1572868
  11.7 2.8 collective-permute-start
  40.8 5.9 %copy-start.15 = (bf16[2,16,64,128]{3,2,1,0:T(8,128)(2,1)S(1)}, bf16[2,16,64,128]{3,2,1,0:T(8,128)(2,1)}, u32[]{:S(2)}) copy-start(bf16[2,16,64,128]{3,2,1,0:T(8,128)(2,1)} %copy-done.14) | copy-start | bytes 1572868
  40.8 7.4 %copy-start.13 = (bf16[2,16,64,128]{3,2,1,0:T(8,128)(2,1)S(1)}, bf16[2,16,64,128]{3,2,1,0:T(8,128)(2,1)}, u32[]{:S(2)}) copy-start(bf16[2,16,64,128]{3,2,1,0:T(8,128)(2,1)} %copy-done.12) | copy-start | bytes 1572868
  40.8 58.0 %all-to-all-start.1 = ((bf16[32,8,16,256]{3,2,1,0:T(8,128)(2,1)}), bf16[32,8,16,256]{3,2,1,0:T(8,128)(2,1)}, u32[]{:S(2)}, u32[]{:S(2)}) async-start(bf16[32,8,16,256]{3,2,1,0:T(8,128)(2,1)} %bitcast.35), calls=%async_computation.1 | async-start | bytes 4194304 | tf_op jit(solution)/shard_map/all_to_all | solution.py:513
  44.9 32.7 %collective-permute-start.1 = (bf16[2,16,64,128]{3,2,1,0:T(8,128)(2,1)}, bf16[2,16,64,128]{3,2,1,0:T(8,128)(2,1)S(1)}, u32[]{:S(2)}, u32[]{:S(2)}) collective-permute-start(bf16[2,16,64,128]{3,2,1,0:T(8,128)(2,1)} %get-tuple-element.42), channel_id=1, source_target_pairs={{0,8},{4,12},{8,0},{12,4},{16,24},{20,28},{24,16},{28,20},{1,9},{5... | collective-permute-start | bytes 1572872 | tf_op jit(solution)/shard_map/ppermute | solution.py:505
  46.7 30.9 %collective-permute-start.2 = (bf16[2,16,64,128]{3,2,1,0:T(8,128)(2,1)S(1)}, bf16[2,16,64,128]{3,2,1,0:T(8,128)(2,1)S(1)}, u32[]{:S(2)}, u32[]{:S(2)}) collective-permute-start(bf16[2,16,64,128]{3,2,1,0:T(8,128)(2,1)S(1)} %copy-done.15), channel_id=1, source_target_pairs={{0,16},{4,20},{8,24},{12,28},{16,0},{20,4},{24,8},{28,12},{1,17},{... | collective-permute-start | bytes 1572872 | tf_op jit(solution)/shard_map/ppermute | solution.py:505
  48.1 47.2 %collective-permute-start.3 = (bf16[2,16,64,128]{3,2,1,0:T(8,128)(2,1)S(1)}, bf16[2,16,64,128]{3,2,1,0:T(8,128)(2,1)S(1)}, u32[]{:S(2)}, u32[]{:S(2)}) collective-permute-start(bf16[2,16,64,128]{3,2,1,0:T(8,128)(2,1)S(1)} %copy-done.13), channel_id=1, source_target_pairs={{0,24},{4,28},{8,16},{12,20},{16,8},{20,12},{24,0},{28,4},{1,25},{... | collective-permute-start | bytes 1572872 | tf_op jit(solution)/shard_map/ppermute | solution.py:505
  98.8 3.3 %copy-start.17 = (bf16[2,1,128,128]{3,2,1,0:T(8,128)(2,1)S(1)}, bf16[2,1,128,128]{3,2,1,0:T(8,128)(2,1)}, u32[]{:S(2)}) copy-start(bf16[2,1,128,128]{3,2,1,0:T(8,128)(2,1)} %param.10) | copy-start | bytes 196612
  98.8 3.3 %copy-start.18 = (bf16[2,1,128,128]{3,2,1,0:T(8,128)(2,1)S(1)}, bf16[2,1,128,128]{3,2,1,0:T(8,128)(2,1)}, u32[]{:S(2)}) copy-start(bf16[2,1,128,128]{3,2,1,0:T(8,128)(2,1)} %param.12) | copy-start | bytes 196612
  98.8 52.1 %copy-start.10 = (f32[2,1,128]{2,1,0:T(1,128)S(1)}, f32[2,1,128]{2,1,0:T(1,128)}, u32[]{:S(2)}) copy-start(f32[2,1,128]{2,1,0:T(1,128)} %param.11) | copy-start | bytes 3076
  98.8 52.1 %copy-start.11 = (f32[2,1,128]{2,1,0:T(1,128)S(1)}, f32[2,1,128]{2,1,0:T(1,128)}, u32[]{:S(2)}) copy-start(f32[2,1,128]{2,1,0:T(1,128)} %param.13) | copy-start | bytes 3076
  98.8 50.8 %all-to-all-start.2 = ((bf16[32,8,16,256]{3,2,1,0:T(8,128)(2,1)}), bf16[32,8,16,256]{3,2,1,0:T(8,128)(2,1)S(1)}, u32[]{:S(2)}, u32[]{:S(2)}) async-start(bf16[32,8,16,256]{3,2,1,0:T(8,128)(2,1)} %bitcast.6), calls=%async_computation.2 | async-start | bytes 4194304 | tf_op jit(solution)/shard_map/all_to_all | solution.py:513
  166.8 51.6 %copy-start.7 = (bf16[32,8,16,256]{3,2,1,0:T(8,128)(2,1)}, bf16[32,8,16,256]{3,2,1,0:T(8,128)(2,1)S(1)}, u32[]{:S(2)}) copy-start(bf16[32,8,16,256]{3,2,1,0:T(8,128)(2,1)S(1)} %get-tuple-element.45) | copy-start | bytes 6291460
  218.4 52.0 %all-to-all-start.3 = ((bf16[32,8,16,256]{3,2,1,0:T(8,128)(2,1)}), bf16[32,8,16,256]{3,2,1,0:T(8,128)(2,1)S(1)}, u32[]{:S(2)}, u32[]{:S(2)}) async-start(bf16[32,8,16,256]{3,2,1,0:T(8,128)(2,1)} %copy-done.7), calls=%async_computation.3 | async-start | bytes 4194304 | tf_op jit(solution)/shard_map/all_to_all | solution.py:513
  222.9 50.7 %copy-start.8 = (bf16[512,512]{1,0:T(8,128)(2,1)S(1)}, bf16[512,512]{1,0:T(8,128)(2,1)}, u32[]{:S(2)}) copy-start(bf16[512,512]{1,0:T(8,128)(2,1)} %constant.53.table_ref) | copy-start | bytes 1572868
  228.9 41.5 %collective-permute-start.4 = (bf16[2,16,64,128]{3,2,1,0:T(8,128)(2,1)}, bf16[2,16,64,128]{3,2,1,0:T(8,128)(2,1)}, u32[]{:S(2)}, u32[]{:S(2)}) collective-permute-start(bf16[2,16,64,128]{3,2,1,0:T(8,128)(2,1)} %get-tuple-element.48), channel_id=1, source_target_pairs={{0,8},{4,12},{8,0},{12,4},{16,24},{20,28},{24,16},{28,20},{1,9},{5... | collective-permute-start | bytes 1572872 | tf_op jit(solution)/shard_map/ppermute | solution.py:505
  230.7 39.7 %collective-permute-start.5 = (bf16[2,16,64,128]{3,2,1,0:T(8,128)(2,1)}, bf16[2,16,64,128]{3,2,1,0:T(8,128)(2,1)}, u32[]{:S(2)}, u32[]{:S(2)}) collective-permute-start(bf16[2,16,64,128]{3,2,1,0:T(8,128)(2,1)} %get-tuple-element.49), channel_id=1, source_target_pairs={{0,16},{4,20},{8,24},{12,28},{16,0},{20,4},{24,8},{28,12},{1,17},{... | collective-permute-start | bytes 1572872 | tf_op jit(solution)/shard_map/ppermute | solution.py:505
  232.2 41.4 %collective-permute-start.6 = (bf16[2,16,64,128]{3,2,1,0:T(8,128)(2,1)}, bf16[2,16,64,128]{3,2,1,0:T(8,128)(2,1)}, u32[]{:S(2)}, u32[]{:S(2)}) collective-permute-start(bf16[2,16,64,128]{3,2,1,0:T(8,128)(2,1)} %get-tuple-element.50), channel_id=1, source_target_pairs={{0,24},{4,28},{8,16},{12,20},{16,8},{20,12},{24,0},{28,4},{1,25},{... | collective-permute-start | bytes 1572872 | tf_op jit(solution)/shard_map/ppermute | solution.py:505
  277.4 30.2 %all-to-all-start.5 = ((bf16[8,16,64,128]{3,2,1,0:T(8,128)(2,1)}), bf16[8,16,64,128]{3,2,1,0:T(8,128)(2,1)S(1)}, u32[]{:S(2)}, u32[]{:S(2)}) async-start(bf16[8,16,64,128]{3,2,1,0:T(8,128)(2,1)} %copy-done.5), calls=%async_computation.5 | async-start | bytes 4194304 | tf_op jit(solution)/shard_map/all_to_all | solution.py:517
  281.0 2.2 copy-start.2
  287.9 2.7 collective-permute-start.7
  307.6 2.2 copy-start.3
  (8 other events, 11.6 us)

commit v4 on v2

--- a/solution.py
+++ b/solution.py
@@ -186,21 +186,13 @@
     return (features.astype(jnp.float32) + filtered.astype(jnp.float32)).astype(jnp.bfloat16)
 
 
-def lat_tables(total_lat, lat_count, scale):
-    half = total_lat // 2
+def lat_tables(total_lat, scale, order):
     row = np.arange(total_lat)
-    angle = (np.outer(np.arange(half), row) % total_lat) * (2.0 * np.pi / total_lat)
+    angle = (np.outer(np.arange(total_lat // 2), row) % total_lat) * (2.0 * np.pi / total_lat)
     sin_part = np.sin(angle)
     sin_part[0] = np.where(row % 2 == 0, 1.0, -1.0)
-    forward = np.concatenate([np.cos(angle), sin_part], axis=0)
-    forward = forward.reshape(total_lat, lat_count, total_lat // lat_count)
-    places = np.arange(lat_count)
-    tables = [forward[:, p ^ places].reshape(total_lat, total_lat) for p in range(lat_count)]
-    tables = np.stack(tables)
-    return (
-        jnp.asarray(tables, jnp.bfloat16),
-        jnp.asarray(tables.transpose(0, 2, 1) * scale, jnp.bfloat16),
-    )
+    forward = np.concatenate([np.cos(angle)[order], sin_part[order]], axis=0)
+    return forward.astype(jnp.bfloat16), (forward.T * scale).astype(jnp.bfloat16)
 
 
 def lon_tables(cell_order, total_lon, scale):
@@ -221,11 +213,15 @@
     return jnp.transpose(values, (1, 0, 2))
 
 
-def call(kernel, place, args, in_specs, out_specs, out_shape, grid, mib=24, alias=None):
+def call(kernel, place, args, in_specs, out_specs, out_shape, grid, scratch=(), mib=24, alias=None):
     return pl.pallas_call(
         kernel,
         grid_spec=pltpu.PrefetchScalarGridSpec(
-            num_scalar_prefetch=1, grid=grid, in_specs=in_specs, out_specs=out_specs
+            num_scalar_prefetch=1,
+            grid=grid,
+            in_specs=in_specs,
+            out_specs=out_specs,
+            scratch_shapes=scratch,
         ),
         out_shape=out_shape,
         input_output_aliases=alias or {},
@@ -234,52 +230,70 @@
     )(place, *args)
 
 
+def split_all(features, place, start, cells, steps=4):
+    rows, chips, cores, _, channels = features.shape
+    tile = rows // steps
+
+    def kernel(place_ref, x_ref, out_ref):
+        for j in range(chips * cores):
+            out_ref[j] = turn(x_ref[:, j // cores, j % cores])
+
+    return call(
+        kernel,
+        place,
+        [features],
+        [pl.BlockSpec((tile, chips, cores, cells, channels), lambda i, p: (i, 0, 0, start // cells, 0))],
+        pl.BlockSpec((chips * cores, cells, tile, channels), lambda i, p: (0, 0, i, 0)),
+        jax.ShapeDtypeStruct((chips * cores, cells, rows, channels), jnp.bfloat16),
+        (steps,),
+    )
+
+
+def join_all(features, part, place, start, partial, steps=4):
+    rows, chips, cores, _, channels = features.shape
+    cells = part.shape[1]
+    tile = rows // steps
+
+    def kernel(place_ref, x_ref, part_ref, *refs):
+        out_ref = refs[-1]
+        for j in range(chips * cores):
+            at = (slice(None), j // cores, j % cores)
+            added = x_ref[at].astype(jnp.float32) + turn(part_ref[j]).astype(jnp.float32)
+            out_ref[at] = added.astype(jnp.bfloat16)
+
+    block = pl.BlockSpec(
+        (tile, chips, cores, cells, channels), lambda i, p: (i, 0, 0, start // cells, 0)
+    )
+    args = [features, part]
+    specs = [block, pl.BlockSpec((chips * cores, cells, tile, channels), lambda i, p: (0, 0, i, 0))]
+    alias = None
+    if partial is not None:
+        args, specs, alias = args + [partial], specs + [pl.BlockSpec(memory_space=pl.ANY)], {3: 0}
+    shape = jax.ShapeDtypeStruct(features.shape, jnp.bfloat16)
+    return call(kernel, place, args, specs, block, shape, (steps,), alias=alias)
+
+
 def own_block(tile, chips, cells, start, flip):
     return pl.BlockSpec(
         (tile, chips, 1, cells, 128), lambda i, p: (i, 0, (p[0] % 2) ^ flip, start // cells, 0)
     )
 
 
-def split_rows(features, twin, place, start, cells, steps=4):
-    rows, chips, _, _, channels = features.shape
-    tile = rows // steps
-
-    def kernel(place_ref, x_ref, twin_ref, *outs):
-        chip = place_ref[0] // 2
-        for d in range(chips):
-            outs[d][:, 0] = turn(x_ref[:, chip ^ d, 0])
-            outs[d][:, 1] = turn(twin_ref[:, chip ^ d])
-
-    out = pl.BlockSpec((cells, 2, tile, channels), lambda i, p: (0, 0, i, 0))
-    return call(
-        kernel,
-        place,
-        [features, twin],
-        [
-            own_block(tile, chips, cells, start, 0),
-            pl.BlockSpec((tile, chips, cells, channels), lambda i, p: (i, 0, 0, 0)),
-        ],
-        [out] * chips,
-        [jax.ShapeDtypeStruct((cells, 2, rows, channels), jnp.bfloat16)] * chips,
-        (steps,),
-    )
-
-
 def join_own(features, parts, place, start, partial, steps=4):
     rows, chips, _, _, channels = features.shape
-    cells = parts[0].shape[0]
+    cells = parts[0].shape[1]
     tile = rows // steps
 
     def kernel(place_ref, x_ref, *refs):
         out_ref, twin_ref = refs[-2:]
         chip = place_ref[0] // 2
         for d in range(chips):
-            added = x_ref[:, chip ^ d, 0].astype(jnp.float32) + turn(refs[d][:, 0]).astype(jnp.float32)
+            added = x_ref[:, chip ^ d, 0].astype(jnp.float32) + turn(refs[d][0]).astype(jnp.float32)
             out_ref[:, chip ^ d, 0] = added.astype(jnp.bfloat16)
-            twin_ref[:, chip ^ d] = turn(refs[d][:, 1])
+            twin_ref[:, chip ^ d] = turn(refs[d][1])
 
     block = own_block(tile, chips, cells, start, 0)
-    part = pl.BlockSpec((cells, 2, tile, channels), lambda i, p: (0, 0, i, 0))
+    part = pl.BlockSpec((2, cells, tile, channels), lambda i, p: (0, 0, i, 0))
     args, specs, alias = [features, *parts], [block] + [part] * chips, None
     if partial is not None:
         args, specs, alias = args + [partial], specs + [pl.BlockSpec(memory_space=pl.ANY)], {len(args) + 1: 0}
@@ -323,50 +337,83 @@
     )
 
 
-def lat_forward(parts, table, place, step_cells=8):
-    cells, rows, channels = parts[0].shape
-    count = len(parts)
-    total = rows * count
+def lat_forward(part, table, place, step_cells=8):
+    sources, cells, rows, channels = part.shape
+    total = sources * rows
     half = total // 2
 
-    def kernel(place_ref, *refs):
-        xs, (table_ref, out_ref) = refs[:count], refs[count:]
-        sums = []
-        for cell in range(0, step_cells, 2):
-            pair = [jnp.concatenate([x[cell + t] for x in xs], axis=0) for t in range(2)]
-            result = dot32(table_ref[0], jnp.concatenate(pair, axis=1)).astype(jnp.bfloat16)
-            sums += [result[:, :channels], result[:, channels:]]
-        for part in range(2):
-            lines = jnp.stack([v[part * half : (part + 1) * half] for v in sums], axis=0)
-            out_ref[:, :, part * channels : (part + 1) * channels] = turn(lines)
-
-    return call(
-        kernel,
-        place,
-        [*parts, table],
-        [pl.BlockSpec((step_cells, rows, channels), lambda i, p: (i, 0, 0))] * count
-        + [pl.BlockSpec((1, total, total), lambda i, p: (p[0], 0, 0))],
+    def kernel(place_ref, x_ref, table_ref, out_ref):
+        sums = lat_sums(x_ref, table_ref, step_cells)
+        for t in range(2):
+            lines = jnp.stack([v[t * half : (t + 1) * half] for v in sums], axis=0)
+            out_ref[:, :, t * channels : (t + 1) * channels] = turn(lines)
+
+    return call(
+        kernel,
+        place,
+        [part, table],
+        [
+            pl.BlockSpec((sources, step_cells, rows, channels), lambda i, p: (0, i, 0, 0)),
+            pl.BlockSpec((total, total), lambda i, p: (0, 0)),
+        ],
         pl.BlockSpec((half, step_cells, 2 * channels), lambda i, p: (0, i, 0)),
         jax.ShapeDtypeStruct((half, cells, 2 * channels), jnp.bfloat16),
         (cells // step_cells,),
     )
 
 
-def lat_back(h, table, place, chips, step_cells=8):
+def lat_sums(x_ref, table_ref, cells):
+    sources, channels = x_ref.shape[0], x_ref.shape[3]
+    sums = []
+    for cell in range(0, cells, 2):
+        pair = [jnp.concatenate([x_ref[j, cell + t] for j in range(sources)], axis=0) for t in range(2)]
+        result = dot32(table_ref[...], jnp.concatenate(pair, axis=1)).astype(jnp.bfloat16)
+        sums += [result[:, :channels], result[:, channels:]]
+    return sums
+
+
+def lat_forward_groups(part, table, place, groups):
+    sources, cells, rows, channels = part.shape
+    total = sources * rows
+    half = total // 2
+    size = half // groups
+
+    def kernel(place_ref, x_ref, table_ref, *refs):
+        outs, stage = refs[:-1], refs[-1]
+        for cell, value in enumerate(lat_sums(x_ref, table_ref, cells)):
+            stage[:, :, cell] = value.reshape(2, groups, size, channels)
+        for e in range(groups):
+            for t in range(2):
+                outs[e][:, :, t * channels : (t + 1) * channels] = turn(stage[t, place_ref[2] ^ e])
+
+    shape = (size, cells, 2 * channels)
+    return call(
+        kernel,
+        place,
+        [part, table],
+        [pl.BlockSpec(part.shape, lambda i, p: (0, 0, 0, 0)), pl.BlockSpec((total, total), lambda i, p: (0, 0))],
+        [pl.BlockSpec(shape, lambda i, p: (0, 0, 0))] * groups,
+        [jax.ShapeDtypeStruct(shape, jnp.bfloat16)] * groups,
+        (1,),
+        [pltpu.VMEM((2, groups, cells, size, channels), jnp.bfloat16)],
+    )
+
+
+def lat_back(h, table, place, groups, count, step_cells=8):
     half, cells, width = h.shape
     channels = width // 2
     total = 2 * half
-    rows = total // chips // 2
+    rows = total // groups // count
 
     def kernel(place_ref, h_ref, table_ref, *outs):
         lines = [turn(h_ref[:, :, part * channels : (part + 1) * channels]) for part in range(2)]
         for cell in range(0, step_cells, 2):
             pair = [jnp.concatenate([v[cell + t] for v in lines], axis=0) for t in range(2)]
-            result = dot32(table_ref[0], jnp.concatenate(pair, axis=1)).astype(jnp.bfloat16)
+            result = dot32(table_ref[...], jnp.concatenate(pair, axis=1)).astype(jnp.bfloat16)
             for t in range(2):
-                part = result[:, t * channels : (t + 1) * channels].reshape(chips, 2, rows, channels)
-                for d in range(chips):
-                    outs[d][cell + t] = part[d]
+                part = result[:, t * channels : (t + 1) * channels].reshape(count, groups, rows, channels)
+                for d in range(count):
+                    outs[d][:, cell + t] = part[d]
 
     return call(
         kernel,
@@ -374,28 +421,57 @@
         [h, table],
         [
             pl.BlockSpec((half, step_cells, width), lambda i, p: (0, i, 0)),
-            pl.BlockSpec((1, total, total), lambda i, p: (p[0], 0, 0)),
+            pl.BlockSpec((total, total), lambda i, p: (0, 0)),
         ],
-        [pl.BlockSpec((step_cells, 2, rows, channels), lambda i, p: (i, 0, 0, 0))] * chips,
-        [jax.ShapeDtypeStruct((cells, 2, rows, channels), jnp.bfloat16)] * chips,
+        [pl.BlockSpec((groups, step_cells, rows, channels), lambda i, p: (0, i, 0, 0))] * count,
+        [jax.ShapeDtypeStruct((groups, cells, rows, channels), jnp.bfloat16)] * count,
         (cells // step_cells,),
     )
 
 
-def spectral_step(chunks, place, fwd, inv, w1, b1, w2, b2, together=2):
-    count = len(chunks)
-    sources, slots, _, width = chunks[0].shape
+def merge(chunks, place):
+    count, groups = len(chunks), len(chunks[0])
+    targets, slots, cells, width = chunks[0][0].shape
+
+    def kernel(place_ref, *refs):
+        ins, outs = refs[: count * groups], refs[count * groups :]
+        for d in range(targets):
+            for c in range(count):
+                for e in range(groups):
+                    outs[d][e, :, c * cells : (c + 1) * cells] = ins[c * groups + e][place_ref[0] ^ d]
+
+    shape = (groups, slots, count * cells, width)
+    return call(
+        kernel,
+        place,
+        [v for chunk in chunks for v in chunk],
+        [pl.BlockSpec(chunks[0][0].shape, lambda i, p: (0, 0, 0, 0))] * (count * groups),
+        [pl.BlockSpec(shape, lambda i, p: (0, 0, 0, 0))] * targets,
+        [jax.ShapeDtypeStruct(shape, jnp.bfloat16)] * targets,
+        (1,),
+    )
+
+
+def spectral_step(parts, chunk, place, fwd, inv, w1, b1, w2, b2, together=2):
+    targets = len(parts)
+    groups, slots, cells, width = parts[0].shape
     channels = width // 2
-    sizes = [sources * g.shape[2] for g in chunks]
-    total = sum(sizes)
+    sources, _, more, _ = chunk.shape
+    first = targets * groups * cells
+    total = first + sources * more
     keep = total // 2
 
     def kernel(place_ref, *refs):
-        gs, (fwd_ref, inv_ref, w1_ref, b1_ref, w2_ref, b2_ref) = refs[:count], refs[count : count + 6]
-        outs = refs[count + 6 :]
+        ins, g_ref, refs = refs[:targets], refs[targets], refs[targets + 1 :]
+        fwd_ref, inv_ref, w1_ref, b1_ref, w2_ref, b2_ref = refs[:6]
+        near_ref, out_ref, stage = refs[6:]
+        pairs = [(d, e) for d in range(targets) for e in range(groups)]
 
         def waves(u):
-            sums = jnp.concatenate([g[:, u].reshape(size, width) for g, size in zip(gs, sizes)], axis=0)
+            for d, e in pairs:
+                stage[u, place_ref[0] ^ d, place_ref[2] ^ e] = ins[d][e, u]
+            near = stage[u].reshape(first, width)
+            sums = jnp.concatenate([near, g_ref[:, u].reshape(total - first, width)], axis=0)
             return dot32(fwd_ref[...], sums)
 
         def mix(u, both):
@@ -418,32 +494,28 @@
 
         def back(u, coefs):
             lines = dot32(inv_ref[...], coefs).astype(jnp.bfloat16)
-            first = 0
-            for out_ref, size in zip(outs, sizes):
-                out_ref[:, u] = lines[first : first + size].reshape(sources, size // sources, width)
-                first += size
+            out_ref[:, u] = lines[first:].reshape(sources, more, width)
+            near_ref[:, u] = lines[:first].reshape(sources, cells, width)
 
         both = [waves(u) for u in range(together)]
         coefs = [mix(u, both[u]) for u in range(together)]
         for u in range(together):
             back(u, coefs[u])
 
-    def block(g):
-        return pl.BlockSpec((sources, together) + g.shape[2:], lambda i, p: (0, i, 0, 0))
-
+    near = pl.BlockSpec((groups, together, cells, width), lambda i, p: (0, i, 0, 0))
+    block = pl.BlockSpec((sources, together, more, width), lambda i, p: (0, i, 0, 0))
     tables = [fwd, inv, w1, b1, w2, b2]
     return call(
         kernel,
         place,
-        [*chunks, *tables],
-        [block(g) for g in chunks] + [pl.BlockSpec(v.shape, lambda i, p: (0, 0)) for v in tables],
-        [block(g) for g in chunks],
-        [jax.ShapeDtypeStruct(g.shape, jnp.bfloat16) for g in chunks],
+        [*parts, chunk, *tables],
+        [near] * targets + [block] + [pl.BlockSpec(v.shape, lambda i, p: (0, 0)) for v in tables],
+        [pl.BlockSpec((sources, together, cells, width), lambda i, p: (0, i, 0, 0)), block],
+        [jax.ShapeDtypeStruct((sources, slots, n, width), jnp.bfloat16) for n in (cells, more)],
         (slots // together,),
+        [pltpu.VMEM((together, targets, groups, cells, width), jnp.bfloat16)],
         mib=48,
     )
-
-
 def complex_weights(weights):
     real, imag = weights[0, 0], weights[1, 0]
     return jnp.concatenate(
@@ -451,76 +523,84 @@
     )
 
 
-def swap(part, axis, bits):
+def swap(parts, axis):
+    return [parts[0]] + [swap_bits(parts[d], axis, d) for d in range(1, len(parts))]
+
+
+def swap_bits(part, axis, bits):
     return lax.ppermute(part, axis, [(j, j ^ bits) for j in range(lax.axis_size(axis))])
 
 
 def swap_chips(parts):
-    return [parts[0]] + [swap(parts[d], "lat", 2 * d) for d in range(1, len(parts))]
+    return [parts[0]] + [swap_bits(parts[d], "lat", 2 * d) for d in range(1, len(parts))]
+
+
+def swap_lat(parts):
+    return lax.all_to_all(parts, "lat", split_axis=0, concat_axis=0, tiled=True)
 
 
 def swap_all(parts):
     return lax.all_to_all(parts, ("lat", "lon"), split_axis=0, concat_axis=0, tiled=True)
-
-
-def chunk_sizes(cells):
-    return [cells // 2, cells // 2]
 
 
 def lat_first_body(features, w_first, bias_first, w_second, bias_second):
     rows, lon_cells, channels = features.shape
     lat_count, lon_count = lax.axis_size("lat"), lax.axis_size("lon")
     total_lat, total_lon = rows * lat_count, lon_cells * lon_count
-    devices, chips = lat_count * lon_count, lat_count // 2
+    devices, width = lat_count * lon_count, 2 * channels
     block_cells = lon_cells // lat_count
     slots = total_lat // 2 // devices
     norm = 1.0 / math.sqrt(total_lat * total_lon)
-    sizes = chunk_sizes(block_cells)
-    count = len(sizes)
-    starts = [sum(sizes[:i]) for i in range(count)]
-    cell_index = np.arange(total_lon).reshape(lon_count, lat_count, block_cells).transpose(1, 0, 2)
-    order = [cell_index[..., s : s + n].reshape(-1) for s, n in zip(starts, sizes)]
-    lat_fwd, lat_inv = lat_tables(total_lat, lat_count, norm)
-    lon_fwd, lon_inv = lon_tables(np.concatenate(order), total_lon, norm)
-    lat_place = lax.axis_index("lat")
-    first_slot = (lat_place * lon_count + lax.axis_index("lon")) * slots
-    place = jnp.stack([lat_place, first_slot]).astype(jnp.int32)
+    half = block_cells // 2
+    sizes, starts = [half // 2, half // 2, half], [0, half // 2, half]
+    cell_index = np.arange(total_lon).reshape(lon_count, lat_count, 2, half).transpose(2, 1, 0, 3)
+    lon_fwd, lon_inv = lon_tables(cell_index.reshape(-1), total_lon, norm)
+    slot_l = np.arange(total_lat // 2)
+    lat_fwd, lat_inv = lat_tables(total_lat, norm, slot_l)
+    by_lon = slot_l.reshape(lat_count, lon_count, slots).transpose(1, 0, 2).reshape(-1)
+    lon_first_fwd, _ = lat_tables(total_lat, norm, by_lon)
+    places = np.arange(lat_count)
+    by_place = lat_inv.reshape(lat_count, rows, total_lat)
+    own_inv = np.stack([by_place[p ^ places].reshape(lat_inv.shape) for p in range(lat_count)])
+    lat_place, lon_place = lax.axis_index("lat"), lax.axis_index("lon")
+    first_slot = (lat_place * lon_count + lon_place) * slots
+    place = jnp.stack([lat_place, first_slot, lon_place]).astype(jnp.int32)
+    own_inv = lax.dynamic_index_in_dim(jnp.asarray(own_inv), lat_place, 0, keepdims=False)
     w1, w2 = complex_weights(w_first), complex_weights(w_second)
     b1, b2 = bias_first.reshape(1, -1), bias_second.reshape(1, -1)
     tie = lax.optimization_barrier
-    field = features.reshape(rows, chips, 2, block_cells, channels)
-
-    def prepare(i):
-        for_twin = lax.dynamic_slice(
-            field, (0, 0, 1 - lat_place % 2, starts[i], 0), (rows, chips, 1, sizes[i], channels)
-        )
-        twin = swap(for_twin.reshape(rows, chips, sizes[i], channels), "lat", 1)
-        return split_rows(field, twin, place, starts[i], sizes[i])
-
-    sums, sent = [], prepare(0)
-    for i, size in enumerate(sizes):
-        parts = swap_chips([v.reshape(size, 2 * rows, channels) for v in sent])
-        if i + 1 < count:
-            parts, sent = tie((parts, prepare(i + 1)))
-        part = lat_forward(parts, lat_fwd, place)
-        sums.append(swap_all(part.reshape(devices, slots, size, 2 * channels)))
-
-    coefs = spectral_step(sums, place, lon_fwd, lon_inv, w1, b1, w2, b2)
-
-    def finish(i, parts, result):
-        result, for_twin = join_own(field, parts, place, starts[i], result)
-        return join_twin(field, swap(for_twin, "lat", 1), place, starts[i], result)
-
-    result, parts = None, None
-    for i in reversed(range(count)):
-        part = swap_all(coefs[i]).reshape(devices * slots, sizes[i], 2 * channels)
-        if parts is not None:
-            part, parts = tie((part, parts))
-        back = lat_back(part, lat_inv, place, chips)
-        if parts is not None:
-            result = finish(i + 1, parts, result)
-        parts = swap_chips(back)
-    result = finish(0, parts, result)
+    field = features.reshape(rows, lat_count // 2, 2, block_cells, channels)
+
+    sent = split_all(field, place, starts[0], sizes[0])
+    later, sent = tie((field, sent))
+    waiting = [split_all(later, place, starts[i], sizes[i]) for i in (1, 2)]
+    got, waiting = tie((swap_lat(sent), waiting))
+    across = []
+    for i in range(2):
+        groups = lat_forward_groups(got, lon_first_fwd, place, lon_count)
+        sent, groups = tie((waiting[i], groups))
+        if across:
+            sent, across[-1] = tie((sent, across[-1]))
+        got = swap_lat(sent)
+        across.append(swap(groups, "lon"))
+    last = lat_forward(got, lat_fwd, place)
+    last, across[-1] = tie((last, across[-1]))
+    last = swap_all(last.reshape(devices, slots, sizes[2], width))
+    near = [[v.reshape(lat_count, slots, sizes[0], width) for v in groups] for groups in across]
+    near = swap(merge(near, place), "lat")
+
+    near, last = spectral_step(near, last, place, lon_fwd, lon_inv, w1, b1, w2, b2)
+
+    last = swap_all(last).reshape(devices * slots, half, width)
+    last = swap_chips(lat_back(last, own_inv, place, 2, lat_count // 2))
+    near = swap_all(near).reshape(devices * slots, half, width)
+    near, last = tie((near, last))
+    near = lat_back(near, lat_inv, place, lat_count, 1)[0]
+    near, last = tie((near, last))
+    near = swap_lat(near)
+    result, for_twin = join_own(field, last, place, half, None)
+    result = join_twin(field, swap_bits(for_twin, "lat", 1), place, half, result)
+    result = join_all(field, near, place, 0, result)
     return result.reshape(features.shape)
 
 
@@ -528,10 +608,11 @@
     rows, lon_cells, channels = features.shape
     lat_count, lon_count = lax.axis_size("lat"), lax.axis_size("lon")
     fits = (
-        (rows * lat_count // 2) % (lat_count * lon_count) == 0
+        (rows * lat_count) % (4 * lat_count * lon_count) == 0
         and lat_count & (lat_count - 1) == 0
         and lat_count > 1
         and lon_cells % (32 * lat_count) == 0
+        and lon_count & (lon_count - 1) == 0
         and rows % 64 == 0
         and channels == 128
         and w_first.shape[1] == 1

time: 322 us -> 309 us (0.960)
  waiting for transfers between devices: 183 us -> 143 us
  starting transfers between devices: 28.9 us -> 49.7 us
  Pallas kernels: 43.1 us -> 49.1 us
    all_to_all x0 -> x4, waiting for transfers between devices: none -> 53.1 us  [swap_lat(): return lax.all_to_all(parts, 'lat', split_axis=0, concat_axis=0, tiled=True)]
    ppermute x16 -> x17, waiting for transfers between devices: 98.5 us -> 51.9 us  [swap_bits(): lax.ppermute(part, axis, [(j, j ^ bits) for j in range(lax.axis_size(axis...]
    all_to_all x3 -> x2, waiting for transfers between devices: 84.5 us -> 38 us  [swap_all(): lax.all_to_all(parts, ('lat', 'lon'), split_axis=0, concat_axis=0, tiled=...]
    all_to_all x0 -> x4, starting transfers between devices: none -> 16.4 us  [swap_lat(): return lax.all_to_all(parts, 'lat', split_axis=0, concat_axis=0, tiled=True)]
    ppermute x16 -> x17, starting transfers between devices: 16.1 us -> 22.3 us  [swap_bits(): lax.ppermute(part, axis, [(j, j ^ bits) for j in range(lax.axis_size(axis...]
    pallas_call x11 -> x13, Pallas kernels: 43.1 us -> 49.1 us  [call(): pl.pallas_call(kernel, grid_spec=pltpu.PrefetchScalarGridSpec(num_scalar_...]
    unnamed x28 -> x42, local copies, waits for them, and re-layouts: 11.7 us -> 13.8 us
    all_to_all x3 -> x2, starting transfers between devices: 12.8 us -> 11 us  [swap_all(): lax.all_to_all(parts, ('lat', 'lon'), split_axis=0, concat_axis=0, tiled=...]
  transfers between devices with their start and end apart: 19 -> 23, of which waited for: 11 -> 12; matrix products, arithmetic and copies ran while one was open for 0% -> 0% of each run, Pallas kernels for 4% -> 7%
where the time goes in v4:
time: 309 us; the launch traced here: 308 us
  waiting for transfers between devices  143 us (46%)
  blocking collectives  51.1 us (17%)
  starting transfers between devices  49.7 us (16%)
  Pallas kernels  49.1 us (16%)
  local copies, waits for them, and re-layouts  15 us (5%)
    all_to_all x4, waiting for transfers between devices, swap_lat(): return lax.all_to_all(parts, 'lat', split_axis=0, concat_axis=0, tiled=True)  53.1 us
    ppermute x17, waiting for transfers between devices, swap_bits(): lax.ppermute(part, axis, [(j, j ^ bits) for j in range(lax.axis_size(axis...  51.9 us
    all_to_all x1, blocking collectives, swap_all(): lax.all_to_all(parts, ('lat', 'lon'), split_axis=0, concat_axis=0, tiled=...  51.1 us
    pallas_call x13, Pallas kernels, call(): pl.pallas_call(kernel, grid_spec=pltpu.PrefetchScalarGridSpec(num_scalar_...  49.1 us
    all_to_all x2, waiting for transfers between devices, swap_all(): lax.all_to_all(parts, ('lat', 'lon'), split_axis=0, concat_axis=0, tiled=...  38 us
    ppermute x17, starting transfers between devices, swap_bits(): lax.ppermute(part, axis, [(j, j ^ bits) for j in range(lax.axis_size(axis...  22.3 us
    all_to_all x4, starting transfers between devices, swap_lat(): return lax.all_to_all(parts, 'lat', split_axis=0, concat_axis=0, tiled=True)  16.4 us
    unnamed x42, local copies, waits for them, and re-layouts  13.8 us
  transfers between devices with their start and end apart: 23, of which 12 were waited for; matrix products, arithmetic and copies ran while one was open for 0% of the time, Pallas kernels for 7%

profile of v4, /device:TPU:0, one launch (start us, length us, event | category | flops | bytes accessed | tf_op | source)
XLA Modules:
  0.0 308.3 jit_solution(905521080258189587)
XLA Ops:
  4.7 5.2 %all-to-all-start = ((bf16[8,8,64,128]{3,2,1,0:T(8,128)(2,1)}), bf16[8,8,64,128]{3,2,1,0:T(8,128)(2,1)S(1)}, u32[]{:S(2)}, u32[]{:S(2)}) async-start(bf16[8,8,64,128]{3,2,1,0:T(8,128)(2,1)} %shard_map.109), calls=%async_computation | async-start | bytes 2097152 | tf_op jit(solution)/shard_map/all_to_all | solution.py:539
  17.3 8.0 %all-to-all-done.x_ref = bf16[8,8,64,128]{3,2,1,0:T(8,128)(2,1)S(1)} async-done(((bf16[8,8,64,128]{3,2,1,0:T(8,128)(2,1)}), bf16[8,8,64,128]{3,2,1,0:T(8,128)(2,1)S(1)}, u32[]{:S(2)}, u32[]{:S(2)}) %all-to-all-start) | async-done | bytes 1048608 | tf_op jit(solution)/shard_map/all_to_all | solution.py:539
  27.6 3.6 %all-to-all-start.1 = ((bf16[8,8,64,128]{3,2,1,0:T(8,128)(2,1)}), bf16[8,8,64,128]{3,2,1,0:T(8,128)(2,1)S(1)}, u32[]{:S(2)}, u32[]{:S(2)}) async-start(bf16[8,8,64,128]{3,2,1,0:T(8,128)(2,1)} %shard_map.110), calls=%async_computation.1 | async-start | bytes 2097152 | tf_op jit(solution)/shard_map/all_to_all | solution.py:539
  35.6 10.9 %all-to-all-done.1.x_ref = bf16[8,8,64,128]{3,2,1,0:T(8,128)(2,1)S(1)} async-done(((bf16[8,8,64,128]{3,2,1,0:T(8,128)(2,1)}), bf16[8,8,64,128]{3,2,1,0:T(8,128)(2,1)S(1)}, u32[]{:S(2)}, u32[]{:S(2)}) %all-to-all-start.1) | async-done | bytes 1048608 | tf_op jit(solution)/shard_map/all_to_all | solution.py:539
  49.5 4.8 %collective-permute-done.1 = bf16[64,8,256]{2,1,0:T(8,128)(2,1)S(1)} collective-permute-done((bf16[64,8,256]{2,1,0:T(8,128)(2,1)}, bf16[64,8,256]{2,1,0:T(8,128)(2,1)S(1)}, u32[]{:S(2)}, u32[]{:S(2)}) %collective-permute-start.1) | collective-permute-done | bytes 262176 | tf_op jit(solution)/shard_map/ppermute | solution.py:531
  55.1 4.0 %all-to-all-start.2 = ((bf16[8,16,64,128]{3,2,1,0:T(8,128)(2,1)}), bf16[8,16,64,128]{3,2,1,0:T(8,128)(2,1)S(1)}, u32[]{:S(2)}, u32[]{:S(2)}) async-start(bf16[8,16,64,128]{3,2,1,0:T(8,128)(2,1)} %shard_map.111), calls=%async_computation.2 | async-start | bytes 4194304 | tf_op jit(solution)/shard_map/all_to_all | solution.py:539
  59.1 5.1 %collective-permute-start.3 = (bf16[64,8,256]{2,1,0:T(8,128)(2,1)}, bf16[64,8,256]{2,1,0:T(8,128)(2,1)}, u32[]{:S(2)}, u32[]{:S(2)}) collective-permute-start(bf16[64,8,256]{2,1,0:T(8,128)(2,1)} %copy-done.18), channel_id=1, source_target_pairs={{0,1},{1,0},{2,3},{3,2},{4,5},{5,4},{6,7},{7,6},{8,9},{9,8},{10,11... | collective-permute-start | bytes 786440 | tf_op jit(solution)/shard_map/ppermute | solution.py:531
  66.7 19.1 %all-to-all-done.2.x_ref = bf16[8,16,64,128]{3,2,1,0:T(8,128)(2,1)S(1)} async-done(((bf16[8,16,64,128]{3,2,1,0:T(8,128)(2,1)}), bf16[8,16,64,128]{3,2,1,0:T(8,128)(2,1)S(1)}, u32[]{:S(2)}, u32[]{:S(2)}) %all-to-all-start.2) | async-done | bytes 2097184 | tf_op jit(solution)/shard_map/all_to_all | solution.py:539
  85.8 3.4 %shard_map.114 = bf16[256,16,256]{2,1,0:T(8,128)(2,1)} custom-call(s32[3]{0:T(128)S(1)} %pad_add_fusion.place_ref, bf16[8,16,64,128]{3,2,1,0:T(8,128)(2,1)S(1)} %all-to-all-done.2.x_ref, bf16[512,512]{1,0:T(8,128)(2,1)S(1)} %copy-done.9), custom_call_target="tpu_custom_call" | custom-call | flops 1 | bytes 1048576 | tf_op jit(solution)/shard_map/pallas_call | solution.py:217
  89.2 6.7 %all-to-all-start.3 = ((bf16[32,8,16,256]{3,2,1,0:T(8,128)(2,1)}), bf16[32,8,16,256]{3,2,1,0:T(8,128)(2,1)}, u32[]{:S(2)}, u32[]{:S(2)}) async-start(bf16[32,8,16,256]{3,2,1,0:T(8,128)(2,1)} %bitcast.12), calls=%async_computation.3 | async-start | bytes 4194304 | tf_op jit(solution)/shard_map/all_to_all | solution.py:543
  104.1 16.0 %collective-permute-done.7.refs_2_ = bf16[4,8,16,256]{3,2,1,0:T(8,128)(2,1)S(1)} collective-permute-done((bf16[4,8,16,256]{3,2,1,0:T(8,128)(2,1)S(1)}, bf16[4,8,16,256]{3,2,1,0:T(8,128)(2,1)S(1)}, u32[]{:S(2)}, u32[]{:S(2)}) %collective-permute-start.7) | collective-permute-done | bytes 262176 | tf_op jit(solution)/shard_map/ppermute | solution.py:531
  120.2 7.4 %collective-permute-done.8.refs_3_ = bf16[4,8,16,256]{3,2,1,0:T(8,128)(2,1)S(1)} collective-permute-done((bf16[4,8,16,256]{3,2,1,0:T(8,128)(2,1)S(1)}, bf16[4,8,16,256]{3,2,1,0:T(8,128)(2,1)S(1)}, u32[]{:S(2)}, u32[]{:S(2)}) %collective-permute-start.8) | collective-permute-done | bytes 262176 | tf_op jit(solution)/shard_map/ppermute | solution.py:531
  127.6 11.0 %collective-permute-done.11.refs_6_ = bf16[4,8,16,256]{3,2,1,0:T(8,128)(2,1)S(1)} collective-permute-done((bf16[4,8,16,256]{3,2,1,0:T(8,128)(2,1)S(1)}, bf16[4,8,16,256]{3,2,1,0:T(8,128)(2,1)S(1)}, u32[]{:S(2)}, u32[]{:S(2)}) %collective-permute-start.11) | collective-permute-done | bytes 262176 | tf_op jit(solution)/shard_map/ppermute | solution.py:531
  138.6 7.2 %collective-permute-done.12.refs_7_ = bf16[4,8,16,256]{3,2,1,0:T(8,128)(2,1)S(1)} collective-permute-done((bf16[4,8,16,256]{3,2,1,0:T(8,128)(2,1)S(1)}, bf16[4,8,16,256]{3,2,1,0:T(8,128)(2,1)S(1)}, u32[]{:S(2)}, u32[]{:S(2)}) %collective-permute-start.12) | collective-permute-done | bytes 262176 | tf_op jit(solution)/shard_map/ppermute | solution.py:531
  145.8 16.9 %shard_map.116 = (bf16[32,8,16,256]{3,2,1,0:T(8,128)(2,1)S(1)}, bf16[32,8,16,256]{3,2,1,0:T(8,128)(2,1)}) custom-call(s32[3]{0:T(128)S(1)} %pad_add_fusion.place_ref, bf16[4,8,16,256]{3,2,1,0:T(8,128)(2,1)S(1)} %get-tuple-element.96.refs_0_, bf16[4,8,16,256]{3,2,1,0:T(8,128)(2,1)S(1)} %collective-permute-done.6.refs_1_, ...), custom_call_target="tpu_custom_call" | custom-call | flops 1 | bytes 1048576 | tf_op jit(solution)/shard_map/pallas_call | solution.py:217
  162.7 51.1 %all_to_all.35 = bf16[32,8,16,256]{3,2,1,0:T(8,128)(2,1)} all-to-all(bf16[32,8,16,256]{3,2,1,0:T(8,128)(2,1)} %get-tuple-element.106), channel_id=1, replica_groups=mesh['lat'=8,'lon'=4] {'lat','lon'}, dimensions={0} | all-to-all | bytes 4194304 | tf_op jit(solution)/shard_map/all_to_all | solution.py:543
  213.8 4.4 %all-to-all-start.4 = ((bf16[32,8,16,256]{3,2,1,0:T(8,128)(2,1)}), bf16[32,8,16,256]{3,2,1,0:T(8,128)(2,1)S(1)}, u32[]{:S(2)}, u32[]{:S(2)}) async-start(bf16[32,8,16,256]{3,2,1,0:T(8,128)(2,1)} %copy-done.6), calls=%async_computation.4 | async-start | bytes 4194304 | tf_op jit(solution)/shard_map/all_to_all | solution.py:543
  220.9 3.2 %shard_map.117 = (bf16[2,16,64,128]{3,2,1,0:T(8,128)(2,1)S(1)}, bf16[2,16,64,128]{3,2,1,0:T(8,128)(2,1)}, bf16[2,16,64,128]{3,2,1,0:T(8,128)(2,1)}, bf16[2,16,64,128]{3,2,1,0:T(8,128)(2,1)}) custom-call(s32[3]{0:T(128)S(1)} %pad_add_fusion.place_ref, bf16[256,16,256]{2,1,0:T(8,128)(2,1)S(1)} %bitcast.39, bf16[512,512]{1,0:T(8,128)(2,1)S(1)} %dynamic-slice_bitcast_fusion.table_ref), custom_call_target="tpu_custom_call" | custom-call | flops 1 | bytes 1048576 | tf_op jit(solution)/shard_map/pallas_call | solution.py:217
  227.6 38.0 %all-to-all-done.4 = bf16[32,8,16,256]{3,2,1,0:T(8,128)(2,1)S(1)} async-done(((bf16[32,8,16,256]{3,2,1,0:T(8,128)(2,1)}), bf16[32,8,16,256]{3,2,1,0:T(8,128)(2,1)S(1)}, u32[]{:S(2)}, u32[]{:S(2)}) %all-to-all-start.4) | async-done | bytes 2097184 | tf_op jit(solution)/shard_map/all_to_all | solution.py:543
  265.7 3.2 %collective-permute-done.15.refs_3_ = bf16[2,16,64,128]{3,2,1,0:T(8,128)(2,1)} collective-permute-done((bf16[2,16,64,128]{3,2,1,0:T(8,128)(2,1)}, bf16[2,16,64,128]{3,2,1,0:T(8,128)(2,1)}, u32[]{:S(2)}, u32[]{:S(2)}) %collective-permute-start.15) | collective-permute-done | bytes 524320 | tf_op jit(solution)/shard_map/ppermute | solution.py:531
  272.6 3.6 %all-to-all-start.6 = ((bf16[8,16,64,128]{3,2,1,0:T(8,128)(2,1)}), bf16[8,16,64,128]{3,2,1,0:T(8,128)(2,1)S(1)}, u32[]{:S(2)}, u32[]{:S(2)}) async-start(bf16[8,16,64,128]{3,2,1,0:T(8,128)(2,1)} %copy-done.4), calls=%async_computation.6 | async-start | bytes 4194304 | tf_op jit(solution)/shard_map/all_to_all | solution.py:539
  278.4 4.7 %shard_map.119 = (bf16[64,4,2,32,128]{4,3,2,1,0:T(8,128)(2,1)}, bf16[64,4,16,128]{3,2,1,0:T(8,128)(2,1)S(1)}) custom-call(s32[3]{0:T(128)S(1)} %pad_add_fusion.place_ref, bf16[64,4,2,32,128]{4,3,2,1,0:T(8,128)(2,1)S(1)} %bitcast.35, bf16[2,16,64,128]{3,2,1,0:T(8,128)(2,1)S(1)} %get-tuple-element.117.refs_0_, ...), custom_call_target="tpu_custom_call" | custom-call | flops 1 | bytes 1048576 | tf_op jit(solution)/shard_map/pallas_call | solution.py:217
  287.6 15.2 %all-to-all-done.6.part_ref = bf16[8,16,64,128]{3,2,1,0:T(8,128)(2,1)S(1)} async-done(((bf16[8,16,64,128]{3,2,1,0:T(8,128)(2,1)}), bf16[8,16,64,128]{3,2,1,0:T(8,128)(2,1)S(1)}, u32[]{:S(2)}, u32[]{:S(2)}) %all-to-all-start.6) | async-done | bytes 2097184 | tf_op jit(solution)/shard_map/all_to_all | solution.py:539
  305.0 3.3 %shard_map.121 = bf16[64,4,2,32,128]{4,3,2,1,0:T(8,128)(2,1)} custom-call(s32[3]{0:T(128)S(1)} %pad_add_fusion.place_ref, bf16[64,4,2,32,128]{4,3,2,1,0:T(8,128)(2,1)S(1)} %bitcast.37, bf16[8,16,64,128]{3,2,1,0:T(8,128)(2,1)S(1)} %all-to-all-done.6.part_ref, bf16[64,4,2,32,128]{4,3,2,1,0:T(8,128)(2,1)} %shard_map.120.refs_0_), custom_call_target="tpu_custom_call", output_to_operand_aliasing={{}: (3, {})} | custom-call | flops 1 | bytes 1048576 | tf_op jit(solution)/shard_map/pallas_call | solution.py:217
  (85 shorter events, 52.2 us)
Async XLA Ops:
  4.7 20.6 %all-to-all-start = ((bf16[8,8,64,128]{3,2,1,0:T(8,128)(2,1)}), bf16[8,8,64,128]{3,2,1,0:T(8,128)(2,1)S(1)}, u32[]{:S(2)}, u32[]{:S(2)}) async-start(bf16[8,8,64,128]{3,2,1,0:T(8,128)(2,1)} %shard_map.109), calls=%async_computation | async-start | bytes 2097152 | tf_op jit(solution)/shard_map/all_to_all | solution.py:539
  27.6 18.9 %all-to-all-start.1 = ((bf16[8,8,64,128]{3,2,1,0:T(8,128)(2,1)}), bf16[8,8,64,128]{3,2,1,0:T(8,128)(2,1)S(1)}, u32[]{:S(2)}, u32[]{:S(2)}) async-start(bf16[8,8,64,128]{3,2,1,0:T(8,128)(2,1)} %shard_map.110), calls=%async_computation.1 | async-start | bytes 2097152 | tf_op jit(solution)/shard_map/all_to_all | solution.py:539
  31.2 18.4 %collective-permute-start = (bf16[64,8,256]{2,1,0:T(8,128)(2,1)}, bf16[64,8,256]{2,1,0:T(8,128)(2,1)S(1)}, u32[]{:S(2)}, u32[]{:S(2)}) collective-permute-start(bf16[64,8,256]{2,1,0:T(8,128)(2,1)} %get-tuple-element.80), channel_id=1, source_target_pairs={{0,1},{1,0},{2,3},{3,2},{4,5},{5,4},{6,7},{7,6},{8,9},{9,8},{10,11... | collective-permute-start | bytes 786440 | tf_op jit(solution)/shard_map/ppermute | solution.py:531
  32.8 21.6 %collective-permute-start.1 = (bf16[64,8,256]{2,1,0:T(8,128)(2,1)}, bf16[64,8,256]{2,1,0:T(8,128)(2,1)S(1)}, u32[]{:S(2)}, u32[]{:S(2)}) collective-permute-start(bf16[64,8,256]{2,1,0:T(8,128)(2,1)} %get-tuple-element.81), channel_id=1, source_target_pairs={{0,2},{1,3},{2,0},{3,1},{4,6},{5,7},{6,4},{7,5},{8,10},{9,11},{10,... | collective-permute-start | bytes 786440 | tf_op jit(solution)/shard_map/ppermute | solution.py:531
  35.4 19.0 %collective-permute-start.2 = (bf16[64,8,256]{2,1,0:T(8,128)(2,1)}, bf16[64,8,256]{2,1,0:T(8,128)(2,1)S(1)}, u32[]{:S(2)}, u32[]{:S(2)}) collective-permute-start(bf16[64,8,256]{2,1,0:T(8,128)(2,1)} %get-tuple-element.82), channel_id=1, source_target_pairs={{0,3},{1,2},{2,1},{3,0},{4,7},{5,6},{6,5},{7,4},{8,11},{9,10},{10,... | collective-permute-start | bytes 786440 | tf_op jit(solution)/shard_map/ppermute | solution.py:531
  55.1 30.7 %all-to-all-start.2 = ((bf16[8,16,64,128]{3,2,1,0:T(8,128)(2,1)}), bf16[8,16,64,128]{3,2,1,0:T(8,128)(2,1)S(1)}, u32[]{:S(2)}, u32[]{:S(2)}) async-start(bf16[8,16,64,128]{3,2,1,0:T(8,128)(2,1)} %shard_map.111), calls=%async_computation.2 | async-start | bytes 4194304 | tf_op jit(solution)/shard_map/all_to_all | solution.py:539
  59.1 30.0 %collective-permute-start.3 = (bf16[64,8,256]{2,1,0:T(8,128)(2,1)}, bf16[64,8,256]{2,1,0:T(8,128)(2,1)}, u32[]{:S(2)}, u32[]{:S(2)}) collective-permute-start(bf16[64,8,256]{2,1,0:T(8,128)(2,1)} %copy-done.18), channel_id=1, source_target_pairs={{0,1},{1,0},{2,3},{3,2},{4,5},{5,4},{6,7},{7,6},{8,9},{9,8},{10,11... | collective-permute-start | bytes 786440 | tf_op jit(solution)/shard_map/ppermute | solution.py:531
  64.2 24.9 %collective-permute-start.4 = (bf16[64,8,256]{2,1,0:T(8,128)(2,1)}, bf16[64,8,256]{2,1,0:T(8,128)(2,1)}, u32[]{:S(2)}, u32[]{:S(2)}) collective-permute-start(bf16[64,8,256]{2,1,0:T(8,128)(2,1)} %copy-done.17), channel_id=1, source_target_pairs={{0,2},{1,3},{2,0},{3,1},{4,6},{5,7},{6,4},{7,5},{8,10},{9,11},{10,... | collective-permute-start | bytes 786440 | tf_op jit(solution)/shard_map/ppermute | solution.py:531
  65.3 23.8 %collective-permute-start.5 = (bf16[64,8,256]{2,1,0:T(8,128)(2,1)}, bf16[64,8,256]{2,1,0:T(8,128)(2,1)}, u32[]{:S(2)}, u32[]{:S(2)}) collective-permute-start(bf16[64,8,256]{2,1,0:T(8,128)(2,1)} %copy-done.16), channel_id=1, source_target_pairs={{0,3},{1,2},{2,1},{3,0},{4,7},{5,6},{6,5},{7,4},{8,11},{9,10},{10,... | collective-permute-start | bytes 786440 | tf_op jit(solution)/shard_map/ppermute | solution.py:531
  89.2 56.6 %all-to-all-start.3 = ((bf16[32,8,16,256]{3,2,1,0:T(8,128)(2,1)}), bf16[32,8,16,256]{3,2,1,0:T(8,128)(2,1)}, u32[]{:S(2)}, u32[]{:S(2)}) async-start(bf16[32,8,16,256]{3,2,1,0:T(8,128)(2,1)} %bitcast.12), calls=%async_computation.3 | async-start | bytes 4194304 | tf_op jit(solution)/shard_map/all_to_all | solution.py:543
  97.7 3.8 %collective-permute-start.6 = (bf16[4,8,16,256]{3,2,1,0:T(8,128)(2,1)S(1)}, bf16[4,8,16,256]{3,2,1,0:T(8,128)(2,1)S(1)}, u32[]{:S(2)}, u32[]{:S(2)}) collective-permute-start(bf16[4,8,16,256]{3,2,1,0:T(8,128)(2,1)S(1)} %get-tuple-element.97), channel_id=1, source_target_pairs={{0,4},{4,0},{8,12},{12,8},{16,20},{20,16},{24,28},{28,24},{1,5},{5... | collective-permute-start | bytes 786440 | tf_op jit(solution)/shard_map/ppermute | solution.py:531
  98.0 22.2 %collective-permute-start.7 = (bf16[4,8,16,256]{3,2,1,0:T(8,128)(2,1)S(1)}, bf16[4,8,16,256]{3,2,1,0:T(8,128)(2,1)S(1)}, u32[]{:S(2)}, u32[]{:S(2)}) collective-permute-start(bf16[4,8,16,256]{3,2,1,0:T(8,128)(2,1)S(1)} %get-tuple-element.98), channel_id=1, source_target_pairs={{0,8},{4,12},{8,0},{12,4},{16,24},{20,28},{24,16},{28,20},{1,9},{5... | collective-permute-start | bytes 786440 | tf_op jit(solution)/shard_map/ppermute | solution.py:531
  99.7 27.9 %collective-permute-start.8 = (bf16[4,8,16,256]{3,2,1,0:T(8,128)(2,1)S(1)}, bf16[4,8,16,256]{3,2,1,0:T(8,128)(2,1)S(1)}, u32[]{:S(2)}, u32[]{:S(2)}) collective-permute-start(bf16[4,8,16,256]{3,2,1,0:T(8,128)(2,1)S(1)} %get-tuple-element.99), channel_id=1, source_target_pairs={{0,12},{4,8},{8,4},{12,0},{16,28},{20,24},{24,20},{28,16},{1,13},{... | collective-permute-start | bytes 786440 | tf_op jit(solution)/shard_map/ppermute | solution.py:531
  99.8 27.8 %collective-permute-start.9 = (bf16[4,8,16,256]{3,2,1,0:T(8,128)(2,1)S(1)}, bf16[4,8,16,256]{3,2,1,0:T(8,128)(2,1)S(1)}, u32[]{:S(2)}, u32[]{:S(2)}) collective-permute-start(bf16[4,8,16,256]{3,2,1,0:T(8,128)(2,1)S(1)} %get-tuple-element.100), channel_id=1, source_target_pairs={{0,16},{4,20},{8,24},{12,28},{16,0},{20,4},{24,8},{28,12},{1,17},{... | collective-permute-start | bytes 786440 | tf_op jit(solution)/shard_map/ppermute | solution.py:531
  101.4 26.2 %collective-permute-start.10 = (bf16[4,8,16,256]{3,2,1,0:T(8,128)(2,1)S(1)}, bf16[4,8,16,256]{3,2,1,0:T(8,128)(2,1)S(1)}, u32[]{:S(2)}, u32[]{:S(2)}) collective-permute-start(bf16[4,8,16,256]{3,2,1,0:T(8,128)(2,1)S(1)} %get-tuple-element.101), channel_id=1, source_target_pairs={{0,20},{4,16},{8,28},{12,24},{16,4},{20,0},{24,12},{28,8},{1,21},{... | collective-permute-start | bytes 786440 | tf_op jit(solution)/shard_map/ppermute | solution.py:531
  101.6 37.1 %collective-permute-start.11 = (bf16[4,8,16,256]{3,2,1,0:T(8,128)(2,1)S(1)}, bf16[4,8,16,256]{3,2,1,0:T(8,128)(2,1)S(1)}, u32[]{:S(2)}, u32[]{:S(2)}) collective-permute-start(bf16[4,8,16,256]{3,2,1,0:T(8,128)(2,1)S(1)} %get-tuple-element.102), channel_id=1, source_target_pairs={{0,24},{4,28},{8,16},{12,20},{16,8},{20,12},{24,0},{28,4},{1,25},{... | collective-permute-start | bytes 786440 | tf_op jit(solution)/shard_map/ppermute | solution.py:531
  120.2 25.6 %collective-permute-start.12 = (bf16[4,8,16,256]{3,2,1,0:T(8,128)(2,1)S(1)}, bf16[4,8,16,256]{3,2,1,0:T(8,128)(2,1)S(1)}, u32[]{:S(2)}, u32[]{:S(2)}) collective-permute-start(bf16[4,8,16,256]{3,2,1,0:T(8,128)(2,1)S(1)} %get-tuple-element.103), channel_id=1, source_target_pairs={{0,28},{4,24},{8,20},{12,16},{16,12},{20,8},{24,4},{28,0},{1,29},{... | collective-permute-start | bytes 786440 | tf_op jit(solution)/shard_map/ppermute | solution.py:531
  162.7 51.1 %copy-start.6 = (bf16[32,8,16,256]{3,2,1,0:T(8,128)(2,1)}, bf16[32,8,16,256]{3,2,1,0:T(8,128)(2,1)S(1)}, u32[]{:S(2)}) copy-start(bf16[32,8,16,256]{3,2,1,0:T(8,128)(2,1)S(1)} %get-tuple-element.105) | copy-start | bytes 6291460
  213.8 51.9 %all-to-all-start.4 = ((bf16[32,8,16,256]{3,2,1,0:T(8,128)(2,1)}), bf16[32,8,16,256]{3,2,1,0:T(8,128)(2,1)S(1)}, u32[]{:S(2)}, u32[]{:S(2)}) async-start(bf16[32,8,16,256]{3,2,1,0:T(8,128)(2,1)} %copy-done.6), calls=%async_computation.4 | async-start | bytes 4194304 | tf_op jit(solution)/shard_map/all_to_all | solution.py:543
  224.1 41.5 %collective-permute-start.13 = (bf16[2,16,64,128]{3,2,1,0:T(8,128)(2,1)}, bf16[2,16,64,128]{3,2,1,0:T(8,128)(2,1)}, u32[]{:S(2)}, u32[]{:S(2)}) collective-permute-start(bf16[2,16,64,128]{3,2,1,0:T(8,128)(2,1)} %get-tuple-element.108), channel_id=1, source_target_pairs={{0,8},{4,12},{8,0},{12,4},{16,24},{20,28},{24,16},{28,20},{1,9},{5... | collective-permute-start | bytes 1572872 | tf_op jit(solution)/shard_map/ppermute | solution.py:531
  225.9 39.8 %collective-permute-start.14 = (bf16[2,16,64,128]{3,2,1,0:T(8,128)(2,1)}, bf16[2,16,64,128]{3,2,1,0:T(8,128)(2,1)}, u32[]{:S(2)}, u32[]{:S(2)}) collective-permute-start(bf16[2,16,64,128]{3,2,1,0:T(8,128)(2,1)} %get-tuple-element.109), channel_id=1, source_target_pairs={{0,16},{4,20},{8,24},{12,28},{16,0},{20,4},{24,8},{28,12},{1,17},{... | collective-permute-start | bytes 1572872 | tf_op jit(solution)/shard_map/ppermute | solution.py:531
  227.4 41.5 %collective-permute-start.15 = (bf16[2,16,64,128]{3,2,1,0:T(8,128)(2,1)}, bf16[2,16,64,128]{3,2,1,0:T(8,128)(2,1)}, u32[]{:S(2)}, u32[]{:S(2)}) collective-permute-start(bf16[2,16,64,128]{3,2,1,0:T(8,128)(2,1)} %get-tuple-element.110), channel_id=1, source_target_pairs={{0,24},{4,28},{8,16},{12,20},{16,8},{20,12},{24,0},{28,4},{1,25},{... | collective-permute-start | bytes 1572872 | tf_op jit(solution)/shard_map/ppermute | solution.py:531
  272.6 30.2 %all-to-all-start.6 = ((bf16[8,16,64,128]{3,2,1,0:T(8,128)(2,1)}), bf16[8,16,64,128]{3,2,1,0:T(8,128)(2,1)S(1)}, u32[]{:S(2)}, u32[]{:S(2)}) async-start(bf16[8,16,64,128]{3,2,1,0:T(8,128)(2,1)} %copy-done.4), calls=%async_computation.6 | async-start | bytes 4194304 | tf_op jit(solution)/shard_map/all_to_all | solution.py:539
  283.1 2.7 collective-permute-start.16
  (20 other events, 245.1 us)

commit v5 on v4

--- a/solution.py
+++ b/solution.py
@@ -196,13 +196,15 @@
 
 
 def lon_tables(cell_order, total_lon, scale):
-    keep = total_lon // 2
-    angle = (np.outer(np.arange(keep), cell_order) % total_lon) * (2.0 * np.pi / total_lon)
-    forward = np.concatenate([np.cos(angle), -np.sin(angle)], axis=0)
-    weight = np.where(np.arange(keep) == 0, 1.0, 2.0)
-    weight = np.concatenate([weight, weight])
-    backward = (forward * weight[:, None]).T
-    return jnp.asarray(forward * scale, jnp.bfloat16), jnp.asarray(backward, jnp.bfloat16)
+    forward, backward = [], []
+    for odd in range(2):
+        waves = np.arange(odd, total_lon // 2, 2)
+        angle = (np.outer(waves, cell_order) % total_lon) * (2.0 * np.pi / total_lon)
+        table = np.concatenate([np.cos(angle), -np.sin(angle)], axis=0)
+        weight = np.where(waves == 0, 1.0, 2.0)
+        forward.append(table * scale)
+        backward.append((table * np.concatenate([weight, weight])[:, None]).T)
+    return jnp.asarray(np.stack(forward), jnp.bfloat16), jnp.asarray(np.stack(backward), jnp.bfloat16)
 
 
 def dot32(left, right):
@@ -270,7 +272,16 @@
     if partial is not None:
         args, specs, alias = args + [partial], specs + [pl.BlockSpec(memory_space=pl.ANY)], {3: 0}
     shape = jax.ShapeDtypeStruct(features.shape, jnp.bfloat16)
-    return call(kernel, place, args, specs, block, shape, (steps,), alias=alias)
+    return call(
+        kernel,
+        place,
+        args,
+        specs,
+        block,
+        shape,
+        (steps,),
+        alias=alias,
+    )
 
 
 def own_block(tile, chips, cells, start, flip):
@@ -452,14 +463,17 @@
     )
 
 
+def whole(array):
+    return pl.BlockSpec(array.shape, lambda i, p: (0,) * array.ndim)
+
+
 def spectral_step(parts, chunk, place, fwd, inv, w1, b1, w2, b2, together=2):
     targets = len(parts)
     groups, slots, cells, width = parts[0].shape
     channels = width // 2
     sources, _, more, _ = chunk.shape
-    first = targets * groups * cells
-    total = first + sources * more
-    keep = total // 2
+    first = targets * groups * cells // 2
+    keep = fwd.shape[1] // 2
 
     def kernel(place_ref, *refs):
         ins, g_ref, refs = refs[:targets], refs[targets], refs[targets + 1 :]
@@ -470,9 +484,13 @@
         def waves(u):
             for d, e in pairs:
                 stage[u, place_ref[0] ^ d, place_ref[2] ^ e] = ins[d][e, u]
-            near = stage[u].reshape(first, width)
-            sums = jnp.concatenate([near, g_ref[:, u].reshape(total - first, width)], axis=0)
-            return dot32(fwd_ref[...], sums)
+            near = stage[u]
+            far = g_ref[:, u].reshape(targets, groups, more, width)
+            halves = [
+                jnp.concatenate([v[:, z : z + groups // 2].reshape(-1, width) for v in (near, far)], axis=0)
+                for z in (0, groups // 2)
+            ]
+            return [dot32(fwd_ref[0], halves[0] + halves[1]), dot32(fwd_ref[1], halves[0] - halves[1])]
 
         def mix(u, both):
             cc, sc = both[:keep, :channels], both[:keep, channels:]
@@ -493,12 +511,14 @@
             return jnp.concatenate(coefs, axis=0)
 
         def back(u, coefs):
-            lines = dot32(inv_ref[...], coefs).astype(jnp.bfloat16)
-            out_ref[:, u] = lines[first:].reshape(sources, more, width)
-            near_ref[:, u] = lines[:first].reshape(sources, cells, width)
+            even, odd = dot32(inv_ref[0], coefs[0]), dot32(inv_ref[1], coefs[1])
+            halves = [(even + odd).astype(jnp.bfloat16), (even - odd).astype(jnp.bfloat16)]
+            for ref, rows in ((near_ref, slice(0, first)), (out_ref, slice(first, None))):
+                parts = [v[rows].reshape(targets, groups // 2, -1, width) for v in halves]
+                ref[:, u] = jnp.concatenate(parts, axis=1).reshape(sources, -1, width)
 
         both = [waves(u) for u in range(together)]
-        coefs = [mix(u, both[u]) for u in range(together)]
+        coefs = [[mix(u, v) for v in both[u]] for u in range(together)]
         for u in range(together):
             back(u, coefs[u])
 
@@ -509,12 +529,12 @@
         kernel,
         place,
         [*parts, chunk, *tables],
-        [near] * targets + [block] + [pl.BlockSpec(v.shape, lambda i, p: (0, 0)) for v in tables],
+        [near] * targets + [block] + [whole(v) for v in tables],
         [pl.BlockSpec((sources, together, cells, width), lambda i, p: (0, i, 0, 0)), block],
         [jax.ShapeDtypeStruct((sources, slots, n, width), jnp.bfloat16) for n in (cells, more)],
         (slots // together,),
         [pltpu.VMEM((together, targets, groups, cells, width), jnp.bfloat16)],
-        mib=48,
+        mib=62,
     )
 def complex_weights(weights):
     real, imag = weights[0, 0], weights[1, 0]
@@ -554,6 +574,7 @@
     half = block_cells // 2
     sizes, starts = [half // 2, half // 2, half], [0, half // 2, half]
     cell_index = np.arange(total_lon).reshape(lon_count, lat_count, 2, half).transpose(2, 1, 0, 3)
+    cell_index = cell_index[:, :, : lon_count // 2]
     lon_fwd, lon_inv = lon_tables(cell_index.reshape(-1), total_lon, norm)
     slot_l = np.arange(total_lat // 2)
     lat_fwd, lat_inv = lat_tables(total_lat, norm, slot_l)
@@ -613,6 +634,7 @@
         and lat_count > 1
         and lon_cells % (32 * lat_count) == 0
         and lon_count & (lon_count - 1) == 0
+        and lon_count > 1
         and rows % 64 == 0
         and channels == 128
         and w_first.shape[1] == 1

time: 309 us -> 305 us (0.987)
  Pallas kernels: 49.1 us -> 44.1 us
    pallas_call x13, Pallas kernels: 49.1 us -> 44.1 us  [call(): pl.pallas_call(kernel, grid_spec=pltpu.PrefetchScalarGridSpec(num_scalar_...]
    unnamed x42 -> x56, local copies, waits for them, and re-layouts: 13.8 us -> 16.6 us
  transfers between devices with their start and end apart: 23 -> 23, of which waited for: 12 -> 12; matrix products, arithmetic and copies ran while one was open for 0% -> 1% of each run, Pallas kernels for 7% -> 7%
where the time goes in v5:
time: 305 us; the launch traced here: 304 us
  waiting for transfers between devices  140 us (46%)
  blocking collectives  51 us (17%)
  starting transfers between devices  49.7 us (16%)
  Pallas kernels  44.1 us (14%)
  local copies, waits for them, and re-layouts  17.8 us (6%)
    all_to_all x4, waiting for transfers between devices, swap_lat(): return lax.all_to_all(parts, 'lat', split_axis=0, concat_axis=0, tiled=True)  53.1 us
    all_to_all x1, blocking collectives, swap_all(): lax.all_to_all(parts, ('lat', 'lon'), split_axis=0, concat_axis=0, tiled=...  51 us
    ppermute x17, waiting for transfers between devices, swap_bits(): lax.ppermute(part, axis, [(j, j ^ bits) for j in range(lax.axis_size(axis...  48.9 us
    pallas_call x13, Pallas kernels, call(): pl.pallas_call(kernel, grid_spec=pltpu.PrefetchScalarGridSpec(num_scalar_...  44.1 us
    all_to_all x2, waiting for transfers between devices, swap_all(): lax.all_to_all(parts, ('lat', 'lon'), split_axis=0, concat_axis=0, tiled=...  38 us
    ppermute x17, starting transfers between devices, swap_bits(): lax.ppermute(part, axis, [(j, j ^ bits) for j in range(lax.axis_size(axis...  22.2 us
    unnamed x56, local copies, waits for them, and re-layouts  16.6 us
    all_to_all x4, starting transfers between devices, swap_lat(): return lax.all_to_all(parts, 'lat', split_axis=0, concat_axis=0, tiled=True)  16.4 us
  transfers between devices with their start and end apart: 23, of which 12 were waited for; matrix products, arithmetic and copies ran while one was open for 1% of the time, Pallas kernels for 7%

profile of v5, /device:TPU:0, one launch (start us, length us, event | category | flops | bytes accessed | tf_op | source)
XLA Modules:
  0.0 303.7 jit_solution(4949282760344519785)
XLA Ops:
  4.8 5.2 %all-to-all-start = ((bf16[8,8,64,128]{3,2,1,0:T(8,128)(2,1)}), bf16[8,8,64,128]{3,2,1,0:T(8,128)(2,1)S(1)}, u32[]{:S(2)}, u32[]{:S(2)}) async-start(bf16[8,8,64,128]{3,2,1,0:T(8,128)(2,1)} %shard_map.109), calls=%async_computation | async-start | bytes 2097152 | tf_op jit(solution)/shard_map/all_to_all | solution.py:559
  17.4 8.0 %all-to-all-done.x_ref = bf16[8,8,64,128]{3,2,1,0:T(8,128)(2,1)S(1)} async-done(((bf16[8,8,64,128]{3,2,1,0:T(8,128)(2,1)}), bf16[8,8,64,128]{3,2,1,0:T(8,128)(2,1)S(1)}, u32[]{:S(2)}, u32[]{:S(2)}) %all-to-all-start) | async-done | bytes 1048608 | tf_op jit(solution)/shard_map/all_to_all | solution.py:559
  26.9 3.6 %all-to-all-start.1 = ((bf16[8,8,64,128]{3,2,1,0:T(8,128)(2,1)}), bf16[8,8,64,128]{3,2,1,0:T(8,128)(2,1)S(1)}, u32[]{:S(2)}, u32[]{:S(2)}) async-start(bf16[8,8,64,128]{3,2,1,0:T(8,128)(2,1)} %shard_map.110), calls=%async_computation.1 | async-start | bytes 2097152 | tf_op jit(solution)/shard_map/all_to_all | solution.py:559
  35.0 10.9 %all-to-all-done.1.x_ref = bf16[8,8,64,128]{3,2,1,0:T(8,128)(2,1)S(1)} async-done(((bf16[8,8,64,128]{3,2,1,0:T(8,128)(2,1)}), bf16[8,8,64,128]{3,2,1,0:T(8,128)(2,1)S(1)}, u32[]{:S(2)}, u32[]{:S(2)}) %all-to-all-start.1) | async-done | bytes 1048608 | tf_op jit(solution)/shard_map/all_to_all | solution.py:559
  50.3 3.2 %collective-permute-done.1 = bf16[64,8,256]{2,1,0:T(8,128)(2,1)S(1)} collective-permute-done((bf16[64,8,256]{2,1,0:T(8,128)(2,1)S(1)}, bf16[64,8,256]{2,1,0:T(8,128)(2,1)S(1)}, u32[]{:S(2)}, u32[]{:S(2)}) %collective-permute-start.1) | collective-permute-done | bytes 262176 | tf_op jit(solution)/shard_map/ppermute | solution.py:551
  54.2 4.0 %all-to-all-start.2 = ((bf16[8,16,64,128]{3,2,1,0:T(8,128)(2,1)}), bf16[8,16,64,128]{3,2,1,0:T(8,128)(2,1)S(1)}, u32[]{:S(2)}, u32[]{:S(2)}) async-start(bf16[8,16,64,128]{3,2,1,0:T(8,128)(2,1)} %shard_map.111), calls=%async_computation.2 | async-start | bytes 4194304 | tf_op jit(solution)/shard_map/all_to_all | solution.py:559
  58.2 5.1 %collective-permute-start.3 = (bf16[64,8,256]{2,1,0:T(8,128)(2,1)}, bf16[64,8,256]{2,1,0:T(8,128)(2,1)}, u32[]{:S(2)}, u32[]{:S(2)}) collective-permute-start(bf16[64,8,256]{2,1,0:T(8,128)(2,1)} %copy-done.18), channel_id=1, source_target_pairs={{0,1},{1,0},{2,3},{3,2},{4,5},{5,4},{6,7},{7,6},{8,9},{9,8},{10,11... | collective-permute-start | bytes 786440 | tf_op jit(solution)/shard_map/ppermute | solution.py:551
  65.8 19.1 %all-to-all-done.2.x_ref = bf16[8,16,64,128]{3,2,1,0:T(8,128)(2,1)S(1)} async-done(((bf16[8,16,64,128]{3,2,1,0:T(8,128)(2,1)}), bf16[8,16,64,128]{3,2,1,0:T(8,128)(2,1)S(1)}, u32[]{:S(2)}, u32[]{:S(2)}) %all-to-all-start.2) | async-done | bytes 2097184 | tf_op jit(solution)/shard_map/all_to_all | solution.py:559
  84.9 3.4 %shard_map.114 = bf16[256,16,256]{2,1,0:T(8,128)(2,1)} custom-call(s32[3]{0:T(128)S(1)} %pad_add_fusion.place_ref, bf16[8,16,64,128]{3,2,1,0:T(8,128)(2,1)S(1)} %all-to-all-done.2.x_ref, bf16[512,512]{1,0:T(8,128)(2,1)S(1)} %copy-done.8), custom_call_target="tpu_custom_call" | custom-call | flops 1 | bytes 1048576 | tf_op jit(solution)/shard_map/pallas_call | solution.py:219
  88.3 6.7 %all-to-all-start.3 = ((bf16[32,8,16,256]{3,2,1,0:T(8,128)(2,1)}), bf16[32,8,16,256]{3,2,1,0:T(8,128)(2,1)}, u32[]{:S(2)}, u32[]{:S(2)}) async-start(bf16[32,8,16,256]{3,2,1,0:T(8,128)(2,1)} %bitcast.12), calls=%async_computation.3 | async-start | bytes 4194304 | tf_op jit(solution)/shard_map/all_to_all | solution.py:563
  103.9 15.4 %collective-permute-done.7.refs_2_ = bf16[4,8,16,256]{3,2,1,0:T(8,128)(2,1)S(1)} collective-permute-done((bf16[4,8,16,256]{3,2,1,0:T(8,128)(2,1)S(1)}, bf16[4,8,16,256]{3,2,1,0:T(8,128)(2,1)S(1)}, u32[]{:S(2)}, u32[]{:S(2)}) %collective-permute-start.7) | collective-permute-done | bytes 262176 | tf_op jit(solution)/shard_map/ppermute | solution.py:551
  120.2 6.6 %collective-permute-done.8.refs_3_ = bf16[4,8,16,256]{3,2,1,0:T(8,128)(2,1)S(1)} collective-permute-done((bf16[4,8,16,256]{3,2,1,0:T(8,128)(2,1)S(1)}, bf16[4,8,16,256]{3,2,1,0:T(8,128)(2,1)S(1)}, u32[]{:S(2)}, u32[]{:S(2)}) %collective-permute-start.8) | collective-permute-done | bytes 262176 | tf_op jit(solution)/shard_map/ppermute | solution.py:551
  126.8 11.0 %collective-permute-done.11.refs_6_ = bf16[4,8,16,256]{3,2,1,0:T(8,128)(2,1)S(1)} collective-permute-done((bf16[4,8,16,256]{3,2,1,0:T(8,128)(2,1)S(1)}, bf16[4,8,16,256]{3,2,1,0:T(8,128)(2,1)S(1)}, u32[]{:S(2)}, u32[]{:S(2)}) %collective-permute-start.11) | collective-permute-done | bytes 262176 | tf_op jit(solution)/shard_map/ppermute | solution.py:551
  137.8 7.2 %collective-permute-done.12.refs_7_ = bf16[4,8,16,256]{3,2,1,0:T(8,128)(2,1)S(1)} collective-permute-done((bf16[4,8,16,256]{3,2,1,0:T(8,128)(2,1)S(1)}, bf16[4,8,16,256]{3,2,1,0:T(8,128)(2,1)S(1)}, u32[]{:S(2)}, u32[]{:S(2)}) %collective-permute-start.12) | collective-permute-done | bytes 262176 | tf_op jit(solution)/shard_map/ppermute | solution.py:551
  145.7 12.5 %shard_map.116 = (bf16[32,8,16,256]{3,2,1,0:T(8,128)(2,1)}, bf16[32,8,16,256]{3,2,1,0:T(8,128)(2,1)}) custom-call(s32[3]{0:T(128)} %copy-done.14, bf16[4,8,16,256]{3,2,1,0:T(8,128)(2,1)} %copy-done.9, bf16[4,8,16,256]{3,2,1,0:T(8,128)(2,1)} %copy-done.19, bf16[4,8,16,256]{3,2,1,0:T(8,128)(2,1)} %copy-done.20, bf16[4,8,16,256]{3,2,1,0:T(8,128)(2,1)} %copy-done.21, ...), custom_call_target="tpu_custom_call" | custom-call | flops 1 | bytes 1048576 | tf_op jit(solution)/shard_map/pallas_call | solution.py:219
  158.1 51.0 %all_to_all.35 = bf16[32,8,16,256]{3,2,1,0:T(8,128)(2,1)} all-to-all(bf16[32,8,16,256]{3,2,1,0:T(8,128)(2,1)} %get-tuple-element.106), channel_id=1, replica_groups=mesh['lat'=8,'lon'=4] {'lat','lon'}, dimensions={0} | all-to-all | bytes 4194304 | tf_op jit(solution)/shard_map/all_to_all | solution.py:563
  209.1 4.4 %all-to-all-start.4 = ((bf16[32,8,16,256]{3,2,1,0:T(8,128)(2,1)}), bf16[32,8,16,256]{3,2,1,0:T(8,128)(2,1)S(1)}, u32[]{:S(2)}, u32[]{:S(2)}) async-start(bf16[32,8,16,256]{3,2,1,0:T(8,128)(2,1)} %get-tuple-element.105), calls=%async_computation.4 | async-start | bytes 4194304 | tf_op jit(solution)/shard_map/all_to_all | solution.py:563
  216.3 3.3 %shard_map.117 = (bf16[2,16,64,128]{3,2,1,0:T(8,128)(2,1)S(1)}, bf16[2,16,64,128]{3,2,1,0:T(8,128)(2,1)}, bf16[2,16,64,128]{3,2,1,0:T(8,128)(2,1)}, bf16[2,16,64,128]{3,2,1,0:T(8,128)(2,1)}) custom-call(s32[3]{0:T(128)S(1)} %copy-done.15, bf16[256,16,256]{2,1,0:T(8,128)(2,1)S(1)} %bitcast.39, bf16[512,512]{1,0:T(8,128)(2,1)S(1)} %dynamic-slice_bitcast_fusion.table_ref), custom_call_target="tpu_custom_call" | custom-call | flops 1 | bytes 1048576 | tf_op jit(solution)/shard_map/pallas_call | solution.py:219
  223.1 38.0 %all-to-all-done.4 = bf16[32,8,16,256]{3,2,1,0:T(8,128)(2,1)S(1)} async-done(((bf16[32,8,16,256]{3,2,1,0:T(8,128)(2,1)}), bf16[32,8,16,256]{3,2,1,0:T(8,128)(2,1)S(1)}, u32[]{:S(2)}, u32[]{:S(2)}) %all-to-all-start.4) | async-done | bytes 2097184 | tf_op jit(solution)/shard_map/all_to_all | solution.py:563
  261.0 3.2 %collective-permute-done.15.refs_3_ = bf16[2,16,64,128]{3,2,1,0:T(8,128)(2,1)} collective-permute-done((bf16[2,16,64,128]{3,2,1,0:T(8,128)(2,1)}, bf16[2,16,64,128]{3,2,1,0:T(8,128)(2,1)}, u32[]{:S(2)}, u32[]{:S(2)}) %collective-permute-start.15) | collective-permute-done | bytes 524320 | tf_op jit(solution)/shard_map/ppermute | solution.py:551
  268.0 3.6 %all-to-all-start.6 = ((bf16[8,16,64,128]{3,2,1,0:T(8,128)(2,1)}), bf16[8,16,64,128]{3,2,1,0:T(8,128)(2,1)S(1)}, u32[]{:S(2)}, u32[]{:S(2)}) async-start(bf16[8,16,64,128]{3,2,1,0:T(8,128)(2,1)} %copy-done.4), calls=%async_computation.6 | async-start | bytes 4194304 | tf_op jit(solution)/shard_map/all_to_all | solution.py:559
  273.8 4.7 %shard_map.119 = (bf16[64,4,2,32,128]{4,3,2,1,0:T(8,128)(2,1)}, bf16[64,4,16,128]{3,2,1,0:T(8,128)(2,1)S(1)}) custom-call(s32[3]{0:T(128)S(1)} %copy-done.15, bf16[64,4,2,32,128]{4,3,2,1,0:T(8,128)(2,1)S(1)} %bitcast.35, bf16[2,16,64,128]{3,2,1,0:T(8,128)(2,1)S(1)} %get-tuple-element.117.refs_0_, bf16[2,16,64,128]{3,2,1,0:T(8,128)(2,1)} %collective-permute-done.13.refs_1_, ...), custom_call_target="tpu_custom_call" | custom-call | flops 1 | bytes 1048576 | tf_op jit(solution)/shard_map/pallas_call | solution.py:219
  283.0 15.2 %all-to-all-done.6.part_ref = bf16[8,16,64,128]{3,2,1,0:T(8,128)(2,1)S(1)} async-done(((bf16[8,16,64,128]{3,2,1,0:T(8,128)(2,1)}), bf16[8,16,64,128]{3,2,1,0:T(8,128)(2,1)S(1)}, u32[]{:S(2)}, u32[]{:S(2)}) %all-to-all-start.6) | async-done | bytes 2097184 | tf_op jit(solution)/shard_map/all_to_all | solution.py:559
  300.4 3.3 %shard_map.121 = bf16[64,4,2,32,128]{4,3,2,1,0:T(8,128)(2,1)} custom-call(s32[3]{0:T(128)S(1)} %copy-done.15, bf16[64,4,2,32,128]{4,3,2,1,0:T(8,128)(2,1)S(1)} %bitcast.37, bf16[8,16,64,128]{3,2,1,0:T(8,128)(2,1)S(1)} %all-to-all-done.6.part_ref, bf16[64,4,2,32,128]{4,3,2,1,0:T(8,128)(2,1)} %shard_map.120.refs_0_), custom_call_target="tpu_custom_call", output_to_operand_aliasing={{}: (3, {})} | custom-call | flops 1 | bytes 1048576 | tf_op jit(solution)/shard_map/pallas_call | solution.py:219
  (99 shorter events, 55.1 us)
Async XLA Ops:
  0.1 95.0 %copy-start.14 = (s32[3]{0:T(128)}, s32[3]{0:T(128)S(1)}, u32[]{:S(2)}) copy-start(s32[3]{0:T(128)S(1)} %pad_add_fusion.place_ref) | copy-start | bytes 40
  4.8 20.6 %all-to-all-start = ((bf16[8,8,64,128]{3,2,1,0:T(8,128)(2,1)}), bf16[8,8,64,128]{3,2,1,0:T(8,128)(2,1)S(1)}, u32[]{:S(2)}, u32[]{:S(2)}) async-start(bf16[8,8,64,128]{3,2,1,0:T(8,128)(2,1)} %shard_map.109), calls=%async_computation | async-start | bytes 2097152 | tf_op jit(solution)/shard_map/all_to_all | solution.py:559
  26.9 18.9 %all-to-all-start.1 = ((bf16[8,8,64,128]{3,2,1,0:T(8,128)(2,1)}), bf16[8,8,64,128]{3,2,1,0:T(8,128)(2,1)S(1)}, u32[]{:S(2)}, u32[]{:S(2)}) async-start(bf16[8,8,64,128]{3,2,1,0:T(8,128)(2,1)} %shard_map.110), calls=%async_computation.1 | async-start | bytes 2097152 | tf_op jit(solution)/shard_map/all_to_all | solution.py:559
  30.5 19.8 %collective-permute-start = (bf16[64,8,256]{2,1,0:T(8,128)(2,1)S(1)}, bf16[64,8,256]{2,1,0:T(8,128)(2,1)S(1)}, u32[]{:S(2)}, u32[]{:S(2)}) collective-permute-start(bf16[64,8,256]{2,1,0:T(8,128)(2,1)S(1)} %get-tuple-element.80), channel_id=1, source_target_pairs={{0,1},{1,0},{2,3},{3,2},{4,5},{5,4},{6,7},{7,6},{8,9},{9,8},{10,11... | collective-permute-start | bytes 786440 | tf_op jit(solution)/shard_map/ppermute | solution.py:551
  32.1 21.3 %collective-permute-start.1 = (bf16[64,8,256]{2,1,0:T(8,128)(2,1)S(1)}, bf16[64,8,256]{2,1,0:T(8,128)(2,1)S(1)}, u32[]{:S(2)}, u32[]{:S(2)}) collective-permute-start(bf16[64,8,256]{2,1,0:T(8,128)(2,1)S(1)} %get-tuple-element.81), channel_id=1, source_target_pairs={{0,2},{1,3},{2,0},{3,1},{4,6},{5,7},{6,4},{7,5},{8,10},{9,11},{10,... | collective-permute-start | bytes 786440 | tf_op jit(solution)/shard_map/ppermute | solution.py:551
  34.7 18.8 %collective-permute-start.2 = (bf16[64,8,256]{2,1,0:T(8,128)(2,1)S(1)}, bf16[64,8,256]{2,1,0:T(8,128)(2,1)S(1)}, u32[]{:S(2)}, u32[]{:S(2)}) collective-permute-start(bf16[64,8,256]{2,1,0:T(8,128)(2,1)S(1)} %get-tuple-element.82), channel_id=1, source_target_pairs={{0,3},{1,2},{2,1},{3,0},{4,7},{5,6},{6,5},{7,4},{8,11},{9,10},{10,... | collective-permute-start | bytes 786440 | tf_op jit(solution)/shard_map/ppermute | solution.py:551
  54.2 30.7 %all-to-all-start.2 = ((bf16[8,16,64,128]{3,2,1,0:T(8,128)(2,1)}), bf16[8,16,64,128]{3,2,1,0:T(8,128)(2,1)S(1)}, u32[]{:S(2)}, u32[]{:S(2)}) async-start(bf16[8,16,64,128]{3,2,1,0:T(8,128)(2,1)} %shard_map.111), calls=%async_computation.2 | async-start | bytes 4194304 | tf_op jit(solution)/shard_map/all_to_all | solution.py:559
  58.2 30.0 %collective-permute-start.3 = (bf16[64,8,256]{2,1,0:T(8,128)(2,1)}, bf16[64,8,256]{2,1,0:T(8,128)(2,1)}, u32[]{:S(2)}, u32[]{:S(2)}) collective-permute-start(bf16[64,8,256]{2,1,0:T(8,128)(2,1)} %copy-done.18), channel_id=1, source_target_pairs={{0,1},{1,0},{2,3},{3,2},{4,5},{5,4},{6,7},{7,6},{8,9},{9,8},{10,11... | collective-permute-start | bytes 786440 | tf_op jit(solution)/shard_map/ppermute | solution.py:551
  63.4 24.9 %collective-permute-start.4 = (bf16[64,8,256]{2,1,0:T(8,128)(2,1)}, bf16[64,8,256]{2,1,0:T(8,128)(2,1)}, u32[]{:S(2)}, u32[]{:S(2)}) collective-permute-start(bf16[64,8,256]{2,1,0:T(8,128)(2,1)} %copy-done.17), channel_id=1, source_target_pairs={{0,2},{1,3},{2,0},{3,1},{4,6},{5,7},{6,4},{7,5},{8,10},{9,11},{10,... | collective-permute-start | bytes 786440 | tf_op jit(solution)/shard_map/ppermute | solution.py:551
  64.4 23.8 %collective-permute-start.5 = (bf16[64,8,256]{2,1,0:T(8,128)(2,1)}, bf16[64,8,256]{2,1,0:T(8,128)(2,1)}, u32[]{:S(2)}, u32[]{:S(2)}) collective-permute-start(bf16[64,8,256]{2,1,0:T(8,128)(2,1)} %copy-done.16), channel_id=1, source_target_pairs={{0,3},{1,2},{2,1},{3,0},{4,7},{5,6},{6,5},{7,4},{8,11},{9,10},{10,... | collective-permute-start | bytes 786440 | tf_op jit(solution)/shard_map/ppermute | solution.py:551
  88.3 56.7 %all-to-all-start.3 = ((bf16[32,8,16,256]{3,2,1,0:T(8,128)(2,1)}), bf16[32,8,16,256]{3,2,1,0:T(8,128)(2,1)}, u32[]{:S(2)}, u32[]{:S(2)}) async-start(bf16[32,8,16,256]{3,2,1,0:T(8,128)(2,1)} %bitcast.12), calls=%async_computation.3 | async-start | bytes 4194304 | tf_op jit(solution)/shard_map/all_to_all | solution.py:563
  97.6 3.8 %collective-permute-start.6 = (bf16[4,8,16,256]{3,2,1,0:T(8,128)(2,1)S(1)}, bf16[4,8,16,256]{3,2,1,0:T(8,128)(2,1)S(1)}, u32[]{:S(2)}, u32[]{:S(2)}) collective-permute-start(bf16[4,8,16,256]{3,2,1,0:T(8,128)(2,1)S(1)} %get-tuple-element.97), channel_id=1, source_target_pairs={{0,4},{4,0},{8,12},{12,8},{16,20},{20,16},{24,28},{28,24},{1,5},{5... | collective-permute-start | bytes 786440 | tf_op jit(solution)/shard_map/ppermute | solution.py:551
  97.7 21.6 %collective-permute-start.7 = (bf16[4,8,16,256]{3,2,1,0:T(8,128)(2,1)S(1)}, bf16[4,8,16,256]{3,2,1,0:T(8,128)(2,1)S(1)}, u32[]{:S(2)}, u32[]{:S(2)}) collective-permute-start(bf16[4,8,16,256]{3,2,1,0:T(8,128)(2,1)S(1)} %get-tuple-element.98), channel_id=1, source_target_pairs={{0,8},{4,12},{8,0},{12,4},{16,24},{20,28},{24,16},{28,20},{1,9},{5... | collective-permute-start | bytes 786440 | tf_op jit(solution)/shard_map/ppermute | solution.py:551
  99.5 27.3 %collective-permute-start.8 = (bf16[4,8,16,256]{3,2,1,0:T(8,128)(2,1)S(1)}, bf16[4,8,16,256]{3,2,1,0:T(8,128)(2,1)S(1)}, u32[]{:S(2)}, u32[]{:S(2)}) collective-permute-start(bf16[4,8,16,256]{3,2,1,0:T(8,128)(2,1)S(1)} %get-tuple-element.99), channel_id=1, source_target_pairs={{0,12},{4,8},{8,4},{12,0},{16,28},{20,24},{24,20},{28,16},{1,13},{... | collective-permute-start | bytes 786440 | tf_op jit(solution)/shard_map/ppermute | solution.py:551
  99.5 27.2 %collective-permute-start.9 = (bf16[4,8,16,256]{3,2,1,0:T(8,128)(2,1)S(1)}, bf16[4,8,16,256]{3,2,1,0:T(8,128)(2,1)S(1)}, u32[]{:S(2)}, u32[]{:S(2)}) collective-permute-start(bf16[4,8,16,256]{3,2,1,0:T(8,128)(2,1)S(1)} %get-tuple-element.100), channel_id=1, source_target_pairs={{0,16},{4,20},{8,24},{12,28},{16,0},{20,4},{24,8},{28,12},{1,17},{... | collective-permute-start | bytes 786440 | tf_op jit(solution)/shard_map/ppermute | solution.py:551
  101.2 25.5 %collective-permute-start.10 = (bf16[4,8,16,256]{3,2,1,0:T(8,128)(2,1)S(1)}, bf16[4,8,16,256]{3,2,1,0:T(8,128)(2,1)S(1)}, u32[]{:S(2)}, u32[]{:S(2)}) collective-permute-start(bf16[4,8,16,256]{3,2,1,0:T(8,128)(2,1)S(1)} %get-tuple-element.101), channel_id=1, source_target_pairs={{0,20},{4,16},{8,28},{12,24},{16,4},{20,0},{24,12},{28,8},{1,21},{... | collective-permute-start | bytes 786440 | tf_op jit(solution)/shard_map/ppermute | solution.py:551
  101.3 36.4 %collective-permute-start.11 = (bf16[4,8,16,256]{3,2,1,0:T(8,128)(2,1)S(1)}, bf16[4,8,16,256]{3,2,1,0:T(8,128)(2,1)S(1)}, u32[]{:S(2)}, u32[]{:S(2)}) collective-permute-start(bf16[4,8,16,256]{3,2,1,0:T(8,128)(2,1)S(1)} %get-tuple-element.102), channel_id=1, source_target_pairs={{0,24},{4,28},{8,16},{12,20},{16,8},{20,12},{24,0},{28,4},{1,25},{... | collective-permute-start | bytes 786440 | tf_op jit(solution)/shard_map/ppermute | solution.py:551
  119.3 25.6 %collective-permute-start.12 = (bf16[4,8,16,256]{3,2,1,0:T(8,128)(2,1)S(1)}, bf16[4,8,16,256]{3,2,1,0:T(8,128)(2,1)S(1)}, u32[]{:S(2)}, u32[]{:S(2)}) collective-permute-start(bf16[4,8,16,256]{3,2,1,0:T(8,128)(2,1)S(1)} %get-tuple-element.103), channel_id=1, source_target_pairs={{0,28},{4,24},{8,20},{12,16},{16,12},{20,8},{24,4},{28,0},{1,29},{... | collective-permute-start | bytes 786440 | tf_op jit(solution)/shard_map/ppermute | solution.py:551
  209.1 51.9 %all-to-all-start.4 = ((bf16[32,8,16,256]{3,2,1,0:T(8,128)(2,1)}), bf16[32,8,16,256]{3,2,1,0:T(8,128)(2,1)S(1)}, u32[]{:S(2)}, u32[]{:S(2)}) async-start(bf16[32,8,16,256]{3,2,1,0:T(8,128)(2,1)} %get-tuple-element.105), calls=%async_computation.4 | async-start | bytes 4194304 | tf_op jit(solution)/shard_map/all_to_all | solution.py:563
  219.6 41.5 %collective-permute-start.13 = (bf16[2,16,64,128]{3,2,1,0:T(8,128)(2,1)}, bf16[2,16,64,128]{3,2,1,0:T(8,128)(2,1)}, u32[]{:S(2)}, u32[]{:S(2)}) collective-permute-start(bf16[2,16,64,128]{3,2,1,0:T(8,128)(2,1)} %get-tuple-element.108), channel_id=1, source_target_pairs={{0,8},{4,12},{8,0},{12,4},{16,24},{20,28},{24,16},{28,20},{1,9},{5... | collective-permute-start | bytes 1572872 | tf_op jit(solution)/shard_map/ppermute | solution.py:551
  221.3 39.7 %collective-permute-start.14 = (bf16[2,16,64,128]{3,2,1,0:T(8,128)(2,1)}, bf16[2,16,64,128]{3,2,1,0:T(8,128)(2,1)}, u32[]{:S(2)}, u32[]{:S(2)}) collective-permute-start(bf16[2,16,64,128]{3,2,1,0:T(8,128)(2,1)} %get-tuple-element.109), channel_id=1, source_target_pairs={{0,16},{4,20},{8,24},{12,28},{16,0},{20,4},{24,8},{28,12},{1,17},{... | collective-permute-start | bytes 1572872 | tf_op jit(solution)/shard_map/ppermute | solution.py:551
  222.8 41.4 %collective-permute-start.15 = (bf16[2,16,64,128]{3,2,1,0:T(8,128)(2,1)}, bf16[2,16,64,128]{3,2,1,0:T(8,128)(2,1)}, u32[]{:S(2)}, u32[]{:S(2)}) collective-permute-start(bf16[2,16,64,128]{3,2,1,0:T(8,128)(2,1)} %get-tuple-element.110), channel_id=1, source_target_pairs={{0,24},{4,28},{8,16},{12,20},{16,8},{20,12},{24,0},{28,4},{1,25},{... | collective-permute-start | bytes 1572872 | tf_op jit(solution)/shard_map/ppermute | solution.py:551
  268.0 30.2 %all-to-all-start.6 = ((bf16[8,16,64,128]{3,2,1,0:T(8,128)(2,1)}), bf16[8,16,64,128]{3,2,1,0:T(8,128)(2,1)S(1)}, u32[]{:S(2)}, u32[]{:S(2)}) async-start(bf16[8,16,64,128]{3,2,1,0:T(8,128)(2,1)} %copy-done.4), calls=%async_computation.6 | async-start | bytes 4194304 | tf_op jit(solution)/shard_map/all_to_all | solution.py:559
  278.5 2.7 collective-permute-start.16
  (27 other events, 274.2 us)

commit v6 on v5

--- a/solution.py
+++ b/solution.py
@@ -251,7 +251,7 @@
     )
 
 
-def join_all(features, part, place, start, partial, steps=4):
+def join_all(features, part, place, start, partial, steps=2):
     rows, chips, cores, _, channels = features.shape
     cells = part.shape[1]
     tile = rows // steps
@@ -592,7 +592,7 @@
     tie = lax.optimization_barrier
     field = features.reshape(rows, lat_count // 2, 2, block_cells, channels)
 
-    sent = split_all(field, place, starts[0], sizes[0])
+    sent = split_all(tie(field[:, :, :, : sizes[0]]), place, 0, sizes[0], 2)
     later, sent = tie((field, sent))
     waiting = [split_all(later, place, starts[i], sizes[i]) for i in (1, 2)]
     got, waiting = tie((swap_lat(sent), waiting))

time: 305 us -> 303 us (level)
    unnamed x56 -> x54, local copies, waits for them, and re-layouts: 16.6 us -> 14.4 us
where the time goes in v6:
time: 303 us; the launch traced here: 302 us
  waiting for transfers between devices  140 us (46%)
  blocking collectives  51 us (17%)
  starting transfers between devices  49.7 us (16%)
  Pallas kernels  43 us (14%)
  local copies, waits for them, and re-layouts  17 us (6%)
    all_to_all x4, waiting for transfers between devices, swap_lat(): return lax.all_to_all(parts, 'lat', split_axis=0, concat_axis=0, tiled=True)  53.1 us
    all_to_all x1, blocking collectives, swap_all(): lax.all_to_all(parts, ('lat', 'lon'), split_axis=0, concat_axis=0, tiled=...  51 us
    ppermute x17, waiting for transfers between devices, swap_bits(): lax.ppermute(part, axis, [(j, j ^ bits) for j in range(lax.axis_size(axis...  48.8 us
    pallas_call x13, Pallas kernels, call(): pl.pallas_call(kernel, grid_spec=pltpu.PrefetchScalarGridSpec(num_scalar_...  43 us
    all_to_all x2, waiting for transfers between devices, swap_all(): lax.all_to_all(parts, ('lat', 'lon'), split_axis=0, concat_axis=0, tiled=...  38 us
    ppermute x17, starting transfers between devices, swap_bits(): lax.ppermute(part, axis, [(j, j ^ bits) for j in range(lax.axis_size(axis...  22.2 us
    all_to_all x4, starting transfers between devices, swap_lat(): return lax.all_to_all(parts, 'lat', split_axis=0, concat_axis=0, tiled=True)  16.4 us
    unnamed x54, local copies, waits for them, and re-layouts  14.4 us
  transfers between devices with their start and end apart: 23, of which 12 were waited for; matrix products, arithmetic and copies ran while one was open for 1% of the time, Pallas kernels for 7%

profile of v6, /device:TPU:0, one launch (start us, length us, event | category | flops | bytes accessed | tf_op | source)
XLA Modules:
  0.0 301.9 jit_solution(3134189317750448734)
XLA Ops:
  3.3 5.2 %all-to-all-start = ((bf16[8,8,64,128]{3,2,1,0:T(8,128)(2,1)}), bf16[8,8,64,128]{3,2,1,0:T(8,128)(2,1)S(1)}, u32[]{:S(2)}, u32[]{:S(2)}) async-start(bf16[8,8,64,128]{3,2,1,0:T(8,128)(2,1)} %shard_map.109), calls=%async_computation | async-start | bytes 2097152 | tf_op jit(solution)/shard_map/all_to_all | solution.py:559
  15.9 8.0 %all-to-all-done.x_ref = bf16[8,8,64,128]{3,2,1,0:T(8,128)(2,1)S(1)} async-done(((bf16[8,8,64,128]{3,2,1,0:T(8,128)(2,1)}), bf16[8,8,64,128]{3,2,1,0:T(8,128)(2,1)S(1)}, u32[]{:S(2)}, u32[]{:S(2)}) %all-to-all-start) | async-done | bytes 1048608 | tf_op jit(solution)/shard_map/all_to_all | solution.py:559
  25.5 3.6 %all-to-all-start.1 = ((bf16[8,8,64,128]{3,2,1,0:T(8,128)(2,1)}), bf16[8,8,64,128]{3,2,1,0:T(8,128)(2,1)S(1)}, u32[]{:S(2)}, u32[]{:S(2)}) async-start(bf16[8,8,64,128]{3,2,1,0:T(8,128)(2,1)} %shard_map.110), calls=%async_computation.1 | async-start | bytes 2097152 | tf_op jit(solution)/shard_map/all_to_all | solution.py:559
  33.5 10.9 %all-to-all-done.1.x_ref = bf16[8,8,64,128]{3,2,1,0:T(8,128)(2,1)S(1)} async-done(((bf16[8,8,64,128]{3,2,1,0:T(8,128)(2,1)}), bf16[8,8,64,128]{3,2,1,0:T(8,128)(2,1)S(1)}, u32[]{:S(2)}, u32[]{:S(2)}) %all-to-all-start.1) | async-done | bytes 1048608 | tf_op jit(solution)/shard_map/all_to_all | solution.py:559
  48.8 3.2 %collective-permute-done.1 = bf16[64,8,256]{2,1,0:T(8,128)(2,1)S(1)} collective-permute-done((bf16[64,8,256]{2,1,0:T(8,128)(2,1)S(1)}, bf16[64,8,256]{2,1,0:T(8,128)(2,1)S(1)}, u32[]{:S(2)}, u32[]{:S(2)}) %collective-permute-start.1) | collective-permute-done | bytes 262176 | tf_op jit(solution)/shard_map/ppermute | solution.py:551
  52.7 4.0 %all-to-all-start.2 = ((bf16[8,16,64,128]{3,2,1,0:T(8,128)(2,1)}), bf16[8,16,64,128]{3,2,1,0:T(8,128)(2,1)S(1)}, u32[]{:S(2)}, u32[]{:S(2)}) async-start(bf16[8,16,64,128]{3,2,1,0:T(8,128)(2,1)} %shard_map.111), calls=%async_computation.2 | async-start | bytes 4194304 | tf_op jit(solution)/shard_map/all_to_all | solution.py:559
  56.8 5.1 %collective-permute-start.3 = (bf16[64,8,256]{2,1,0:T(8,128)(2,1)}, bf16[64,8,256]{2,1,0:T(8,128)(2,1)}, u32[]{:S(2)}, u32[]{:S(2)}) collective-permute-start(bf16[64,8,256]{2,1,0:T(8,128)(2,1)} %copy-done.17), channel_id=1, source_target_pairs={{0,1},{1,0},{2,3},{3,2},{4,5},{5,4},{6,7},{7,6},{8,9},{9,8},{10,11... | collective-permute-start | bytes 786440 | tf_op jit(solution)/shard_map/ppermute | solution.py:551
  64.4 19.1 %all-to-all-done.2.x_ref = bf16[8,16,64,128]{3,2,1,0:T(8,128)(2,1)S(1)} async-done(((bf16[8,16,64,128]{3,2,1,0:T(8,128)(2,1)}), bf16[8,16,64,128]{3,2,1,0:T(8,128)(2,1)S(1)}, u32[]{:S(2)}, u32[]{:S(2)}) %all-to-all-start.2) | async-done | bytes 2097184 | tf_op jit(solution)/shard_map/all_to_all | solution.py:559
  83.4 3.4 %shard_map.114 = bf16[256,16,256]{2,1,0:T(8,128)(2,1)} custom-call(s32[3]{0:T(128)S(1)} %pad_add_fusion.place_ref, bf16[8,16,64,128]{3,2,1,0:T(8,128)(2,1)S(1)} %all-to-all-done.2.x_ref, bf16[512,512]{1,0:T(8,128)(2,1)S(1)} %copy-done.7), custom_call_target="tpu_custom_call" | custom-call | flops 1 | bytes 1048576 | tf_op jit(solution)/shard_map/pallas_call | solution.py:219
  86.9 6.7 %all-to-all-start.3 = ((bf16[32,8,16,256]{3,2,1,0:T(8,128)(2,1)}), bf16[32,8,16,256]{3,2,1,0:T(8,128)(2,1)}, u32[]{:S(2)}, u32[]{:S(2)}) async-start(bf16[32,8,16,256]{3,2,1,0:T(8,128)(2,1)} %bitcast.12), calls=%async_computation.3 | async-start | bytes 4194304 | tf_op jit(solution)/shard_map/all_to_all | solution.py:563
  102.5 15.4 %collective-permute-done.7.refs_2_ = bf16[4,8,16,256]{3,2,1,0:T(8,128)(2,1)S(1)} collective-permute-done((bf16[4,8,16,256]{3,2,1,0:T(8,128)(2,1)S(1)}, bf16[4,8,16,256]{3,2,1,0:T(8,128)(2,1)S(1)}, u32[]{:S(2)}, u32[]{:S(2)}) %collective-permute-start.7) | collective-permute-done | bytes 262176 | tf_op jit(solution)/shard_map/ppermute | solution.py:551
  118.7 6.6 %collective-permute-done.8.refs_3_ = bf16[4,8,16,256]{3,2,1,0:T(8,128)(2,1)S(1)} collective-permute-done((bf16[4,8,16,256]{3,2,1,0:T(8,128)(2,1)S(1)}, bf16[4,8,16,256]{3,2,1,0:T(8,128)(2,1)S(1)}, u32[]{:S(2)}, u32[]{:S(2)}) %collective-permute-start.8) | collective-permute-done | bytes 262176 | tf_op jit(solution)/shard_map/ppermute | solution.py:551
  125.3 11.0 %collective-permute-done.11.refs_6_ = bf16[4,8,16,256]{3,2,1,0:T(8,128)(2,1)S(1)} collective-permute-done((bf16[4,8,16,256]{3,2,1,0:T(8,128)(2,1)S(1)}, bf16[4,8,16,256]{3,2,1,0:T(8,128)(2,1)S(1)}, u32[]{:S(2)}, u32[]{:S(2)}) %collective-permute-start.11) | collective-permute-done | bytes 262176 | tf_op jit(solution)/shard_map/ppermute | solution.py:551
  136.3 7.2 %collective-permute-done.12.refs_7_ = bf16[4,8,16,256]{3,2,1,0:T(8,128)(2,1)S(1)} collective-permute-done((bf16[4,8,16,256]{3,2,1,0:T(8,128)(2,1)S(1)}, bf16[4,8,16,256]{3,2,1,0:T(8,128)(2,1)S(1)}, u32[]{:S(2)}, u32[]{:S(2)}) %collective-permute-start.12) | collective-permute-done | bytes 262176 | tf_op jit(solution)/shard_map/ppermute | solution.py:551
  144.2 12.5 %shard_map.116 = (bf16[32,8,16,256]{3,2,1,0:T(8,128)(2,1)}, bf16[32,8,16,256]{3,2,1,0:T(8,128)(2,1)}) custom-call(s32[3]{0:T(128)} %copy-done.13, bf16[4,8,16,256]{3,2,1,0:T(8,128)(2,1)} %copy-done.8, bf16[4,8,16,256]{3,2,1,0:T(8,128)(2,1)} %copy-done.18, bf16[4,8,16,256]{3,2,1,0:T(8,128)(2,1)} %copy-done.19, bf16[4,8,16,256]{3,2,1,0:T(8,128)(2,1)} %copy-done.20, ...), custom_call_target="tpu_custom_call" | custom-call | flops 1 | bytes 1048576 | tf_op jit(solution)/shard_map/pallas_call | solution.py:219
  156.7 51.0 %all_to_all.35 = bf16[32,8,16,256]{3,2,1,0:T(8,128)(2,1)} all-to-all(bf16[32,8,16,256]{3,2,1,0:T(8,128)(2,1)} %get-tuple-element.106), channel_id=1, replica_groups=mesh['lat'=8,'lon'=4] {'lat','lon'}, dimensions={0} | all-to-all | bytes 4194304 | tf_op jit(solution)/shard_map/all_to_all | solution.py:563
  207.7 4.4 %all-to-all-start.4 = ((bf16[32,8,16,256]{3,2,1,0:T(8,128)(2,1)}), bf16[32,8,16,256]{3,2,1,0:T(8,128)(2,1)S(1)}, u32[]{:S(2)}, u32[]{:S(2)}) async-start(bf16[32,8,16,256]{3,2,1,0:T(8,128)(2,1)} %get-tuple-element.105), calls=%async_computation.4 | async-start | bytes 4194304 | tf_op jit(solution)/shard_map/all_to_all | solution.py:563
  214.8 3.3 %shard_map.117 = (bf16[2,16,64,128]{3,2,1,0:T(8,128)(2,1)S(1)}, bf16[2,16,64,128]{3,2,1,0:T(8,128)(2,1)}, bf16[2,16,64,128]{3,2,1,0:T(8,128)(2,1)}, bf16[2,16,64,128]{3,2,1,0:T(8,128)(2,1)}) custom-call(s32[3]{0:T(128)S(1)} %copy-done.14, bf16[256,16,256]{2,1,0:T(8,128)(2,1)S(1)} %bitcast.39, bf16[512,512]{1,0:T(8,128)(2,1)S(1)} %dynamic-slice_bitcast_fusion.table_ref), custom_call_target="tpu_custom_call" | custom-call | flops 1 | bytes 1048576 | tf_op jit(solution)/shard_map/pallas_call | solution.py:219
  221.6 38.0 %all-to-all-done.4 = bf16[32,8,16,256]{3,2,1,0:T(8,128)(2,1)S(1)} async-done(((bf16[32,8,16,256]{3,2,1,0:T(8,128)(2,1)}), bf16[32,8,16,256]{3,2,1,0:T(8,128)(2,1)S(1)}, u32[]{:S(2)}, u32[]{:S(2)}) %all-to-all-start.4) | async-done | bytes 2097184 | tf_op jit(solution)/shard_map/all_to_all | solution.py:563
  259.6 3.2 %collective-permute-done.15.refs_3_ = bf16[2,16,64,128]{3,2,1,0:T(8,128)(2,1)} collective-permute-done((bf16[2,16,64,128]{3,2,1,0:T(8,128)(2,1)}, bf16[2,16,64,128]{3,2,1,0:T(8,128)(2,1)}, u32[]{:S(2)}, u32[]{:S(2)}) %collective-permute-start.15) | collective-permute-done | bytes 524320 | tf_op jit(solution)/shard_map/ppermute | solution.py:551
  266.6 3.6 %all-to-all-start.6 = ((bf16[8,16,64,128]{3,2,1,0:T(8,128)(2,1)}), bf16[8,16,64,128]{3,2,1,0:T(8,128)(2,1)S(1)}, u32[]{:S(2)}, u32[]{:S(2)}) async-start(bf16[8,16,64,128]{3,2,1,0:T(8,128)(2,1)} %copy-done.3), calls=%async_computation.6 | async-start | bytes 4194304 | tf_op jit(solution)/shard_map/all_to_all | solution.py:559
  272.4 4.7 %shard_map.119 = (bf16[64,4,2,32,128]{4,3,2,1,0:T(8,128)(2,1)}, bf16[64,4,16,128]{3,2,1,0:T(8,128)(2,1)S(1)}) custom-call(s32[3]{0:T(128)S(1)} %copy-done.14, bf16[64,4,2,32,128]{4,3,2,1,0:T(8,128)(2,1)S(1)} %bitcast.35, bf16[2,16,64,128]{3,2,1,0:T(8,128)(2,1)S(1)} %get-tuple-element.117.refs_0_, bf16[2,16,64,128]{3,2,1,0:T(8,128)(2,1)} %collective-permute-done.13.refs_1_, ...), custom_call_target="tpu_custom_call" | custom-call | flops 1 | bytes 1048576 | tf_op jit(solution)/shard_map/pallas_call | solution.py:219
  281.6 15.2 %all-to-all-done.6.part_ref = bf16[8,16,64,128]{3,2,1,0:T(8,128)(2,1)S(1)} async-done(((bf16[8,16,64,128]{3,2,1,0:T(8,128)(2,1)}), bf16[8,16,64,128]{3,2,1,0:T(8,128)(2,1)S(1)}, u32[]{:S(2)}, u32[]{:S(2)}) %all-to-all-start.6) | async-done | bytes 2097184 | tf_op jit(solution)/shard_map/all_to_all | solution.py:559
  298.9 2.9 shard_map.121
  (98 shorter events, 53.7 us)
Async XLA Ops:
  1.5 92.1 %copy-start.13 = (s32[3]{0:T(128)}, s32[3]{0:T(128)S(1)}, u32[]{:S(2)}) copy-start(s32[3]{0:T(128)S(1)} %pad_add_fusion.place_ref) | copy-start | bytes 40
  3.3 20.6 %all-to-all-start = ((bf16[8,8,64,128]{3,2,1,0:T(8,128)(2,1)}), bf16[8,8,64,128]{3,2,1,0:T(8,128)(2,1)S(1)}, u32[]{:S(2)}, u32[]{:S(2)}) async-start(bf16[8,8,64,128]{3,2,1,0:T(8,128)(2,1)} %shard_map.109), calls=%async_computation | async-start | bytes 2097152 | tf_op jit(solution)/shard_map/all_to_all | solution.py:559
  25.5 18.9 %all-to-all-start.1 = ((bf16[8,8,64,128]{3,2,1,0:T(8,128)(2,1)}), bf16[8,8,64,128]{3,2,1,0:T(8,128)(2,1)S(1)}, u32[]{:S(2)}, u32[]{:S(2)}) async-start(bf16[8,8,64,128]{3,2,1,0:T(8,128)(2,1)} %shard_map.110), calls=%async_computation.1 | async-start | bytes 2097152 | tf_op jit(solution)/shard_map/all_to_all | solution.py:559
  29.1 19.8 %collective-permute-start = (bf16[64,8,256]{2,1,0:T(8,128)(2,1)S(1)}, bf16[64,8,256]{2,1,0:T(8,128)(2,1)S(1)}, u32[]{:S(2)}, u32[]{:S(2)}) collective-permute-start(bf16[64,8,256]{2,1,0:T(8,128)(2,1)S(1)} %get-tuple-element.80), channel_id=1, source_target_pairs={{0,1},{1,0},{2,3},{3,2},{4,5},{5,4},{6,7},{7,6},{8,9},{9,8},{10,11... | collective-permute-start | bytes 786440 | tf_op jit(solution)/shard_map/ppermute | solution.py:551
  30.7 21.3 %collective-permute-start.1 = (bf16[64,8,256]{2,1,0:T(8,128)(2,1)S(1)}, bf16[64,8,256]{2,1,0:T(8,128)(2,1)S(1)}, u32[]{:S(2)}, u32[]{:S(2)}) collective-permute-start(bf16[64,8,256]{2,1,0:T(8,128)(2,1)S(1)} %get-tuple-element.81), channel_id=1, source_target_pairs={{0,2},{1,3},{2,0},{3,1},{4,6},{5,7},{6,4},{7,5},{8,10},{9,11},{10,... | collective-permute-start | bytes 786440 | tf_op jit(solution)/shard_map/ppermute | solution.py:551
  33.3 18.8 %collective-permute-start.2 = (bf16[64,8,256]{2,1,0:T(8,128)(2,1)S(1)}, bf16[64,8,256]{2,1,0:T(8,128)(2,1)S(1)}, u32[]{:S(2)}, u32[]{:S(2)}) collective-permute-start(bf16[64,8,256]{2,1,0:T(8,128)(2,1)S(1)} %get-tuple-element.82), channel_id=1, source_target_pairs={{0,3},{1,2},{2,1},{3,0},{4,7},{5,6},{6,5},{7,4},{8,11},{9,10},{10,... | collective-permute-start | bytes 786440 | tf_op jit(solution)/shard_map/ppermute | solution.py:551
  52.7 30.7 %all-to-all-start.2 = ((bf16[8,16,64,128]{3,2,1,0:T(8,128)(2,1)}), bf16[8,16,64,128]{3,2,1,0:T(8,128)(2,1)S(1)}, u32[]{:S(2)}, u32[]{:S(2)}) async-start(bf16[8,16,64,128]{3,2,1,0:T(8,128)(2,1)} %shard_map.111), calls=%async_computation.2 | async-start | bytes 4194304 | tf_op jit(solution)/shard_map/all_to_all | solution.py:559
  56.8 30.0 %collective-permute-start.3 = (bf16[64,8,256]{2,1,0:T(8,128)(2,1)}, bf16[64,8,256]{2,1,0:T(8,128)(2,1)}, u32[]{:S(2)}, u32[]{:S(2)}) collective-permute-start(bf16[64,8,256]{2,1,0:T(8,128)(2,1)} %copy-done.17), channel_id=1, source_target_pairs={{0,1},{1,0},{2,3},{3,2},{4,5},{5,4},{6,7},{7,6},{8,9},{9,8},{10,11... | collective-permute-start | bytes 786440 | tf_op jit(solution)/shard_map/ppermute | solution.py:551
  61.9 24.9 %collective-permute-start.4 = (bf16[64,8,256]{2,1,0:T(8,128)(2,1)}, bf16[64,8,256]{2,1,0:T(8,128)(2,1)}, u32[]{:S(2)}, u32[]{:S(2)}) collective-permute-start(bf16[64,8,256]{2,1,0:T(8,128)(2,1)} %copy-done.16), channel_id=1, source_target_pairs={{0,2},{1,3},{2,0},{3,1},{4,6},{5,7},{6,4},{7,5},{8,10},{9,11},{10,... | collective-permute-start | bytes 786440 | tf_op jit(solution)/shard_map/ppermute | solution.py:551
  63.0 23.8 %collective-permute-start.5 = (bf16[64,8,256]{2,1,0:T(8,128)(2,1)}, bf16[64,8,256]{2,1,0:T(8,128)(2,1)}, u32[]{:S(2)}, u32[]{:S(2)}) collective-permute-start(bf16[64,8,256]{2,1,0:T(8,128)(2,1)} %copy-done.15), channel_id=1, source_target_pairs={{0,3},{1,2},{2,1},{3,0},{4,7},{5,6},{6,5},{7,4},{8,11},{9,10},{10,... | collective-permute-start | bytes 786440 | tf_op jit(solution)/shard_map/ppermute | solution.py:551
  86.9 56.6 %all-to-all-start.3 = ((bf16[32,8,16,256]{3,2,1,0:T(8,128)(2,1)}), bf16[32,8,16,256]{3,2,1,0:T(8,128)(2,1)}, u32[]{:S(2)}, u32[]{:S(2)}) async-start(bf16[32,8,16,256]{3,2,1,0:T(8,128)(2,1)} %bitcast.12), calls=%async_computation.3 | async-start | bytes 4194304 | tf_op jit(solution)/shard_map/all_to_all | solution.py:563
  96.1 3.8 %collective-permute-start.6 = (bf16[4,8,16,256]{3,2,1,0:T(8,128)(2,1)S(1)}, bf16[4,8,16,256]{3,2,1,0:T(8,128)(2,1)S(1)}, u32[]{:S(2)}, u32[]{:S(2)}) collective-permute-start(bf16[4,8,16,256]{3,2,1,0:T(8,128)(2,1)S(1)} %get-tuple-element.97), channel_id=1, source_target_pairs={{0,4},{4,0},{8,12},{12,8},{16,20},{20,16},{24,28},{28,24},{1,5},{5... | collective-permute-start | bytes 786440 | tf_op jit(solution)/shard_map/ppermute | solution.py:551
  96.3 21.6 %collective-permute-start.7 = (bf16[4,8,16,256]{3,2,1,0:T(8,128)(2,1)S(1)}, bf16[4,8,16,256]{3,2,1,0:T(8,128)(2,1)S(1)}, u32[]{:S(2)}, u32[]{:S(2)}) collective-permute-start(bf16[4,8,16,256]{3,2,1,0:T(8,128)(2,1)S(1)} %get-tuple-element.98), channel_id=1, source_target_pairs={{0,8},{4,12},{8,0},{12,4},{16,24},{20,28},{24,16},{28,20},{1,9},{5... | collective-permute-start | bytes 786440 | tf_op jit(solution)/shard_map/ppermute | solution.py:551
  98.0 27.3 %collective-permute-start.8 = (bf16[4,8,16,256]{3,2,1,0:T(8,128)(2,1)S(1)}, bf16[4,8,16,256]{3,2,1,0:T(8,128)(2,1)S(1)}, u32[]{:S(2)}, u32[]{:S(2)}) collective-permute-start(bf16[4,8,16,256]{3,2,1,0:T(8,128)(2,1)S(1)} %get-tuple-element.99), channel_id=1, source_target_pairs={{0,12},{4,8},{8,4},{12,0},{16,28},{20,24},{24,20},{28,16},{1,13},{... | collective-permute-start | bytes 786440 | tf_op jit(solution)/shard_map/ppermute | solution.py:551
  98.1 27.2 %collective-permute-start.9 = (bf16[4,8,16,256]{3,2,1,0:T(8,128)(2,1)S(1)}, bf16[4,8,16,256]{3,2,1,0:T(8,128)(2,1)S(1)}, u32[]{:S(2)}, u32[]{:S(2)}) collective-permute-start(bf16[4,8,16,256]{3,2,1,0:T(8,128)(2,1)S(1)} %get-tuple-element.100), channel_id=1, source_target_pairs={{0,16},{4,20},{8,24},{12,28},{16,0},{20,4},{24,8},{28,12},{1,17},{... | collective-permute-start | bytes 786440 | tf_op jit(solution)/shard_map/ppermute | solution.py:551
  99.8 25.5 %collective-permute-start.10 = (bf16[4,8,16,256]{3,2,1,0:T(8,128)(2,1)S(1)}, bf16[4,8,16,256]{3,2,1,0:T(8,128)(2,1)S(1)}, u32[]{:S(2)}, u32[]{:S(2)}) collective-permute-start(bf16[4,8,16,256]{3,2,1,0:T(8,128)(2,1)S(1)} %get-tuple-element.101), channel_id=1, source_target_pairs={{0,20},{4,16},{8,28},{12,24},{16,4},{20,0},{24,12},{28,8},{1,21},{... | collective-permute-start | bytes 786440 | tf_op jit(solution)/shard_map/ppermute | solution.py:551
  99.9 36.4 %collective-permute-start.11 = (bf16[4,8,16,256]{3,2,1,0:T(8,128)(2,1)S(1)}, bf16[4,8,16,256]{3,2,1,0:T(8,128)(2,1)S(1)}, u32[]{:S(2)}, u32[]{:S(2)}) collective-permute-start(bf16[4,8,16,256]{3,2,1,0:T(8,128)(2,1)S(1)} %get-tuple-element.102), channel_id=1, source_target_pairs={{0,24},{4,28},{8,16},{12,20},{16,8},{20,12},{24,0},{28,4},{1,25},{... | collective-permute-start | bytes 786440 | tf_op jit(solution)/shard_map/ppermute | solution.py:551
  117.9 25.6 %collective-permute-start.12 = (bf16[4,8,16,256]{3,2,1,0:T(8,128)(2,1)S(1)}, bf16[4,8,16,256]{3,2,1,0:T(8,128)(2,1)S(1)}, u32[]{:S(2)}, u32[]{:S(2)}) collective-permute-start(bf16[4,8,16,256]{3,2,1,0:T(8,128)(2,1)S(1)} %get-tuple-element.103), channel_id=1, source_target_pairs={{0,28},{4,24},{8,20},{12,16},{16,12},{20,8},{24,4},{28,0},{1,29},{... | collective-permute-start | bytes 786440 | tf_op jit(solution)/shard_map/ppermute | solution.py:551
  207.7 51.9 %all-to-all-start.4 = ((bf16[32,8,16,256]{3,2,1,0:T(8,128)(2,1)}), bf16[32,8,16,256]{3,2,1,0:T(8,128)(2,1)S(1)}, u32[]{:S(2)}, u32[]{:S(2)}) async-start(bf16[32,8,16,256]{3,2,1,0:T(8,128)(2,1)} %get-tuple-element.105), calls=%async_computation.4 | async-start | bytes 4194304 | tf_op jit(solution)/shard_map/all_to_all | solution.py:563
  218.1 41.5 %collective-permute-start.13 = (bf16[2,16,64,128]{3,2,1,0:T(8,128)(2,1)}, bf16[2,16,64,128]{3,2,1,0:T(8,128)(2,1)}, u32[]{:S(2)}, u32[]{:S(2)}) collective-permute-start(bf16[2,16,64,128]{3,2,1,0:T(8,128)(2,1)} %get-tuple-element.108), channel_id=1, source_target_pairs={{0,8},{4,12},{8,0},{12,4},{16,24},{20,28},{24,16},{28,20},{1,9},{5... | collective-permute-start | bytes 1572872 | tf_op jit(solution)/shard_map/ppermute | solution.py:551
  219.9 39.7 %collective-permute-start.14 = (bf16[2,16,64,128]{3,2,1,0:T(8,128)(2,1)}, bf16[2,16,64,128]{3,2,1,0:T(8,128)(2,1)}, u32[]{:S(2)}, u32[]{:S(2)}) collective-permute-start(bf16[2,16,64,128]{3,2,1,0:T(8,128)(2,1)} %get-tuple-element.109), channel_id=1, source_target_pairs={{0,16},{4,20},{8,24},{12,28},{16,0},{20,4},{24,8},{28,12},{1,17},{... | collective-permute-start | bytes 1572872 | tf_op jit(solution)/shard_map/ppermute | solution.py:551
  221.4 41.4 %collective-permute-start.15 = (bf16[2,16,64,128]{3,2,1,0:T(8,128)(2,1)}, bf16[2,16,64,128]{3,2,1,0:T(8,128)(2,1)}, u32[]{:S(2)}, u32[]{:S(2)}) collective-permute-start(bf16[2,16,64,128]{3,2,1,0:T(8,128)(2,1)} %get-tuple-element.110), channel_id=1, source_target_pairs={{0,24},{4,28},{8,16},{12,20},{16,8},{20,12},{24,0},{28,4},{1,25},{... | collective-permute-start | bytes 1572872 | tf_op jit(solution)/shard_map/ppermute | solution.py:551
  266.6 30.2 %all-to-all-start.6 = ((bf16[8,16,64,128]{3,2,1,0:T(8,128)(2,1)}), bf16[8,16,64,128]{3,2,1,0:T(8,128)(2,1)S(1)}, u32[]{:S(2)}, u32[]{:S(2)}) async-start(bf16[8,16,64,128]{3,2,1,0:T(8,128)(2,1)} %copy-done.3), calls=%async_computation.6 | async-start | bytes 4194304 | tf_op jit(solution)/shard_map/all_to_all | solution.py:559
  277.1 2.7 collective-permute-start.16
  (26 other events, 272.0 us)
